TPU v7x, 32 devices: a whole 2x2x4 slice. The times are simulated.
32 devices in a mesh: dp: 8 (over y, x, core), tensor: 4 (over z).
Axes of the slice: x: 2, y: 2, z: 4, core: 2. Of those that a mesh axis runs over, the one named last changes fastest.
Arguments:
- queries: bfloat16 [4096, 2048], P('dp', 'tensor'), may hold values from -5 to 5
- keys: bfloat16 [4096, 256], P('dp', 'tensor'), may hold values from -5 to 5
- values: bfloat16 [4096, 256], P('dp', 'tensor'), may hold values from -6 to 6
- grad_out: bfloat16 [4096, 4096], P(('dp', 'tensor')), may hold values from -6 to 6
- out_weight: bfloat16 [4096, 2048], P('dp', 'tensor'), may hold values from -0.375 to 0.375
Outputs:
- grad_queries: bfloat16 [4096, 2048], P('dp', 'tensor')
- grad_keys: bfloat16 [4096, 256], P('dp', 'tensor')
- grad_values: bfloat16 [4096, 256], P('dp', 'tensor')
- grad_weight: bfloat16 [4096, 2048], P('dp', 'tensor')
All inputs are finite; a program needn't handle non-finite values.
Results may differ from a plain program's by a relative error of at most 0.03.
Values may be sent and summed in bfloat16 or wider, within the bound.
No kernel may reach another device: no remote copies, remote signals or barrier semaphores. Data moves between devices by JAX's collectives and lax.ppermute only.
A program may use at most 64 MiB of HBM per device.

v0:
```python
import jax
import jax.numpy as jnp
from jax import lax
from jax.sharding import PartitionSpec as P

HEAD_DIM = 128


def partner(value, axis, apart):
    return lax.ppermute(value, axis, [(i, i ^ 1 << apart) for i in range(lax.axis_size(axis))])


def weight_gradient(grad_full, attended):
    return lax.psum_scatter(
        lax.dot_general(
            grad_full, attended, (((0,), (0,)), ((), ())), preferred_element_type=jnp.float32
        ).astype(jnp.bfloat16),
        "dp",
        scatter_dimension=0,
        tiled=True,
    )


def body(queries, keys, values, grad_out, out_weight):
    scale = HEAD_DIM ** (-0.5)
    half = HEAD_DIM // 2
    parity = lax.axis_index("tensor") % 2
    other_key, other_value = partner((keys, values), "tensor", 0)
    key_full = jnp.where(
        parity == 0, jnp.concatenate([keys, other_key], 1), jnp.concatenate([other_key, keys], 1)
    )
    value_full = jnp.where(
        parity == 0,
        jnp.concatenate([values, other_value], 1),
        jnp.concatenate([other_value, values], 1),
    )
    length = queries.shape[0]
    head_count = queries.shape[1] // HEAD_DIM
    query_heads = queries.reshape(length, head_count, HEAD_DIM)
    scores = (
        jnp.einsum("shd,td->hst", query_heads, key_full, preferred_element_type=jnp.float32) * scale
    )
    row_index = lax.broadcasted_iota(jnp.int32, (length, length), 0)
    column_index = lax.broadcasted_iota(jnp.int32, (length, length), 1)
    scores = jnp.where(column_index <= row_index, scores, -jnp.inf)
    probs = jax.nn.softmax(scores, axis=-1)
    probs_half = probs.astype(jnp.bfloat16)
    attended = jnp.einsum("hst,td->shd", probs_half, value_full, preferred_element_type=jnp.float32)
    attended = attended.astype(jnp.bfloat16).reshape(length, head_count * HEAD_DIM)
    grad_full = lax.all_gather(grad_out, "tensor", axis=0, tiled=True)
    grad_att = jnp.dot(
        grad_full,
        lax.all_gather(out_weight, "dp", axis=0, tiled=True),
        preferred_element_type=jnp.float32,
    ).astype(jnp.bfloat16)
    grad_heads = grad_att.reshape(length, head_count, HEAD_DIM)
    dprobs = jnp.einsum("shd,td->hst", grad_heads, value_full, preferred_element_type=jnp.float32)
    delta = jnp.sum(probs * dprobs, axis=-1, keepdims=True)
    dscores = (probs * (dprobs - delta) * scale).astype(jnp.bfloat16)
    grad_q = jnp.einsum("hst,td->shd", dscores, key_full, preferred_element_type=jnp.float32)
    grad_q = grad_q.astype(jnp.bfloat16).reshape(length, head_count * HEAD_DIM)
    key_part = jnp.einsum(
        "hst,shd->td", dscores, query_heads, preferred_element_type=jnp.float32
    ).astype(jnp.bfloat16)
    value_part = jnp.einsum(
        "hst,shd->td", probs_half, grad_heads, preferred_element_type=jnp.float32
    ).astype(jnp.bfloat16)
    partner_key, partner_value = partner((key_part, value_part), "tensor", 0)
    key_total = (key_part.astype(jnp.float32) + partner_key.astype(jnp.float32)).astype(
        jnp.bfloat16
    )
    value_total = (value_part.astype(jnp.float32) + partner_value.astype(jnp.float32)).astype(
        jnp.bfloat16
    )
    grad_k = lax.dynamic_slice_in_dim(key_total, parity * half, half, 1)
    grad_v = lax.dynamic_slice_in_dim(value_total, parity * half, half, 1)
    grad_weight = weight_gradient(grad_full, attended)
    return (grad_q, grad_k, grad_v, grad_weight)


def solution(mesh):
    placed = (
        P("dp", "tensor"),
        P("dp", "tensor"),
        P("dp", "tensor"),
        P(("dp", "tensor"), None),
        P("dp", "tensor"),
    )
    return jax.shard_map(
        body,
        mesh=mesh,
        in_specs=placed,
        out_specs=(P("dp", "tensor"), P("dp", "tensor"), P("dp", "tensor"), P("dp", "tensor")),
        check_vma=False,
    )
```

profile of v0, /device:TPU:0, one launch (start us, length us, event | category | flops | bytes accessed | tf_op | source)
XLA Modules:
  0.0 193.5 jit_solution(1124777499148752553)
XLA Ops:
  7.2 0.0 all-gather.3.cloned.1.call-start
  7.2 0.7 all-gather.3.cloned.1.call-update
  7.9 0.0 all-gather.5.cloned.1.call-start
  7.9 0.7 all-gather.5.cloned.1.call-update
  8.6 0.0 reduce-scatter.2.cloned.1.call-start
  8.7 3.1 %collective-permute-start = (bf16[512,64]{0,1:T(8,128)(2,1)}, bf16[512,64]{0,1:T(8,128)(2,1)S(1)}, u32[]{:S(2)}, u32[]{:S(2)}) collective-permute-start(bf16[512,64]{0,1:T(8,128)(2,1)} %param.6), channel_id=1, source_target_pairs={{0,1},{1,0},{2,3},{3,2},{4,5},{5,4},{6,7},{7,6},{8,9},{9,8},{10,11... | collective-permute-start | bytes 196616 | tf_op jit(solution)/shard_map/ppermute | solution.py:10
  11.8 0.1 collective-permute-start.1
  11.9 1.3 copy.29
  13.1 0.1 iota_compare_fusion
  13.2 0.0 copy-start
  13.2 1.2 collective-permute-done
  14.4 4.6 %fusion.47 = (f32[4,512]{1,0:T(4,128)S(1)}, f32[4,512,512]{1,2,0:T(8,128)}) fusion(pred[512,512]{0,1:T(8,128)(4,1)S(1)} %iota_compare_fusion, bf16[512,4,128]{0,2,1:T(8,128)(2,1)S(1)} %bitcast.91, bf16[512,64]{0,1:T(8,128)(2,1)S(1)} %collective-permute-done, bf16[512,64]{0,1:T(8,128)(2,1)} %param.6, pred[]{:T(512)S(6)} %eq.6), kind=kOutput, calls=%fused_computation.49 | convolution fusion | flops 273220096 | bytes 5120001 | tf_op jit(solution)/shard_map/sub | solution.py:46
  19.0 0.0 collective-permute-done.1
  19.0 3.1 %convolution_convert_fusion.2 = bf16[128,4,512]{2,0,1:T(8,128)(2,1)S(1)} fusion(bf16[512,64]{0,1:T(8,128)(2,1)S(1)} %collective-permute-done.1, bf16[512,64]{0,1:T(8,128)(2,1)S(1)} %copy-done, pred[]{:T(512)S(6)} %eq.6, f32[4,512,512]{1,2,0:T(8,128)} %get-tuple-element.9, f32[4,512]{1,0:T(4,128)S(1)} %get-tuple-element.8), kind=kOutput, calls=%fused_computation.21 | convolution fusion | flops 271384576 | bytes 4857857 | tf_op jit(solution)/shard_map/hst,td->shd/dot_general | solution.py:48
  22.0 71.0 %all-gather.3.cloned.1.call-done = bf16[512,4096]{1,0:T(8,128)(2,1)} async-done(((bf16[128,4096]{1,0:T(8,128)(2,1)}), bf16[512,4096]{1,0:T(8,128)(2,1)}) %all-gather.3.cloned.1.call-update) | async-done | bytes 4194320 | tf_op jit(solution)/shard_map/all_gather | solution.py:50
  93.1 6.5 %fusion.2 = bf16[4096,512]{0,1:T(8,128)(2,1)} fusion(bf16[512,512]{0,1:T(8,128)(2,1)S(1)} %bitcast.94, bf16[512,4096]{1,0:T(8,128)(2,1)} %all-gather.3.cloned.1.call-done), kind=kOutput, calls=%fused_computation.3 | convolution fusion | flops 2149580800 | bytes 8912896 | tf_op jit(solution)/shard_map/dot_general | solution.py:15
  99.5 0.0 reduce-scatter.2.cloned.1.call-update
  99.6 30.7 %all-gather.5.cloned.1.call-done = bf16[4096,512]{1,0:T(8,128)(2,1)} async-done(((bf16[512,512]{1,0:T(8,128)(2,1)}), bf16[4096,512]{1,0:T(8,128)(2,1)}) %all-gather.5.cloned.1.call-update) | async-done | bytes 4194320 | tf_op jit(solution)/shard_map/all_gather | solution.py:53
  130.2 6.0 %convolution_convert_fusion.1 = bf16[512,512]{0,1:T(8,128)(2,1)S(1)} fusion(bf16[512,4096]{1,0:T(8,128)(2,1)} %all-gather.3.cloned.1.call-done, bf16[4096,512]{1,0:T(8,128)(2,1)} %all-gather.5.cloned.1.call-done), kind=kOutput, calls=%fused_computation.20 | convolution fusion | flops 2147745792 | bytes 8912896 | tf_op jit(solution)/shard_map/dot_general | solution.py:51
  136.2 0.8 fusion.16
  137.0 1.6 collective-permute-start.3
  138.6 2.7 %fusion.24 = f32[512,512,4]{1,0,2:T(8,128)} fusion(bf16[512,4,128]{0,2,1:T(8,128)(2,1)S(1)} %bitcast.90, bf16[512,64]{0,1:T(8,128)(2,1)S(1)} %collective-permute-done.1, bf16[512,64]{0,1:T(8,128)(2,1)S(1)} %copy-done, pred[]{:T(512)S(6)} %eq.6), kind=kOutput, calls=%fused_computation.36 | convolution fusion | flops 269025280 | bytes 4849665 | tf_op jit(solution)/shard_map/shd,td->hst/dot_general | solution.py:57
  141.3 8.9 %fusion.15 = bf16[512,128]{0,1:T(8,128)(2,1)S(1)} fusion(bf16[512,4,128]{0,2,1:T(8,128)(2,1)S(1)} %bitcast.92, f32[512,512,4]{1,0,2:T(8,128)} %fusion.24, f32[4,512,512]{1,2,0:T(8,128)} %get-tuple-element.9, f32[4,512]{1,0:T(4,128)S(1)} %get-tuple-element.8), kind=kOutput, calls=%fused_computation.24 | convolution fusion | flops 275843584 | bytes 9052160 | tf_op jit(solution)/shard_map/hst,shd->td/dot_general | solution.py:62
  150.2 0.9 collective-permute-start.2
  151.1 8.4 %fusion.13 = bf16[128,4,512]{2,0,1:T(8,128)(2,1)S(1)} fusion(f32[512,512,4]{1,0,2:T(8,128)} %fusion.24, bf16[512,64]{0,1:T(8,128)(2,1)S(1)} %collective-permute-done, bf16[512,64]{0,1:T(8,128)(2,1)S(1)} %copy-done.1, pred[]{:T(512)S(6)} %eq.6, f32[4,512,512]{1,2,0:T(8,128)} %get-tuple-element.9, f32[4,512]{1,0:T(4,128)S(1)} %get-tuple-element.8), kind=kOutput, calls=%fused_computation.19 | convolution fusion | flops 276630016 | bytes 9052161 | tf_op jit(solution)/shard_map/hst,td->shd/dot_general | solution.py:60
  159.5 1.0 copy.18
  160.5 0.0 collective-permute-done.3
  160.5 0.6 add_convert_fusion
  161.1 0.0 collective-permute-done.2
  161.1 0.6 add_convert_fusion.1
  161.8 23.2 %reduce-scatter.2.cloned.1.call-done = bf16[512,512]{0,1:T(8,128)(2,1)} async-done(((bf16[4096,512]{0,1:T(8,128)(2,1)}), bf16[512,512]{0,1:T(8,128)(2,1)}) %reduce-scatter.2.cloned.1.call-update) | async-done | bytes 524304 | tf_op jit(solution)/shard_map/reduce_scatter | solution.py:14
  185.0 2.0 %copy.19 = bf16[512,512]{1,0:T(8,128)(2,1)} copy(bf16[512,512]{0,1:T(8,128)(2,1)} %reduce-scatter.2.cloned.1.call-done) | data formatting | bytes 1048576
  (5 shorter events, 0.0 us)
Async XLA Ops:
  7.2 85.9 %all-gather.3.cloned.1.call-start = ((), (), s32[]{:S(2)}) async-start(), calls=%async_computation.1 | async-start | bytes 5242880 | tf_op jit(solution)/shard_map/all_gather | solution.py:50
  7.9 122.3 %all-gather.5.cloned.1.call-start = ((), (), s32[]{:S(2)}) async-start(), calls=%async_computation.2 | async-start | bytes 4718592 | tf_op jit(solution)/shard_map/all_gather | solution.py:53
  8.6 176.3 %reduce-scatter.2.cloned.1.call-start = ((), (), s32[]{:S(2)}) async-start(), calls=%async_computation.3 | async-start | bytes 4718592 | tf_op jit(solution)/shard_map/reduce_scatter | solution.py:14
  8.7 5.7 %collective-permute-start = (bf16[512,64]{0,1:T(8,128)(2,1)}, bf16[512,64]{0,1:T(8,128)(2,1)S(1)}, u32[]{:S(2)}, u32[]{:S(2)}) collective-permute-start(bf16[512,64]{0,1:T(8,128)(2,1)} %param.6), channel_id=1, source_target_pairs={{0,1},{1,0},{2,3},{3,2},{4,5},{5,4},{6,7},{7,6},{8,9},{9,8},{10,11... | collective-permute-start | bytes 196616 | tf_op jit(solution)/shard_map/ppermute | solution.py:10
  11.8 7.2 %collective-permute-start.1 = (bf16[512,64]{0,1:T(8,128)(2,1)}, bf16[512,64]{0,1:T(8,128)(2,1)S(1)}, u32[]{:S(2)}, u32[]{:S(2)}) collective-permute-start(bf16[512,64]{0,1:T(8,128)(2,1)} %param.7), channel_id=1, source_target_pairs={{0,1},{1,0},{2,3},{3,2},{4,5},{5,4},{6,7},{7,6},{8,9},{9,8},{10,11... | collective-permute-start | bytes 196616 | tf_op jit(solution)/shard_map/ppermute | solution.py:10
  13.2 5.8 %copy-start = (bf16[512,64]{0,1:T(8,128)(2,1)S(1)}, bf16[512,64]{0,1:T(8,128)(2,1)}, u32[]{:S(2)}) copy-start(bf16[512,64]{0,1:T(8,128)(2,1)} %param.7) | copy-start | bytes 196612
  130.2 6.0 %copy-start.2 = (f32[4,512,512]{1,2,0:T(8,128)S(1)}, f32[4,512,512]{1,2,0:T(8,128)}, u32[]{:S(2)}) copy-start(f32[4,512,512]{1,2,0:T(8,128)} %get-tuple-element.9) | copy-start | bytes 12582916
  137.0 23.4 %collective-permute-start.3 = (bf16[512,128]{0,1:T(8,128)(2,1)S(1)}, bf16[512,128]{0,1:T(8,128)(2,1)S(1)}, u32[]{:S(2)}, u32[]{:S(2)}) collective-permute-start(bf16[512,128]{0,1:T(8,128)(2,1)S(1)} %fusion.16), channel_id=1, source_target_pairs={{0,1},{1,0},{2,3},{3,2},{4,5},{5,4},{6,7},{7,6},{8,9},{9,8},{10,11... | collective-permute-start | bytes 393224 | tf_op jit(solution)/shard_map/ppermute | solution.py:10
  141.3 9.8 %copy-start.1 = (bf16[512,64]{0,1:T(8,128)(2,1)S(1)}, bf16[512,64]{0,1:T(8,128)(2,1)}, u32[]{:S(2)}) copy-start(bf16[512,64]{0,1:T(8,128)(2,1)} %param.6) | copy-start | bytes 196612
  150.2 11.0 %collective-permute-start.2 = (bf16[512,128]{0,1:T(8,128)(2,1)S(1)}, bf16[512,128]{0,1:T(8,128)(2,1)S(1)}, u32[]{:S(2)}, u32[]{:S(2)}) collective-permute-start(bf16[512,128]{0,1:T(8,128)(2,1)S(1)} %fusion.15), channel_id=1, source_target_pairs={{0,1},{1,0},{2,3},{3,2},{4,5},{5,4},{6,7},{7,6},{8,9},{9,8},{10,11... | collective-permute-start | bytes 393224 | tf_op jit(solution)/shard_map/ppermute | solution.py:10
Sparse Core Ops, SparseCore 0:
  9.6 83.4 all-gather.2
  94.9 35.2 all-gather.4
  133.6 51.3 reduce-scatter.1
where the time goes:
time: 194 us
  waiting for transfers between devices  127 us (65%)
  matrix products  40.9 us (21%)
  between operations  13.8 us (7%)
  starting transfers between devices  5.72 us (3%)
  local copies, waits for them, and re-layouts  4.32 us (2%)
    all_gather x1, waiting for transfers between devices, body(): grad_full = lax.all_gather(grad_out, 'tensor', axis=0, tiled=True)  71 us
    all_gather x1, waiting for transfers between devices, body(): lax.all_gather(out_weight, 'dp', axis=0, tiled=True)  30.7 us
    reduce_scatter x1, waiting for transfers between devices, weight_gradient(): lax.psum_scatter(lax.dot_general(grad_full, attended, (((0,), (0,)), ((),...  23.2 us
    dot_general x1, matrix products, body(): jnp.einsum('hst,shd->td', dscores, query_heads, preferred_element_type=jn...  8.86 us
    dot_general x1, matrix products, body(): jnp.einsum('hst,td->shd', dscores, key_full, preferred_element_type=jnp.f...  8.42 us
    dot_general x1, matrix products, weight_gradient(): lax.dot_general(grad_full, attended, (((0,), (0,)), ((), ())), preferred_...  6.47 us
    dot_general x1, matrix products, body(): jnp.dot(grad_full, lax.all_gather(out_weight, 'dp', axis=0, tiled=True),...  5.97 us
    ppermute x4, starting transfers between devices, partner(): lax.ppermute(value, axis, [(i, i ^ 1 << apart) for i in range(lax.axis_si...  5.61 us
  transfers between devices with their start and end apart: 7, of which 4 were waited for; matrix products, arithmetic and copies ran while one was open for 23% of the time, Pallas kernels for 0%

commit v1 on v0

v1 whole, which is shorter than its diff:
```python
import functools
import math

import jax
import jax.numpy as jnp
from jax import lax
from jax.experimental import pallas as pl
from jax.experimental.pallas import tpu as pltpu
from jax.sharding import PartitionSpec as P

HEAD_DIM = 128
BLOCK = 128
VMEM_BYTES = 20 * 1024 * 1024
SLOTS = 4
SCALE = HEAD_DIM ** (-0.5)
SCALE2 = SCALE * math.log2(math.e)
VMEM = pl.BlockSpec(memory_space=pltpu.VMEM)
SMEM = pl.BlockSpec(memory_space=pltpu.SMEM)
F32 = jnp.float32
BF16 = jnp.bfloat16


def call(kernel, outs, args, flops, scratch=(), scalars=0):
    size = sum(math.prod(a.shape) * a.dtype.itemsize for a in list(args) + list(outs))
    return pl.pallas_call(
        kernel,
        out_shape=tuple(outs),
        in_specs=[SMEM] * scalars + [VMEM] * (len(args) - scalars),
        out_specs=tuple([VMEM] * len(outs)),
        scratch_shapes=list(scratch),
        cost_estimate=pl.CostEstimate(flops=flops, bytes_accessed=size // 100, transcendentals=0),
        compiler_params=pltpu.CompilerParams(vmem_limit_bytes=VMEM_BYTES),
    )(*args)


def dot(a, b, ca, cb):
    return lax.dot_general(a, b, (((ca,), (cb,)), ((), ())), preferred_element_type=F32)


def prep_kernel(order, place, keys, values, grad, own, own_kv, give):
    core, chip = place[0], place[1]
    chips, rows, width = own.shape
    half, length = keys.shape
    for k, s in enumerate(order):
        first = (chip ^ s) * 2
        own[k] = grad[:, pl.ds(pl.multiple_of((first + core) * width, 128), width)]
        own_kv[k * rows : (k + 1) * rows, :] = own[k]
        give[k] = grad[:, pl.ds(pl.multiple_of((first + 1 - core) * width, 128), width)]
    for i in range(length // width):
        at = chips * rows + i * 2 * half
        own_kv[at : at + half, :] = keys[:, i * width : (i + 1) * width]
        own_kv[at + half : at + 2 * half, :] = values[:, i * width : (i + 1) * width]


def forward_kernel(place, queries, keys, values, near, kv, attended, lse):
    parity = place[2]
    half, length = keys.shape
    depth = near.shape[1]
    mine = pl.multiple_of(parity * half, half)
    theirs = pl.multiple_of((1 - parity) * half, half)
    tail = near.shape[0] - length // depth * 2 * half
    for part, ref in enumerate((keys, values)):
        kv[part, pl.ds(mine, half), :] = ref[...]
        for i in range(length // depth):
            at = tail + (2 * i + part) * half
            kv[part, pl.ds(theirs, half), i * depth : (i + 1) * depth] = near[at : at + half, :]
    length, width = queries.shape
    row = lax.broadcasted_iota(jnp.int32, (BLOCK, BLOCK), 0)
    col = lax.broadcasted_iota(jnp.int32, (BLOCK, BLOCK), 1)
    for i in range(length // BLOCK):
        rows = pl.ds(i * BLOCK, BLOCK)
        keys = (i + 1) * BLOCK
        stats = []
        for h in range(width // HEAD_DIM):
            cols = pl.ds(h * HEAD_DIM, HEAD_DIM)
            scores = dot(queries[rows, cols], kv[0, :, :keys], 1, 0) * SCALE2
            last = jnp.where(col <= row, scores[:, keys - BLOCK :], -jnp.inf)
            top = jnp.max(last, axis=1, keepdims=True)
            if i:
                top = jnp.maximum(top, jnp.max(scores[:, : keys - BLOCK], axis=1, keepdims=True))
            powers = jnp.exp2(last - top)
            total = jnp.sum(powers, axis=1, keepdims=True)
            if i:
                early = jnp.exp2(scores[:, : keys - BLOCK] - top)
                total = total + jnp.sum(early, axis=1, keepdims=True)
                powers = jnp.concatenate([early, powers], axis=1)
            probs = (powers / total).astype(BF16)
            attended[rows, cols] = dot(probs, kv[1, :, :keys], 1, 1).astype(BF16)
            stats.append(jnp.broadcast_to(top + jnp.log2(total), (BLOCK, HEAD_DIM)))
        lane = lax.broadcasted_iota(jnp.int32, (BLOCK, HEAD_DIM), 1)
        packed = stats[0]
        for h, stat in enumerate(stats):
            packed = jnp.where(lane == h, stat, packed)
        lse[rows, :] = packed


def backward_kernel(first, final, base, place, queries, kv, lse, grad_own, grad_other, *refs):
    if not first:
        early_q, early_k, early_v = refs[:3]
        refs = refs[3:]
    if final:
        grad_q, keep, send, dk, dv, ds_all, p_all = refs
    else:
        grad_q, dk, dv, ds_all, p_all = refs
    if first:
        dk[...] = jnp.zeros_like(dk)
        dv[...] = jnp.zeros_like(dv)
    else:
        grad_q[...] = early_q[...]
        dk[...] = early_k[...]
        dv[...] = early_v[...]
    length, width = queries.shape
    heads = width // HEAD_DIM
    count, size, _ = grad_own.shape
    row = lax.broadcasted_iota(jnp.int32, (size, BLOCK), 0)
    col = lax.broadcasted_iota(jnp.int32, (size, BLOCK), 1)

    def block(slot, j):
        rows = pl.ds(j * size, size)
        keys = -(-(j + 1) * size // BLOCK) * BLOCK
        early = keys - BLOCK
        grads = []
        for h in range(heads):
            cols = pl.ds(h * HEAD_DIM, HEAD_DIM)
            grad = grad_own[slot, :, cols] + grad_other[slot, :, cols].astype(F32)
            grad = grad.astype(BF16)
            grads.append(grad)
            scores = dot(queries[rows, cols], kv[0, :, :keys], 1, 0) * SCALE2
            probs = jnp.exp2(scores - lse[rows, h : h + 1])
            last = jnp.where(col + early <= row + j * size, probs[:, early:], 0.0)
            probs = jnp.concatenate([probs[:, :early], last], axis=1) if early else last
            dprobs = dot(grad, kv[1, :, :keys], 1, 0)
            delta = jnp.sum(probs * dprobs, axis=1, keepdims=True)
            dscores = (probs * (dprobs - delta) * SCALE).astype(BF16)
            grad_q[rows, cols] = dot(dscores, kv[0, :, :keys], 1, 1).astype(BF16)
            ds_all[pl.ds(h * size, size), :keys] = dscores
            p_all[pl.ds(h * size, size), :keys] = probs.astype(BF16)
        stacked_q = jnp.concatenate(
            [queries[rows, h * HEAD_DIM : (h + 1) * HEAD_DIM] for h in range(heads)], axis=0
        )
        stacked_g = jnp.concatenate(grads, axis=0)
        dk[:, :keys] += dot(stacked_q, ds_all[:, :keys], 0, 0)
        dv[:, :keys] += dot(stacked_g, p_all[:, :keys], 0, 0)

    def step(slot, carry):
        for j in range(length // size):
            pl.when(place[SLOTS + base + slot] == j)(functools.partial(block, slot, j))
        return carry

    lax.fori_loop(0, count, step, 0)
    if final:
        half = HEAD_DIM // 2
        mine = pl.ds(pl.multiple_of(place[2] * half, half), half)
        theirs = pl.ds(pl.multiple_of((1 - place[2]) * half, half), half)
        keep[:half] = dk[mine, :]
        keep[half:] = dv[mine, :]
        send[:half] = dk[theirs, :].astype(BF16)
        send[half:] = dv[theirs, :].astype(BF16)


def finish_kernel(keep, other, partial, *refs):
    received, (grad_k, grad_v, grad_weight) = refs[:-3], refs[-3:]
    half = keep.shape[0] // 2
    total = (keep[...].astype(BF16).astype(F32) + other[...].astype(F32)).astype(BF16)
    grad_k[...] = total[:half]
    grad_v[...] = total[half:]
    total = partial[...]
    for ref in received:
        total = total + ref[...].astype(F32)
    grad_weight[...] = total.astype(BF16)


def chunk(ref, c, rows):
    return ref[c] if len(ref.shape) == 3 else ref[c * rows : (c + 1) * rows, :]


def merge_kernel(first, second, *halves):
    rows = second.shape[1]
    c = 0
    for half in halves:
        for i in range(half.shape[0]):
            half[i, :rows] = chunk(first, c, rows)
            half[i, rows:] = second[c]
            c += 1


def pieces(place, refs, c):
    rows = refs[1].shape[1]
    both = [
        jnp.concatenate([chunk(refs[i], c, rows), refs[i + 1][c]], axis=0)
        for i in range(0, len(refs), 2)
    ]
    if len(both) != 4:
        return both
    inner = (place[3] == 1) | (place[3] == 2)
    return both[:2] + [jnp.where(inner, both[2], both[3])]


def late_piece(place, refs, i):
    inner = (place[3] == 1) | (place[3] == 2)
    return jnp.where(inner, refs[0][i], refs[1][i])


def attended_rows(att_own, att_other, j, rows):
    at = pl.ds(pl.multiple_of(j * rows, rows), rows)
    return jnp.concatenate([att_own[at, :], att_other[at, :]], axis=0)


def early_kernel(count, place, *refs):
    blocks, weights, (own, give) = refs[:count], refs[count:-2], refs[-2:]
    rows = own.shape[1]
    totals = None
    for c, weight in enumerate(weights):
        products = [dot(value, weight[...], 1, 0) for value in pieces(place, blocks, c)]
        totals = [a + b for a, b in zip(totals, products)] if totals else products
    for i, total in enumerate(totals):
        own[i] = total[:rows]
        give[i] = total[rows:].astype(BF16)


def early_term_kernel(count, place, att_own, att_other, *refs):
    blocks, outs = refs[:count], refs[count:]
    rows = blocks[1].shape[1]
    for c, out in enumerate(outs):
        total = None
        for i, value in enumerate(pieces(place, blocks, c)):
            product = dot(value, attended_rows(att_own, att_other, place[SLOTS + i], rows), 0, 0)
            total = product if total is None else total + product
        out[...] = total.astype(BF16)


def late_kernel(sizes, steps, first, place, *refs):
    late, refs = refs[: 2 * len(steps)], refs[2 * len(steps) :]
    count = sum(sizes[side] for side in steps)
    weights, refs = refs[:count], refs[count:]
    total = None if first else refs[0][...]
    c = 0
    for n, side in enumerate(steps):
        for i in range(sizes[side]):
            value = late_piece(place, late[2 * n : 2 * n + 2], i)
            product = dot(value, weights[c][...], 1, 0)
            total = product if total is None else total + product
            c += 1
    if first:
        refs[0][...] = total
    else:
        own, give = refs[1:]
        rows = own.shape[1]
        own[0] = total[:rows]
        give[0] = total[rows:].astype(BF16)


def term_kernel(i, late, spans, place, att_own, att_other, partial, *refs):
    received, outs = refs[late : late + len(spans)], refs[late + len(spans) :]
    total = partial[...].astype(F32)
    if late:
        value = late_piece(place, refs[:late], i)
        rhs = attended_rows(att_own, att_other, place[place.shape[0] - 1], value.shape[0] // 2)
        total = total + dot(value, rhs, 0, 0)
    middle = total.shape[0] // 2
    sides = [total[:middle], total[middle:]]
    for ref, span in zip(received, spans):
        for side in span:
            part = ref[...] if len(span) == 1 else ref[side * middle : (side + 1) * middle]
            sides[side] = sides[side] + part.astype(F32)
    if len(outs) == 2:
        for out, side in zip(outs, sides):
            out[...] = side.astype(out.dtype)
    else:
        outs[0][:middle] = sides[0].astype(outs[0].dtype)
        outs[0][middle:] = sides[1].astype(outs[0].dtype)


def tie(value, *others):
    return lax.optimization_barrier((value, *others))[0]


def body(queries, keys, values, grad_out, out_weight):
    dp, tensor = lax.axis_size("dp"), lax.axis_size("tensor")
    chips = dp // 2
    length, width = queries.shape
    half = keys.shape[1]
    rows = grad_out.shape[0]
    depth = out_weight.shape[0]
    index, part = lax.axis_index("dp"), lax.axis_index("tensor")
    if tensor == 4:
        inner = (part == 1) | (part == 2)
        early = 3
        slots = [0, 1, jnp.where(inner, 3, 2), jnp.where(inner, 2, 3)]
    else:
        early = tensor
        slots = list(range(tensor))
    place = jnp.stack(
        [index % 2, index // 2, part % 2, part] + [part ^ k for k in slots]
    ).astype(jnp.int32)

    def swap(value, axis, mask):
        return lax.ppermute(value, axis, [(i, i ^ mask) for i in range(lax.axis_size(axis))])

    def across(value):
        return lax.ppermute(value, "tensor", [(1, 2), (2, 1)])

    def outward(value):
        return lax.ppermute(value, "tensor", [(1, 0), (2, 3)])

    shape = jax.ShapeDtypeStruct
    order = sorted(range(chips), key=lambda s: (-s.bit_count(), s))
    half_block = shape((chips, rows, depth), BF16)
    tail = length // depth * 2 * half
    own, own_kv, give = call(
        functools.partial(prep_kernel, order),
        [half_block, shape((chips * rows + tail, depth), BF16), half_block],
        [place, keys.T, values.T, grad_out],
        0,
        scalars=1,
    )
    taken = swap(give, "dp", 1)

    near = [swap(own_kv, "tensor", 1), swap(taken, "tensor", 1)]
    weights = {0: out_weight}
    for s in reversed(order[:-1]):
        operand = tie(out_weight, near[0]) if s & (s - 1) else out_weight
        weights[s] = swap(operand, "dp", 2 * s)
    weights = [weights[s] for s in order]

    blocks = [own_kv, taken] + near
    late, second = [], []
    sizes = [1, chips - 2, 1] if chips > 2 else [1] * chips
    flops = 4 * length * depth * width // 100
    if tensor == 4:
        middle_own = across(own)
        direct = [w for s, w in zip(order, weights) if s & (s - 1) == 0]
        middle_taken = across(tie(taken, middle_own, near[0]))
        hold = []
        kv, attended, lse = call(
            forward_kernel,
            [
                shape((2, HEAD_DIM, length), BF16),
                shape((length, width), BF16),
                shape((length, HEAD_DIM), F32),
            ],
            [place, tie(queries, *hold), keys.T, values.T, near[0]],
            4 * length * length * width // 100,
            scalars=1,
        )
        in_own = outward(middle_own)
        in_taken = outward(tie(middle_taken, near[1]))
        blocks += [middle_own, middle_taken, in_own, in_taken]
        att_other = swap(attended, "dp", 1)
        relay = call(
            merge_kernel,
            [shape((size, 2 * rows, depth), BF16) for size in sizes],
            near,
            400 * flops,
        )
        after = [[middle_taken, attended, *direct], [in_own, weights[0], att_other], []]
        for side in range(len(sizes)):
            second.append(across(tie(relay[side], *after[side], *second[-1:])))
    else:
        hold = []
        kv, attended, lse = call(
            forward_kernel,
            [
                shape((2, HEAD_DIM, length), BF16),
                shape((length, width), BF16),
                shape((length, HEAD_DIM), F32),
            ],
            [place, tie(queries, *hold), keys.T, values.T, near[0]],
            4 * length * length * width // 100,
            scalars=1,
        )
        att_other = swap(attended, "dp", 1)
        for k in range(2, tensor):
            blocks += [swap(own, "tensor", k), swap(taken, "tensor", k)]
    grad_own, grad_give = call(
        functools.partial(early_kernel, len(blocks)),
        [shape((early, rows, width), F32), shape((early, rows, width), BF16)],
        [place] + blocks + weights,
        300 * flops,
        scalars=1,
    )
    partials = call(
        functools.partial(early_term_kernel, len(blocks)),
        [shape((depth, width), BF16)] * chips,
        [tie(place, grad_give), attended, att_other] + blocks,
        flops,
        scalars=1,
    )
    grad_other = swap(grad_give, "dp", 1)
    if tensor == 4:
        after = [[], [in_taken, partials[0]], []]
        for side, size in enumerate(sizes):
            arrived = outward(tie(second[side], *after[side]))
            late += [(i, [second[side], arrived]) for i in range(size)]
    else:
        late = [(0, [])] * chips

    def backward(first, final, base, own, other, carry):
        state = [shape((HEAD_DIM, length), F32)] * 2
        ends = [shape((2 * half, length), F32), shape((2 * half, length), BF16)]
        size = (width // HEAD_DIM * rows, length)
        scratch = [pltpu.VMEM(size, BF16)] * 2
        if final:
            scratch = [pltpu.VMEM((HEAD_DIM, length), F32)] * 2 + scratch
        return call(
            functools.partial(backward_kernel, first, final, base),
            [shape((length, width), BF16)] + (ends if final else state),
            [place, queries, kv, lse, own, other] + carry,
            flops,
            scratch=scratch,
            scalars=1,
        )

    received = {s: [] for s in order}

    def term(c, *others, kind=BF16):
        s = order[c]
        low, high = s & -s, 1 << s.bit_length() >> 1
        spans, extra = zip(*received[s]) if received[s] and s else ((), ())
        shapes = [(depth, width)] if low == high else [(depth // 2, width)] * 2
        found = call(
            functools.partial(term_kernel, late[c][0], len(late[c][1]), spans),
            [shape(size, kind) for size in shapes],
            [tie(place, *others), attended, att_other, partials[c]]
            + late[c][1]
            + list(extra),
            300 * flops,
            scalars=1,
        )
        if len(found) == 2:
            received[s ^ low].append(((0,), swap(found[0], "dp", 2 * low)))
            received[s ^ high].append(((1,), swap(found[1], "dp", 2 * high)))
        elif s:
            received[0].append(((0, 1), swap(found[0], "dp", 2 * s)))
        return found[0]

    terms = [term(0)]
    done = backward(
        True,
        early == tensor,
        0,
        grad_own,
        tie(grad_other, terms[0]),
        [],
    )
    terms += [term(c, done[1]) for c in range(1, chips - 1)]

    if tensor == 4:
        pairs = [pair for i, pair in late if i == 0]
        steps = list(range(len(sizes)))
        (total,) = call(
            functools.partial(late_kernel, sizes, steps[:-1], True),
            [shape((2 * rows, width), F32)],
            [tie(place, terms[-1])] + sum(pairs[:-1], []) + weights[: -sizes[-1]],
            flops,
            scalars=1,
        )
        grad_own, grad_give = call(
            functools.partial(late_kernel, sizes, steps[-1:], False),
            [shape((1, rows, width), F32), shape((1, rows, width), BF16)],
            [place] + pairs[-1] + weights[-sizes[-1] :] + [total],
            flops,
            scalars=1,
        )
        grad_other = swap(grad_give, "dp", 1)
        done = backward(False, True, early, grad_own, grad_other, list(done))
    grad_q, keep, send = done
    grad_k, grad_v, grad_weight = call(
        finish_kernel,
        [shape((half, length), BF16)] * 2 + [shape((depth, width), BF16)],
        [keep, swap(send, "tensor", 1), term(chips - 1, kind=F32)]
        + [value for _, value in received[0]],
        flops,
    )
    return grad_q, grad_k.T, grad_v.T, grad_weight


def solution(mesh):
    placed = (
        P("dp", "tensor"),
        P("dp", "tensor"),
        P("dp", "tensor"),
        P(("dp", "tensor"), None),
        P("dp", "tensor"),
    )
    return jax.shard_map(
        body,
        mesh=mesh,
        in_specs=placed,
        out_specs=(P("dp", "tensor"), P("dp", "tensor"), P("dp", "tensor"), P("dp", "tensor")),
        check_vma=False,
    )
```

time: 194 us -> 98.2 us (0.51)
  waiting for transfers between devices: 127 us -> 40.7 us
  matrix products: 40.9 us -> 0 us
  starting transfers between devices: 5.72 us -> 30.1 us
  Pallas kernels: 0 us -> 23.2 us
  between operations: 13.8 us -> 0.94 us
    all_gather x2 -> x0, waiting for transfers between devices: 102 us -> none  [the longest x1 71 us: body(): grad_full = lax.all_gather(grad_out, 'tensor', axis=0, tiled=True)]
    ppermute x4 -> x24, waiting for transfers between devices: 1.19 us -> 40.7 us  [the longest x5 24.7 us: outward(): return lax.ppermute(value, 'tensor', [(1, 0), (2, 3)])]
    dot_general x7 -> x0, matrix products: 36.3 us -> none  [the longest x1 8.86 us: body(): jnp.einsum('hst,shd->td', dscores, query_heads, preferred_element_type=jn...]
    ppermute x4 -> x24, starting transfers between devices: 5.61 us -> 30.1 us  [the longest x14 20.2 us: swap(): lax.ppermute(value, axis, [(i, i ^ mask) for i in range(lax.axis_size(axi...]
    pallas_call x0 -> x14, Pallas kernels: none -> 23.2 us  [call(): pl.pallas_call(kernel, out_shape=tuple(outs), in_specs=[SMEM] * scalars +...]
    reduce_scatter x1 -> x0, waiting for transfers between devices: 23.2 us -> none  [weight_gradient(): lax.psum_scatter(lax.dot_general(grad_full, attended, (((0,), (0,)), ((),...]
    sub x1 -> x0, matrix products: 4.55 us -> none  [body(): probs = jax.nn.softmax(scores, axis=-1)]
  transfers between devices with their start and end apart: 7 -> 24, of which waited for: 4 -> 9; matrix products, arithmetic and copies ran while one was open for 23% -> 0% of each run, Pallas kernels for 0% -> 22%
where the time goes in v1:
time: 98.2 us; the launch traced here: 97.8 us
  waiting for transfers between devices  40.7 us (41%)
  starting transfers between devices  30.1 us (31%)
  Pallas kernels  23.2 us (24%)
  local copies, waits for them, and re-layouts  2.87 us (3%)
    ppermute x5, waiting for transfers between devices, outward(): return lax.ppermute(value, 'tensor', [(1, 0), (2, 3)])  24.7 us
    pallas_call x14, Pallas kernels, call(): pl.pallas_call(kernel, out_shape=tuple(outs), in_specs=[SMEM] * scalars +...  23.2 us
    ppermute x14, starting transfers between devices, swap(): lax.ppermute(value, axis, [(i, i ^ mask) for i in range(lax.axis_size(axi...  20.2 us
    ppermute x14, waiting for transfers between devices, swap(): lax.ppermute(value, axis, [(i, i ^ mask) for i in range(lax.axis_size(axi...  15.9 us
    ppermute x5, starting transfers between devices, outward(): return lax.ppermute(value, 'tensor', [(1, 0), (2, 3)])  6.46 us
    ppermute x5, starting transfers between devices, across(): return lax.ppermute(value, 'tensor', [(1, 2), (2, 1)])  3.41 us
    unnamed x10, local copies, waits for them, and re-layouts  2.78 us
  transfers between devices with their start and end apart: 24, of which 9 were waited for; matrix products, arithmetic and copies ran while one was open for 0% of the time, Pallas kernels for 22%

profile of v1, /device:TPU:0, one launch (start us, length us, event | category | flops | bytes accessed | tf_op | source)
XLA Modules:
  0.0 97.8 jit_solution(17645817149156057377)
XLA Ops:
  1.5 1.2 %copy-done.2 = bf16[128,4096]{1,0:T(8,128)(2,1)S(1)} copy-done((bf16[128,4096]{1,0:T(8,128)(2,1)S(1)}, bf16[128,4096]{1,0:T(8,128)(2,1)}, u32[]{:S(2)}) %copy-start.2) | copy-done | bytes 1048600
  4.7 2.6 %collective-permute-start = (bf16[640,512]{1,0:T(8,128)(2,1)S(1)}, bf16[640,512]{1,0:T(8,128)(2,1)S(1)}, u32[]{:S(2)}, u32[]{:S(2)}) collective-permute-start(bf16[640,512]{1,0:T(8,128)(2,1)S(1)} %get-tuple-element.43.refs_0_), channel_id=1, source_target_pairs={{0,1},{1,0},{2,3},{3,2},{4,5},{5,4},{6,7},{7,6},{8,9},{9,8},{10,11... | collective-permute-start | bytes 1966088 | tf_op jit(solution)/shard_map/ppermute | solution.py:298
  8.1 1.6 %collective-permute-start.8 = (bf16[512,512]{1,0:T(8,128)(2,1)S(1)}, bf16[512,512]{1,0:T(8,128)(2,1)S(1)}, u32[]{:S(2)}, u32[]{:S(2)}) collective-permute-start(bf16[512,512]{1,0:T(8,128)(2,1)S(1)} %copy-done.1), channel_id=1, source_target_pairs={{0,8},{4,12},{8,0},{12,4},{16,24},{20,28},{24,16},{28,20},{1,9},{5... | collective-permute-start | bytes 1572872 | tf_op jit(solution)/shard_map/ppermute | solution.py:298
  9.6 4.4 %collective-permute-start.2 = (bf16[4,128,512]{2,1,0:T(8,128)(2,1)S(1)}, bf16[4,128,512]{2,1,0:T(8,128)(2,1)S(1)}, u32[]{:S(2)}, u32[]{:S(2)}) collective-permute-start(bf16[4,128,512]{2,1,0:T(8,128)(2,1)S(1)} %collective-permute-done.1.refs_1_), channel_id=1, source_target_pairs={{0,1},{1,0},{2,3},{3,2},{4,5},{5,4},{6,7},{7,6},{8,9},{9,8},{10,11... | collective-permute-start | bytes 1572872 | tf_op jit(solution)/shard_map/ppermute | solution.py:298
  14.0 1.5 %collective-permute-start.9 = (bf16[512,512]{1,0:T(8,128)(2,1)S(1)}, bf16[512,512]{1,0:T(8,128)(2,1)S(1)}, u32[]{:S(2)}, u32[]{:S(2)}) collective-permute-start(bf16[512,512]{1,0:T(8,128)(2,1)S(1)} %copy-done.1), channel_id=1, source_target_pairs={{0,16},{4,20},{8,24},{12,28},{16,0},{20,4},{24,8},{28,12},{1,17},{... | collective-permute-start | bytes 1572872 | tf_op jit(solution)/shard_map/ppermute | solution.py:298
  15.5 7.4 %collective-permute-done.near.first.refs_2_ = bf16[640,512]{1,0:T(8,128)(2,1)S(1)} collective-permute-done((bf16[640,512]{1,0:T(8,128)(2,1)S(1)}, bf16[640,512]{1,0:T(8,128)(2,1)S(1)}, u32[]{:S(2)}, u32[]{:S(2)}) %collective-permute-start) | collective-permute-done | bytes 655392 | tf_op jit(solution)/shard_map/ppermute | solution.py:298
  23.6 1.3 %collective-permute-start.4 = (bf16[4,128,512]{2,1,0:T(8,128)(2,1)S(1)}, bf16[4,128,512]{2,1,0:T(8,128)(2,1)S(1)}, u32[]{:S(2)}, u32[]{:S(2)}) collective-permute-start(bf16[4,128,512]{2,1,0:T(8,128)(2,1)S(1)} %collective-permute-done.3.refs_4_), channel_id=1, source_target_pairs={{1,0},{2,3},{5,4},{6,7},{9,8},{10,11},{13,12},{14,15},{17,16},{18,... | collective-permute-start | bytes 1572872 | tf_op jit(solution)/shard_map/ppermute | solution.py:304
  25.0 4.2 %shard_map.85 = (bf16[2,128,512]{2,1,0:T(8,128)(2,1)S(1)}, bf16[512,512]{1,0:T(8,128)(2,1)S(1)}, f32[512,128]{1,0:T(8,128)S(1)}) custom-call(s32[8]{0:T(128)S(1)} %stack.32.place, bf16[512,512]{1,0:T(8,128)(2,1)S(1)} %copy-done, bf16[64,512]{1,0:T(8,128)(2,1)S(1)} %bitcast.12, bf16[64,512]{1,0:T(8,128)(2,1)S(1)} %bitcast.14, ...), custom_call_target="tpu_custom_call" | custom-call | flops 5368709 | bytes 23593 | tf_op jit(solution)/shard_map/pallas_call | solution.py:25
  29.2 2.9 %collective-permute-start.5 = (bf16[512,512]{1,0:T(8,128)(2,1)S(1)}, bf16[512,512]{1,0:T(8,128)(2,1)S(1)}, u32[]{:S(2)}, u32[]{:S(2)}) collective-permute-start(bf16[512,512]{1,0:T(8,128)(2,1)S(1)} %copy-done.1), channel_id=1, source_target_pairs={{0,24},{4,28},{8,16},{12,20},{16,8},{20,12},{24,0},{28,4},{1,25},{... | collective-permute-start | bytes 1572872 | tf_op jit(solution)/shard_map/ppermute | solution.py:298
  32.0 2.1 %collective-permute-done.2.second.refs_3_ = bf16[4,128,512]{2,1,0:T(8,128)(2,1)S(1)} collective-permute-done((bf16[4,128,512]{2,1,0:T(8,128)(2,1)S(1)}, bf16[4,128,512]{2,1,0:T(8,128)(2,1)S(1)}, u32[]{:S(2)}, u32[]{:S(2)}) %collective-permute-start.2) | collective-permute-done | bytes 524320 | tf_op jit(solution)/shard_map/ppermute | solution.py:298
  35.0 1.3 %collective-permute-start.14 = (bf16[4,128,512]{2,1,0:T(8,128)(2,1)S(1)}, bf16[4,128,512]{2,1,0:T(8,128)(2,1)S(1)}, u32[]{:S(2)}, u32[]{:S(2)}) collective-permute-start(bf16[4,128,512]{2,1,0:T(8,128)(2,1)S(1)} %collective-permute-done.7.refs_5_), channel_id=1, source_target_pairs={{1,0},{2,3},{5,4},{6,7},{9,8},{10,11},{13,12},{14,15},{17,16},{18,... | collective-permute-start | bytes 1572872 | tf_op jit(solution)/shard_map/ppermute | solution.py:304
  36.3 9.2 %collective-permute-done.4.refs_6_ = bf16[4,128,512]{2,1,0:T(8,128)(2,1)S(1)} collective-permute-done((bf16[4,128,512]{2,1,0:T(8,128)(2,1)S(1)}, bf16[4,128,512]{2,1,0:T(8,128)(2,1)S(1)}, u32[]{:S(2)}, u32[]{:S(2)}) %collective-permute-start.4) | collective-permute-done | bytes 524320 | tf_op jit(solution)/shard_map/ppermute | solution.py:304
  46.1 1.3 %collective-permute-start.16 = (bf16[1,256,512]{2,1,0:T(8,128)(2,1)S(1)}, bf16[1,256,512]{2,1,0:T(8,128)(2,1)S(1)}, u32[]{:S(2)}, u32[]{:S(2)}) collective-permute-start(bf16[1,256,512]{2,1,0:T(8,128)(2,1)S(1)} %collective-permute-done.10.refs_0_), channel_id=1, source_target_pairs={{1,0},{2,3},{5,4},{6,7},{9,8},{10,11},{13,12},{14,15},{17,16},{18,... | collective-permute-start | bytes 786440 | tf_op jit(solution)/shard_map/ppermute | solution.py:304
  47.4 10.0 %collective-permute-done.14.refs_7_ = bf16[4,128,512]{2,1,0:T(8,128)(2,1)S(1)} collective-permute-done((bf16[4,128,512]{2,1,0:T(8,128)(2,1)S(1)}, bf16[4,128,512]{2,1,0:T(8,128)(2,1)S(1)}, u32[]{:S(2)}, u32[]{:S(2)}) %collective-permute-start.14) | collective-permute-done | bytes 524320 | tf_op jit(solution)/shard_map/ppermute | solution.py:304
  57.5 2.3 %shard_map.87 = (f32[3,128,512]{2,1,0:T(8,128)S(1)}, bf16[3,128,512]{2,1,0:T(8,128)(2,1)S(1)}) custom-call(s32[8]{0:T(128)S(1)} %stack.32.place, bf16[640,512]{1,0:T(8,128)(2,1)S(1)} %get-tuple-element.43.refs_0_, bf16[4,128,512]{2,1,0:T(8,128)(2,1)S(1)} %collective-permute-done.1.refs_1_, bf16[640,512]{1,0:T(8,128)(2,1)S(1)} %collective-permute-done.near.first.refs_2_, ...), custom_call_target="tpu_custom_call" | custom-call | flops 1610612736 | bytes 77332 | tf_op jit(solution)/shard_map/pallas_call | solution.py:25
  59.8 2.4 %shard_map.88 = (bf16[512,512]{1,0:T(8,128)(2,1)S(1)}, bf16[512,512]{1,0:T(8,128)(2,1)S(1)}, bf16[512,512]{1,0:T(8,128)(2,1)S(1)}, bf16[512,512]{1,0:T(8,128)(2,1)S(1)}) custom-call(s32[8]{0:T(128)S(1)} %stack.32.place, bf16[512,512]{1,0:T(8,128)(2,1)S(1)} %get-tuple-element.51.att_own, bf16[512,512]{1,0:T(8,128)(2,1)S(1)} %collective-permute-done.6.att_other, ...), custom_call_target="tpu_custom_call" | custom-call | flops 5368709 | bytes 76022 | tf_op jit(solution)/shard_map/pallas_call | solution.py:25
  62.2 1.3 %collective-permute-start.17 = (bf16[2,256,512]{2,1,0:T(8,128)(2,1)S(1)}, bf16[2,256,512]{2,1,0:T(8,128)(2,1)S(1)}, u32[]{:S(2)}, u32[]{:S(2)}) collective-permute-start(bf16[2,256,512]{2,1,0:T(8,128)(2,1)S(1)} %collective-permute-done.11.refs_0_.refs_2_), channel_id=1, source_target_pairs={{1,0},{2,3},{5,4},{6,7},{9,8},{10,11},{13,12},{14,15},{17,16},{18,... | collective-permute-start | bytes 1572872 | tf_op jit(solution)/shard_map/ppermute | solution.py:304
  64.3 0.9 shard_map.89
  65.1 1.6 %collective-permute-start.21 = (bf16[256,512]{1,0:T(8,128)(2,1)S(1)}, bf16[256,512]{1,0:T(8,128)(2,1)S(1)}, u32[]{:S(2)}, u32[]{:S(2)}) collective-permute-start(bf16[256,512]{1,0:T(8,128)(2,1)S(1)} %get-tuple-element.78), channel_id=1, source_target_pairs={{0,16},{4,20},{8,24},{12,28},{16,0},{20,4},{24,8},{28,12},{1,17},{... | collective-permute-start | bytes 786440 | tf_op jit(solution)/shard_map/ppermute | solution.py:298
  66.7 1.5 %collective-permute-start.18 = (bf16[256,512]{1,0:T(8,128)(2,1)S(1)}, bf16[256,512]{1,0:T(8,128)(2,1)S(1)}, u32[]{:S(2)}, u32[]{:S(2)}) collective-permute-start(bf16[256,512]{1,0:T(8,128)(2,1)S(1)} %get-tuple-element.62), channel_id=1, source_target_pairs={{0,8},{4,12},{8,0},{12,4},{16,24},{20,28},{24,16},{28,20},{1,9},{5... | collective-permute-start | bytes 786440 | tf_op jit(solution)/shard_map/ppermute | solution.py:298
  68.2 4.1 %shard_map.90 = (bf16[512,512]{1,0:T(8,128)(2,1)S(1)}, f32[128,512]{1,0:T(8,128)S(1)}, f32[128,512]{1,0:T(8,128)S(1)}) custom-call(s32[8]{0:T(128)S(1)} %stack.32.place, bf16[512,512]{1,0:T(8,128)(2,1)S(1)} %copy-done, bf16[2,128,512]{2,1,0:T(8,128)(2,1)S(1)} %get-tuple-element.44.kv, f32[512,128]{1,0:T(8,128)S(1)} %get-tuple-element.45.lse, ...), custom_call_target="tpu_custom_call" | custom-call | flops 5368709 | bytes 32768 | tf_op jit(solution)/shard_map/pallas_call | solution.py:25
  72.3 1.3 %collective-permute-start.13 = (bf16[1,256,512]{2,1,0:T(8,128)(2,1)S(1)}, bf16[1,256,512]{2,1,0:T(8,128)(2,1)S(1)}, u32[]{:S(2)}, u32[]{:S(2)}) collective-permute-start(bf16[1,256,512]{2,1,0:T(8,128)(2,1)S(1)} %collective-permute-done.12.refs_0_), channel_id=1, source_target_pairs={{1,0},{2,3},{5,4},{6,7},{9,8},{10,11},{13,12},{14,15},{17,16},{18,... | collective-permute-start | bytes 786440 | tf_op jit(solution)/shard_map/ppermute | solution.py:304
  73.9 2.0 %collective-permute-done.17.refs_1_.refs_3_ = bf16[2,256,512]{2,1,0:T(8,128)(2,1)S(1)} collective-permute-done((bf16[2,256,512]{2,1,0:T(8,128)(2,1)S(1)}, bf16[2,256,512]{2,1,0:T(8,128)(2,1)S(1)}, u32[]{:S(2)}, u32[]{:S(2)}) %collective-permute-start.17) | collective-permute-done | bytes 524320 | tf_op jit(solution)/shard_map/ppermute | solution.py:304
  75.9 0.9 shard_map.96
  76.8 1.9 %collective-permute-start.22 = (bf16[512,512]{1,0:T(8,128)(2,1)S(1)}, bf16[512,512]{1,0:T(8,128)(2,1)S(1)}, u32[]{:S(2)}, u32[]{:S(2)}) collective-permute-start(bf16[512,512]{1,0:T(8,128)(2,1)S(1)} %shard_map.96), channel_id=1, source_target_pairs={{0,8},{4,12},{8,0},{12,4},{16,24},{20,28},{24,16},{28,20},{1,9},{5... | collective-permute-start | bytes 1572872 | tf_op jit(solution)/shard_map/ppermute | solution.py:298
  79.5 1.6 %collective-permute-start.23 = (bf16[512,512]{1,0:T(8,128)(2,1)S(1)}, bf16[512,512]{1,0:T(8,128)(2,1)S(1)}, u32[]{:S(2)}, u32[]{:S(2)}) collective-permute-start(bf16[512,512]{1,0:T(8,128)(2,1)S(1)} %shard_map.91), channel_id=1, source_target_pairs={{0,16},{4,20},{8,24},{12,28},{16,0},{20,4},{24,8},{28,12},{1,17},{... | collective-permute-start | bytes 1572872 | tf_op jit(solution)/shard_map/ppermute | solution.py:298
  81.1 1.1 %shard_map.92.refs_3_ = f32[256,512]{1,0:T(8,128)S(1)} custom-call(s32[8]{0:T(128)S(1)} %stack.32.place, bf16[1,256,512]{2,1,0:T(8,128)(2,1)S(1)} %collective-permute-done.10.refs_0_, bf16[1,256,512]{2,1,0:T(8,128)(2,1)S(1)} %collective-permute-done.16.refs_1_, bf16[2,256,512]{2,1,0:T(8,128)(2,1)S(1)} %collective-permute-done.11.refs_0_.refs_2_, ...), custom_call_target="tpu_custom_call" | custom-call | flops 5368709 | bytes 36700 | tf_op jit(solution)/shard_map/pallas_call | solution.py:25
  82.2 3.6 %collective-permute-done.13.refs_1_ = bf16[1,256,512]{2,1,0:T(8,128)(2,1)S(1)} collective-permute-done((bf16[1,256,512]{2,1,0:T(8,128)(2,1)S(1)}, bf16[1,256,512]{2,1,0:T(8,128)(2,1)S(1)}, u32[]{:S(2)}, u32[]{:S(2)}) %collective-permute-start.13) | collective-permute-done | bytes 262176 | tf_op jit(solution)/shard_map/ppermute | solution.py:304
  86.7 1.3 %collective-permute-done.19.grad_other = bf16[1,128,512]{2,1,0:T(8,128)(2,1)S(1)} collective-permute-done((bf16[1,128,512]{2,1,0:T(8,128)(2,1)S(1)}, bf16[1,128,512]{2,1,0:T(8,128)(2,1)S(1)}, u32[]{:S(2)}, u32[]{:S(2)}) %collective-permute-start.19) | collective-permute-done | bytes 131104 | tf_op jit(solution)/shard_map/ppermute | solution.py:298
  88.1 3.1 %shard_map.94 = (bf16[512,512]{1,0:T(8,128)(2,1)}, f32[128,512]{1,0:T(8,128)S(1)}, bf16[128,512]{1,0:T(8,128)(2,1)S(1)}) custom-call(s32[8]{0:T(128)S(1)} %stack.32.place, bf16[512,512]{1,0:T(8,128)(2,1)S(1)} %copy-done, bf16[2,128,512]{2,1,0:T(8,128)(2,1)S(1)} %get-tuple-element.44.kv, f32[512,128]{1,0:T(8,128)S(1)} %get-tuple-element.45.lse, ...), custom_call_target="tpu_custom_call" | custom-call | flops 5368709 | bytes 34079 | tf_op jit(solution)/shard_map/pallas_call | solution.py:25
  92.1 4.7 %collective-permute-done.20.other = bf16[128,512]{1,0:T(8,128)(2,1)S(1)} collective-permute-done((bf16[128,512]{1,0:T(8,128)(2,1)S(1)}, bf16[128,512]{1,0:T(8,128)(2,1)S(1)}, u32[]{:S(2)}, u32[]{:S(2)}) %collective-permute-start.20) | collective-permute-done | bytes 131104 | tf_op jit(solution)/shard_map/ppermute | solution.py:298
  96.8 1.0 %shard_map.97 = (bf16[64,512]{1,0:T(8,128)(2,1)}, bf16[64,512]{1,0:T(8,128)(2,1)}, bf16[512,512]{1,0:T(8,128)(2,1)}) custom-call(f32[128,512]{1,0:T(8,128)S(1)} %get-tuple-element.74.keep, bf16[128,512]{1,0:T(8,128)(2,1)S(1)} %collective-permute-done.20.other, f32[512,512]{1,0:T(8,128)S(1)} %shard_map.95.partial, ...), custom_call_target="tpu_custom_call" | custom-call | flops 5368709 | bytes 31457 | tf_op jit(solution)/shard_map/pallas_call | solution.py:25
  (41 shorter events, 9.4 us)
Async XLA Ops:
  0.6 0.8 copy-start.3
  1.5 1.2 %copy-start.2 = (bf16[128,4096]{1,0:T(8,128)(2,1)S(1)}, bf16[128,4096]{1,0:T(8,128)(2,1)}, u32[]{:S(2)}) copy-start(bf16[128,4096]{1,0:T(8,128)(2,1)} %grad.1) | copy-start | bytes 3145732
  2.7 0.8 copy-start.4
  3.5 4.5 %copy-start.1 = (bf16[512,512]{1,0:T(8,128)(2,1)S(1)}, bf16[512,512]{1,0:T(8,128)(2,1)}, u32[]{:S(2)}) copy-start(bf16[512,512]{1,0:T(8,128)(2,1)} %refs_2_.1) | copy-start | bytes 1572868
  3.5 21.4 %copy-start = (bf16[512,512]{1,0:T(8,128)(2,1)S(1)}, bf16[512,512]{1,0:T(8,128)(2,1)}, u32[]{:S(2)}) copy-start(bf16[512,512]{1,0:T(8,128)(2,1)} %queries.4) | copy-start | bytes 1572868
  4.2 5.4 %collective-permute-start.1 = (bf16[4,128,512]{2,1,0:T(8,128)(2,1)S(1)}, bf16[4,128,512]{2,1,0:T(8,128)(2,1)S(1)}, u32[]{:S(2)}, u32[]{:S(2)}) collective-permute-start(bf16[4,128,512]{2,1,0:T(8,128)(2,1)S(1)} %get-tuple-element.46), channel_id=1, source_target_pairs={{0,4},{4,0},{8,12},{12,8},{16,20},{20,16},{24,28},{28,24},{1,5},{5... | collective-permute-start | bytes 1572872 | tf_op jit(solution)/shard_map/ppermute | solution.py:298
  4.7 18.2 %collective-permute-start = (bf16[640,512]{1,0:T(8,128)(2,1)S(1)}, bf16[640,512]{1,0:T(8,128)(2,1)S(1)}, u32[]{:S(2)}, u32[]{:S(2)}) collective-permute-start(bf16[640,512]{1,0:T(8,128)(2,1)S(1)} %get-tuple-element.43.refs_0_), channel_id=1, source_target_pairs={{0,1},{1,0},{2,3},{3,2},{4,5},{5,4},{6,7},{7,6},{8,9},{9,8},{10,11... | collective-permute-start | bytes 1966088 | tf_op jit(solution)/shard_map/ppermute | solution.py:298
  7.4 8.2 %collective-permute-start.3 = (bf16[4,128,512]{2,1,0:T(8,128)(2,1)S(1)}, bf16[4,128,512]{2,1,0:T(8,128)(2,1)S(1)}, u32[]{:S(2)}, u32[]{:S(2)}) collective-permute-start(bf16[4,128,512]{2,1,0:T(8,128)(2,1)S(1)} %get-tuple-element.49), channel_id=1, source_target_pairs={{1,2},{2,1},{5,6},{6,5},{9,10},{10,9},{13,14},{14,13},{17,18},{18,... | collective-permute-start | bytes 1572872 | tf_op jit(solution)/shard_map/ppermute | solution.py:301
  8.1 21.1 %collective-permute-start.8 = (bf16[512,512]{1,0:T(8,128)(2,1)S(1)}, bf16[512,512]{1,0:T(8,128)(2,1)S(1)}, u32[]{:S(2)}, u32[]{:S(2)}) collective-permute-start(bf16[512,512]{1,0:T(8,128)(2,1)S(1)} %copy-done.1), channel_id=1, source_target_pairs={{0,8},{4,12},{8,0},{12,4},{16,24},{20,28},{24,16},{28,20},{1,9},{5... | collective-permute-start | bytes 1572872 | tf_op jit(solution)/shard_map/ppermute | solution.py:298
  9.6 24.6 %collective-permute-start.2 = (bf16[4,128,512]{2,1,0:T(8,128)(2,1)S(1)}, bf16[4,128,512]{2,1,0:T(8,128)(2,1)S(1)}, u32[]{:S(2)}, u32[]{:S(2)}) collective-permute-start(bf16[4,128,512]{2,1,0:T(8,128)(2,1)S(1)} %collective-permute-done.1.refs_1_), channel_id=1, source_target_pairs={{0,1},{1,0},{2,3},{3,2},{4,5},{5,4},{6,7},{7,6},{8,9},{9,8},{10,11... | collective-permute-start | bytes 1572872 | tf_op jit(solution)/shard_map/ppermute | solution.py:298
  14.0 20.3 %collective-permute-start.9 = (bf16[512,512]{1,0:T(8,128)(2,1)S(1)}, bf16[512,512]{1,0:T(8,128)(2,1)S(1)}, u32[]{:S(2)}, u32[]{:S(2)}) collective-permute-start(bf16[512,512]{1,0:T(8,128)(2,1)S(1)} %copy-done.1), channel_id=1, source_target_pairs={{0,16},{4,20},{8,24},{12,28},{16,0},{20,4},{24,8},{28,12},{1,17},{... | collective-permute-start | bytes 1572872 | tf_op jit(solution)/shard_map/ppermute | solution.py:298
  23.0 11.3 %collective-permute-start.7 = (bf16[4,128,512]{2,1,0:T(8,128)(2,1)S(1)}, bf16[4,128,512]{2,1,0:T(8,128)(2,1)S(1)}, u32[]{:S(2)}, u32[]{:S(2)}) collective-permute-start(bf16[4,128,512]{2,1,0:T(8,128)(2,1)S(1)} %collective-permute-done.1.refs_1_), channel_id=1, source_target_pairs={{1,2},{2,1},{5,6},{6,5},{9,10},{10,9},{13,14},{14,13},{17,18},{18,... | collective-permute-start | bytes 1572872 | tf_op jit(solution)/shard_map/ppermute | solution.py:301
  23.6 21.8 %collective-permute-start.4 = (bf16[4,128,512]{2,1,0:T(8,128)(2,1)S(1)}, bf16[4,128,512]{2,1,0:T(8,128)(2,1)S(1)}, u32[]{:S(2)}, u32[]{:S(2)}) collective-permute-start(bf16[4,128,512]{2,1,0:T(8,128)(2,1)S(1)} %collective-permute-done.3.refs_4_), channel_id=1, source_target_pairs={{1,0},{2,3},{5,4},{6,7},{9,8},{10,11},{13,12},{14,15},{17,16},{18,... | collective-permute-start | bytes 1572872 | tf_op jit(solution)/shard_map/ppermute | solution.py:304
  29.2 16.3 %collective-permute-start.5 = (bf16[512,512]{1,0:T(8,128)(2,1)S(1)}, bf16[512,512]{1,0:T(8,128)(2,1)S(1)}, u32[]{:S(2)}, u32[]{:S(2)}) collective-permute-start(bf16[512,512]{1,0:T(8,128)(2,1)S(1)} %copy-done.1), channel_id=1, source_target_pairs={{0,24},{4,28},{8,16},{12,20},{16,8},{20,12},{24,0},{28,4},{1,25},{... | collective-permute-start | bytes 1572872 | tf_op jit(solution)/shard_map/ppermute | solution.py:298
  34.2 11.2 %collective-permute-start.6 = (bf16[512,512]{1,0:T(8,128)(2,1)S(1)}, bf16[512,512]{1,0:T(8,128)(2,1)S(1)}, u32[]{:S(2)}, u32[]{:S(2)}) collective-permute-start(bf16[512,512]{1,0:T(8,128)(2,1)S(1)} %get-tuple-element.51.att_own), channel_id=1, source_target_pairs={{0,4},{4,0},{8,12},{12,8},{16,20},{20,16},{24,28},{28,24},{1,5},{5... | collective-permute-start | bytes 1572872 | tf_op jit(solution)/shard_map/ppermute | solution.py:298
  34.3 11.1 %collective-permute-start.10 = (bf16[1,256,512]{2,1,0:T(8,128)(2,1)S(1)}, bf16[1,256,512]{2,1,0:T(8,128)(2,1)S(1)}, u32[]{:S(2)}, u32[]{:S(2)}) collective-permute-start(bf16[1,256,512]{2,1,0:T(8,128)(2,1)S(1)} %get-tuple-element.54), channel_id=1, source_target_pairs={{1,2},{2,1},{5,6},{6,5},{9,10},{10,9},{13,14},{14,13},{17,18},{18,... | collective-permute-start | bytes 786440 | tf_op jit(solution)/shard_map/ppermute | solution.py:301
  35.0 22.5 %collective-permute-start.14 = (bf16[4,128,512]{2,1,0:T(8,128)(2,1)S(1)}, bf16[4,128,512]{2,1,0:T(8,128)(2,1)S(1)}, u32[]{:S(2)}, u32[]{:S(2)}) collective-permute-start(bf16[4,128,512]{2,1,0:T(8,128)(2,1)S(1)} %collective-permute-done.7.refs_5_), channel_id=1, source_target_pairs={{1,0},{2,3},{5,4},{6,7},{9,8},{10,11},{13,12},{14,15},{17,16},{18,... | collective-permute-start | bytes 1572872 | tf_op jit(solution)/shard_map/ppermute | solution.py:304
  45.4 16.7 %collective-permute-start.11 = (bf16[2,256,512]{2,1,0:T(8,128)(2,1)S(1)}, bf16[2,256,512]{2,1,0:T(8,128)(2,1)S(1)}, u32[]{:S(2)}, u32[]{:S(2)}) collective-permute-start(bf16[2,256,512]{2,1,0:T(8,128)(2,1)S(1)} %get-tuple-element.55), channel_id=1, source_target_pairs={{1,2},{2,1},{5,6},{6,5},{9,10},{10,9},{13,14},{14,13},{17,18},{18,... | collective-permute-start | bytes 1572872 | tf_op jit(solution)/shard_map/ppermute | solution.py:301
  46.1 18.1 %collective-permute-start.16 = (bf16[1,256,512]{2,1,0:T(8,128)(2,1)S(1)}, bf16[1,256,512]{2,1,0:T(8,128)(2,1)S(1)}, u32[]{:S(2)}, u32[]{:S(2)}) collective-permute-start(bf16[1,256,512]{2,1,0:T(8,128)(2,1)S(1)} %collective-permute-done.10.refs_0_), channel_id=1, source_target_pairs={{1,0},{2,3},{5,4},{6,7},{9,8},{10,11},{13,12},{14,15},{17,16},{18,... | collective-permute-start | bytes 786440 | tf_op jit(solution)/shard_map/ppermute | solution.py:304
  62.2 13.7 %collective-permute-start.17 = (bf16[2,256,512]{2,1,0:T(8,128)(2,1)S(1)}, bf16[2,256,512]{2,1,0:T(8,128)(2,1)S(1)}, u32[]{:S(2)}, u32[]{:S(2)}) collective-permute-start(bf16[2,256,512]{2,1,0:T(8,128)(2,1)S(1)} %collective-permute-done.11.refs_0_.refs_2_), channel_id=1, source_target_pairs={{1,0},{2,3},{5,4},{6,7},{9,8},{10,11},{13,12},{14,15},{17,16},{18,... | collective-permute-start | bytes 1572872 | tf_op jit(solution)/shard_map/ppermute | solution.py:304
  63.5 4.7 %collective-permute-start.15 = (bf16[3,128,512]{2,1,0:T(8,128)(2,1)S(1)}, bf16[3,128,512]{2,1,0:T(8,128)(2,1)S(1)}, u32[]{:S(2)}, u32[]{:S(2)}) collective-permute-start(bf16[3,128,512]{2,1,0:T(8,128)(2,1)S(1)} %get-tuple-element.59), channel_id=1, source_target_pairs={{0,4},{4,0},{8,12},{12,8},{16,20},{20,16},{24,28},{28,24},{1,5},{5... | collective-permute-start | bytes 1179656 | tf_op jit(solution)/shard_map/ppermute | solution.py:298
  63.6 8.7 %collective-permute-start.12 = (bf16[1,256,512]{2,1,0:T(8,128)(2,1)S(1)}, bf16[1,256,512]{2,1,0:T(8,128)(2,1)S(1)}, u32[]{:S(2)}, u32[]{:S(2)}) collective-permute-start(bf16[1,256,512]{2,1,0:T(8,128)(2,1)S(1)} %get-tuple-element.56), channel_id=1, source_target_pairs={{1,2},{2,1},{5,6},{6,5},{9,10},{10,9},{13,14},{14,13},{17,18},{18,... | collective-permute-start | bytes 786440 | tf_op jit(solution)/shard_map/ppermute | solution.py:301
  65.1 8.8 %collective-permute-start.21 = (bf16[256,512]{1,0:T(8,128)(2,1)S(1)}, bf16[256,512]{1,0:T(8,128)(2,1)S(1)}, u32[]{:S(2)}, u32[]{:S(2)}) collective-permute-start(bf16[256,512]{1,0:T(8,128)(2,1)S(1)} %get-tuple-element.78), channel_id=1, source_target_pairs={{0,16},{4,20},{8,24},{12,28},{16,0},{20,4},{24,8},{28,12},{1,17},{... | collective-permute-start | bytes 786440 | tf_op jit(solution)/shard_map/ppermute | solution.py:298
  66.7 12.0 %collective-permute-start.18 = (bf16[256,512]{1,0:T(8,128)(2,1)S(1)}, bf16[256,512]{1,0:T(8,128)(2,1)S(1)}, u32[]{:S(2)}, u32[]{:S(2)}) collective-permute-start(bf16[256,512]{1,0:T(8,128)(2,1)S(1)} %get-tuple-element.62), channel_id=1, source_target_pairs={{0,8},{4,12},{8,0},{12,4},{16,24},{20,28},{24,16},{28,20},{1,9},{5... | collective-permute-start | bytes 786440 | tf_op jit(solution)/shard_map/ppermute | solution.py:298
  72.3 13.5 %collective-permute-start.13 = (bf16[1,256,512]{2,1,0:T(8,128)(2,1)S(1)}, bf16[1,256,512]{2,1,0:T(8,128)(2,1)S(1)}, u32[]{:S(2)}, u32[]{:S(2)}) collective-permute-start(bf16[1,256,512]{2,1,0:T(8,128)(2,1)S(1)} %collective-permute-done.12.refs_0_), channel_id=1, source_target_pairs={{1,0},{2,3},{5,4},{6,7},{9,8},{10,11},{13,12},{14,15},{17,16},{18,... | collective-permute-start | bytes 786440 | tf_op jit(solution)/shard_map/ppermute | solution.py:304
  76.8 20.0 %collective-permute-start.22 = (bf16[512,512]{1,0:T(8,128)(2,1)S(1)}, bf16[512,512]{1,0:T(8,128)(2,1)S(1)}, u32[]{:S(2)}, u32[]{:S(2)}) collective-permute-start(bf16[512,512]{1,0:T(8,128)(2,1)S(1)} %shard_map.96), channel_id=1, source_target_pairs={{0,8},{4,12},{8,0},{12,4},{16,24},{20,28},{24,16},{28,20},{1,9},{5... | collective-permute-start | bytes 1572872 | tf_op jit(solution)/shard_map/ppermute | solution.py:298
  79.5 17.2 %collective-permute-start.23 = (bf16[512,512]{1,0:T(8,128)(2,1)S(1)}, bf16[512,512]{1,0:T(8,128)(2,1)S(1)}, u32[]{:S(2)}, u32[]{:S(2)}) collective-permute-start(bf16[512,512]{1,0:T(8,128)(2,1)S(1)} %shard_map.91), channel_id=1, source_target_pairs={{0,16},{4,20},{8,24},{12,28},{16,0},{20,4},{24,8},{28,12},{1,17},{... | collective-permute-start | bytes 1572872 | tf_op jit(solution)/shard_map/ppermute | solution.py:298
  86.7 1.4 %collective-permute-start.19 = (bf16[1,128,512]{2,1,0:T(8,128)(2,1)S(1)}, bf16[1,128,512]{2,1,0:T(8,128)(2,1)S(1)}, u32[]{:S(2)}, u32[]{:S(2)}) collective-permute-start(bf16[1,128,512]{2,1,0:T(8,128)(2,1)S(1)} %get-tuple-element.70), channel_id=1, source_target_pairs={{0,4},{4,0},{8,12},{12,8},{16,20},{20,16},{24,28},{28,24},{1,5},{5... | collective-permute-start | bytes 393224 | tf_op jit(solution)/shard_map/ppermute | solution.py:298
  91.2 5.5 %collective-permute-start.20 = (bf16[128,512]{1,0:T(8,128)(2,1)S(1)}, bf16[128,512]{1,0:T(8,128)(2,1)S(1)}, u32[]{:S(2)}, u32[]{:S(2)}) collective-permute-start(bf16[128,512]{1,0:T(8,128)(2,1)S(1)} %get-tuple-element.75), channel_id=1, source_target_pairs={{0,1},{1,0},{2,3},{3,2},{4,5},{5,4},{6,7},{7,6},{8,9},{9,8},{10,11... | collective-permute-start | bytes 393224 | tf_op jit(solution)/shard_map/ppermute | solution.py:298

commit v2 on v1

--- a/solution.py
+++ b/solution.py
@@ -184,21 +184,23 @@
             c += 1
 
 
-def pieces(place, refs, c):
+def pieces(refs, c):
     rows = refs[1].shape[1]
-    both = [
+    return [
         jnp.concatenate([chunk(refs[i], c, rows), refs[i + 1][c]], axis=0)
         for i in range(0, len(refs), 2)
     ]
-    if len(both) != 4:
-        return both
+
+
+def middle_piece(place, refs, c):
     inner = (place[3] == 1) | (place[3] == 2)
-    return both[:2] + [jnp.where(inner, both[2], both[3])]
-
-
-def late_piece(place, refs, i):
+    found = pieces(refs, c)
+    return jnp.where(inner, found[0], found[1])
+
+
+def late_piece(place, refs, i, j):
     inner = (place[3] == 1) | (place[3] == 2)
-    return jnp.where(inner, refs[0][i], refs[1][i])
+    return jnp.where(inner, refs[0][i], refs[1][j])
 
 
 def attended_rows(att_own, att_other, j, rows):
@@ -211,7 +213,7 @@
     rows = own.shape[1]
     totals = None
     for c, weight in enumerate(weights):
-        products = [dot(value, weight[...], 1, 0) for value in pieces(place, blocks, c)]
+        products = [dot(value, weight[...], 1, 0) for value in pieces(blocks, c)]
         totals = [a + b for a, b in zip(totals, products)] if totals else products
     for i, total in enumerate(totals):
         own[i] = total[:rows]
@@ -223,40 +225,50 @@
     rows = blocks[1].shape[1]
     for c, out in enumerate(outs):
         total = None
-        for i, value in enumerate(pieces(place, blocks, c)):
+        for i, value in enumerate(pieces(blocks, c)):
             product = dot(value, attended_rows(att_own, att_other, place[SLOTS + i], rows), 0, 0)
             total = product if total is None else total + product
         out[...] = total.astype(BF16)
 
 
-def late_kernel(sizes, steps, first, place, *refs):
-    late, refs = refs[: 2 * len(steps)], refs[2 * len(steps) :]
-    count = sum(sizes[side] for side in steps)
-    weights, refs = refs[:count], refs[count:]
-    total = None if first else refs[0][...]
-    c = 0
-    for n, side in enumerate(steps):
-        for i in range(sizes[side]):
-            value = late_piece(place, late[2 * n : 2 * n + 2], i)
-            product = dot(value, weights[c][...], 1, 0)
-            total = product if total is None else total + product
-            c += 1
-    if first:
-        refs[0][...] = total
-    else:
-        own, give = refs[1:]
-        rows = own.shape[1]
-        own[0] = total[:rows]
-        give[0] = total[rows:].astype(BF16)
-
-
-def term_kernel(i, late, spans, place, att_own, att_other, partial, *refs):
-    received, outs = refs[late : late + len(spans)], refs[late + len(spans) :]
+def middle_kernel(count, place, *refs):
+    middle, late, weights = refs[:4], refs[4:6], refs[6 : 6 + count]
+    total, own, give = refs[6 + count :]
+    rows = own.shape[1]
+    value = None
+    for c, weight in enumerate(weights):
+        product = dot(middle_piece(place, middle, c), weight[...], 1, 0)
+        value = product if value is None else value + product
+    own[0] = value[:rows]
+    give[0] = value[rows:].astype(BF16)
+    value = None
+    for i in range(late[0].shape[0]):
+        product = dot(late_piece(place, late, i, i), weights[i][...], 1, 0)
+        value = product if value is None else value + product
+    total[...] = value
+
+
+def late_kernel(chunks, place, *refs):
+    count = len(chunks)
+    late, weights, (early, own, give) = refs[: 2 * count], refs[2 * count : 3 * count], refs[3 * count :]
+    total = early[...]
+    for c, (i, j) in enumerate(chunks):
+        total += dot(late_piece(place, late[2 * c : 2 * c + 2], i, j), weights[c][...], 1, 0)
+    rows = own.shape[1]
+    own[0] = total[:rows]
+    give[0] = total[rows:].astype(BF16)
+
+
+def term_kernel(c, i, j, late, spans, place, att_own, att_other, partial, *refs):
+    blocks, received = refs[:late], refs[late : late + len(spans)]
+    outs = refs[late + len(spans) :]
     total = partial[...].astype(F32)
     if late:
-        value = late_piece(place, refs[:late], i)
-        rhs = attended_rows(att_own, att_other, place[place.shape[0] - 1], value.shape[0] // 2)
-        total = total + dot(value, rhs, 0, 0)
+        values = [middle_piece(place, blocks[:4], c), late_piece(place, blocks[4:], i, j)]
+        rows = values[0].shape[0] // 2
+        slots = [place[place.shape[0] - 2], place[place.shape[0] - 1]]
+        for slot, value in zip(slots, values):
+            total = total + dot(value, attended_rows(att_own, att_other, slot, rows), 0, 0)
     middle = total.shape[0] // 2
     sides = [total[:middle], total[middle:]]
     for ref, span in zip(received, spans):
@@ -285,7 +297,7 @@
     index, part = lax.axis_index("dp"), lax.axis_index("tensor")
     if tensor == 4:
         inner = (part == 1) | (part == 2)
-        early = 3
+        early = 2
         slots = [0, 1, jnp.where(inner, 3, 2), jnp.where(inner, 2, 3)]
     else:
         early = tensor
@@ -345,7 +357,7 @@
         )
         in_own = outward(middle_own)
         in_taken = outward(tie(middle_taken, near[1]))
-        blocks += [middle_own, middle_taken, in_own, in_taken]
+        middle = [middle_own, middle_taken, in_own, in_taken]
         att_other = swap(attended, "dp", 1)
         relay = call(
             merge_kernel,
@@ -387,14 +399,6 @@
         scalars=1,
     )
     grad_other = swap(grad_give, "dp", 1)
-    if tensor == 4:
-        after = [[], [in_taken, partials[0]], []]
-        for side, size in enumerate(sizes):
-            arrived = outward(tie(second[side], *after[side]))
-            late += [(i, [second[side], arrived]) for i in range(size)]
-    else:
-        late = [(0, [])] * chips
-
     def backward(first, final, base, own, other, carry):
         state = [shape((HEAD_DIM, length), F32)] * 2
         ends = [shape((2 * half, length), F32), shape((2 * half, length), BF16)]
@@ -411,6 +415,17 @@
             scalars=1,
         )
 
+    done = backward(True, early == tensor, 0, grad_own, grad_other, [])
+    if tensor == 4:
+        after = [[], [in_taken, partials[0], done[1]], []]
+        for side, size in enumerate(sizes):
+            arrived = outward(tie(second[side], *after[side]))
+            late += [(i, i, [second[side], arrived]) for i in range(size)]
+    else:
+        late = [(0, 0, [])] * chips
+        middle = []
+
+
     received = {s: [] for s in order}
 
     def term(c, *others, kind=BF16):
@@ -419,10 +434,11 @@
         spans, extra = zip(*received[s]) if received[s] and s else ((), ())
         shapes = [(depth, width)] if low == high else [(depth // 2, width)] * 2
         found = call(
-            functools.partial(term_kernel, late[c][0], len(late[c][1]), spans),
+            functools.partial(term_kernel, c, *late[c][:2], len(middle + late[c][2]), spans),
             [shape(size, kind) for size in shapes],
             [tie(place, *others), attended, att_other, partials[c]]
-            + late[c][1]
+            + middle
+            + late[c][2]
             + list(extra),
             300 * flops,
             scalars=1,
@@ -435,35 +451,35 @@
         return found[0]
 
     terms = [term(0)]
-    done = backward(
-        True,
-        early == tensor,
-        0,
-        grad_own,
-        tie(grad_other, terms[0]),
-        [],
-    )
-    terms += [term(c, done[1]) for c in range(1, chips - 1)]
-
     if tensor == 4:
-        pairs = [pair for i, pair in late if i == 0]
-        steps = list(range(len(sizes)))
-        (total,) = call(
-            functools.partial(late_kernel, sizes, steps[:-1], True),
-            [shape((2 * rows, width), F32)],
-            [tie(place, terms[-1])] + sum(pairs[:-1], []) + weights[: -sizes[-1]],
+        total, grad_own, grad_give = call(
+            functools.partial(middle_kernel, chips),
+            [
+                shape((2 * rows, width), F32),
+                shape((1, rows, width), F32),
+                shape((1, rows, width), BF16),
+            ],
+            [tie(place, terms[0])] + middle + late[0][2] + weights,
             flops,
             scalars=1,
         )
-        grad_own, grad_give = call(
-            functools.partial(late_kernel, sizes, steps[-1:], False),
+        grad_other = swap(grad_give, "dp", 1)
+        done = backward(False, False, early, grad_own, grad_other, list(done))
+    terms += [term(c, done[1]) for c in range(1, chips - 1)]
+
+    if tensor == 4:
+        (grad_own, grad_give) = call(
+            functools.partial(late_kernel, [item[:2] for item in late[sizes[0] :]]),
             [shape((1, rows, width), F32), shape((1, rows, width), BF16)],
-            [place] + pairs[-1] + weights[-sizes[-1] :] + [total],
+            [tie(place, done[1])]
+            + sum([item[2] for item in late[sizes[0] :]], [])
+            + weights[sizes[0] :]
+            + [total],
             flops,
             scalars=1,
         )
         grad_other = swap(grad_give, "dp", 1)
-        done = backward(False, True, early, grad_own, grad_other, list(done))
+        done = backward(False, True, early + 1, grad_own, grad_other, list(done))
     grad_q, keep, send = done
     grad_k, grad_v, grad_weight = call(
         finish_kernel,

time: 98.2 us -> 97.6 us (level)
  waiting for transfers between devices: 40.7 us -> 39.7 us
    ppermute x5, waiting for transfers between devices: 24.7 us -> 18.3 us  [outward(): return lax.ppermute(value, 'tensor', [(1, 0), (2, 3)])]
    ppermute x14 -> x15, waiting for transfers between devices: 15.9 us -> 21.4 us  [swap(): lax.ppermute(value, axis, [(i, i ^ mask) for i in range(lax.axis_size(axi...]
    pallas_call x14 -> x15, Pallas kernels: 23.2 us -> 23.8 us  [call(): pl.pallas_call(kernel, out_shape=tuple(outs), in_specs=[SMEM] * scalars +...]
    ppermute x14 -> x15, starting transfers between devices: 20.2 us -> 20 us  [swap(): lax.ppermute(value, axis, [(i, i ^ mask) for i in range(lax.axis_size(axi...]
  transfers between devices with their start and end apart: 24 -> 25, of which waited for: 9 -> 9; matrix products, arithmetic and copies ran while one was open for 0% -> 0% of each run, Pallas kernels for 22% -> 23%
where the time goes in v2:
time: 97.6 us; the launch traced here: 97.2 us
  waiting for transfers between devices  39.7 us (41%)
  starting transfers between devices  29.9 us (31%)
  Pallas kernels  23.8 us (24%)
  local copies, waits for them, and re-layouts  2.87 us (3%)
    pallas_call x15, Pallas kernels, call(): pl.pallas_call(kernel, out_shape=tuple(outs), in_specs=[SMEM] * scalars +...  23.8 us
    ppermute x15, waiting for transfers between devices, swap(): lax.ppermute(value, axis, [(i, i ^ mask) for i in range(lax.axis_size(axi...  21.4 us
    ppermute x15, starting transfers between devices, swap(): lax.ppermute(value, axis, [(i, i ^ mask) for i in range(lax.axis_size(axi...  20 us
    ppermute x5, waiting for transfers between devices, outward(): return lax.ppermute(value, 'tensor', [(1, 0), (2, 3)])  18.3 us
    ppermute x5, starting transfers between devices, outward(): return lax.ppermute(value, 'tensor', [(1, 0), (2, 3)])  6.46 us
    ppermute x5, starting transfers between devices, across(): return lax.ppermute(value, 'tensor', [(1, 2), (2, 1)])  3.4 us
    unnamed x10, local copies, waits for them, and re-layouts  2.78 us
  transfers between devices with their start and end apart: 25, of which 9 were waited for; matrix products, arithmetic and copies ran while one was open for 0% of the time, Pallas kernels for 23%

profile of v2, /device:TPU:0, one launch (start us, length us, event | category | flops | bytes accessed | tf_op | source)
XLA Modules:
  0.0 97.2 jit_solution(15133784439917937123)
XLA Ops:
  1.5 1.2 %copy-done.2 = bf16[128,4096]{1,0:T(8,128)(2,1)S(1)} copy-done((bf16[128,4096]{1,0:T(8,128)(2,1)S(1)}, bf16[128,4096]{1,0:T(8,128)(2,1)}, u32[]{:S(2)}) %copy-start.2) | copy-done | bytes 1048600
  4.7 2.6 %collective-permute-start = (bf16[640,512]{1,0:T(8,128)(2,1)S(1)}, bf16[640,512]{1,0:T(8,128)(2,1)S(1)}, u32[]{:S(2)}, u32[]{:S(2)}) collective-permute-start(bf16[640,512]{1,0:T(8,128)(2,1)S(1)} %get-tuple-element.48.refs_0_), channel_id=1, source_target_pairs={{0,1},{1,0},{2,3},{3,2},{4,5},{5,4},{6,7},{7,6},{8,9},{9,8},{10,11... | collective-permute-start | bytes 1966088 | tf_op jit(solution)/shard_map/ppermute | solution.py:310
  8.1 1.6 %collective-permute-start.5 = (bf16[512,512]{1,0:T(8,128)(2,1)S(1)}, bf16[512,512]{1,0:T(8,128)(2,1)S(1)}, u32[]{:S(2)}, u32[]{:S(2)}) collective-permute-start(bf16[512,512]{1,0:T(8,128)(2,1)S(1)} %copy-done.1), channel_id=1, source_target_pairs={{0,8},{4,12},{8,0},{12,4},{16,24},{20,28},{24,16},{28,20},{1,9},{5... | collective-permute-start | bytes 1572872 | tf_op jit(solution)/shard_map/ppermute | solution.py:310
  9.6 4.4 %collective-permute-start.3 = (bf16[4,128,512]{2,1,0:T(8,128)(2,1)S(1)}, bf16[4,128,512]{2,1,0:T(8,128)(2,1)S(1)}, u32[]{:S(2)}, u32[]{:S(2)}) collective-permute-start(bf16[4,128,512]{2,1,0:T(8,128)(2,1)S(1)} %collective-permute-done.2.refs_1_), channel_id=1, source_target_pairs={{0,1},{1,0},{2,3},{3,2},{4,5},{5,4},{6,7},{7,6},{8,9},{9,8},{10,11... | collective-permute-start | bytes 1572872 | tf_op jit(solution)/shard_map/ppermute | solution.py:310
  14.0 1.5 %collective-permute-start.6 = (bf16[512,512]{1,0:T(8,128)(2,1)S(1)}, bf16[512,512]{1,0:T(8,128)(2,1)S(1)}, u32[]{:S(2)}, u32[]{:S(2)}) collective-permute-start(bf16[512,512]{1,0:T(8,128)(2,1)S(1)} %copy-done.1), channel_id=1, source_target_pairs={{0,16},{4,20},{8,24},{12,28},{16,0},{20,4},{24,8},{28,12},{1,17},{... | collective-permute-start | bytes 1572872 | tf_op jit(solution)/shard_map/ppermute | solution.py:310
  15.5 7.4 %collective-permute-done.near.refs_2_.first = bf16[640,512]{1,0:T(8,128)(2,1)S(1)} collective-permute-done((bf16[640,512]{1,0:T(8,128)(2,1)S(1)}, bf16[640,512]{1,0:T(8,128)(2,1)S(1)}, u32[]{:S(2)}, u32[]{:S(2)}) %collective-permute-start) | collective-permute-done | bytes 655392 | tf_op jit(solution)/shard_map/ppermute | solution.py:310
  23.6 1.3 %collective-permute-start.9 = (bf16[4,128,512]{2,1,0:T(8,128)(2,1)S(1)}, bf16[4,128,512]{2,1,0:T(8,128)(2,1)S(1)}, u32[]{:S(2)}, u32[]{:S(2)}) collective-permute-start(bf16[4,128,512]{2,1,0:T(8,128)(2,1)S(1)} %collective-permute-done.7.refs_0_), channel_id=1, source_target_pairs={{1,0},{2,3},{5,4},{6,7},{9,8},{10,11},{13,12},{14,15},{17,16},{18,... | collective-permute-start | bytes 1572872 | tf_op jit(solution)/shard_map/ppermute | solution.py:316
  25.0 4.2 %shard_map.85 = (bf16[2,128,512]{2,1,0:T(8,128)(2,1)S(1)}, bf16[512,512]{1,0:T(8,128)(2,1)S(1)}, f32[512,128]{1,0:T(8,128)S(1)}) custom-call(s32[8]{0:T(128)S(1)} %stack.32.place, bf16[512,512]{1,0:T(8,128)(2,1)S(1)} %copy-done, bf16[64,512]{1,0:T(8,128)(2,1)S(1)} %bitcast.12, bf16[64,512]{1,0:T(8,128)(2,1)S(1)} %bitcast.14, ...), custom_call_target="tpu_custom_call" | custom-call | flops 5368709 | bytes 23593 | tf_op jit(solution)/shard_map/pallas_call | solution.py:25
  29.2 5.0 %collective-permute-done.3.refs_3_.second = bf16[4,128,512]{2,1,0:T(8,128)(2,1)S(1)} collective-permute-done((bf16[4,128,512]{2,1,0:T(8,128)(2,1)S(1)}, bf16[4,128,512]{2,1,0:T(8,128)(2,1)S(1)}, u32[]{:S(2)}, u32[]{:S(2)}) %collective-permute-start.3) | collective-permute-done | bytes 524320 | tf_op jit(solution)/shard_map/ppermute | solution.py:310
  34.2 2.8 %collective-permute-start.4 = (bf16[512,512]{1,0:T(8,128)(2,1)S(1)}, bf16[512,512]{1,0:T(8,128)(2,1)S(1)}, u32[]{:S(2)}, u32[]{:S(2)}) collective-permute-start(bf16[512,512]{1,0:T(8,128)(2,1)S(1)} %copy-done.1), channel_id=1, source_target_pairs={{0,24},{4,28},{8,16},{12,20},{16,8},{20,12},{24,0},{28,4},{1,25},{... | collective-permute-start | bytes 1572872 | tf_op jit(solution)/shard_map/ppermute | solution.py:310
  37.8 1.3 %collective-permute-start.10 = (bf16[4,128,512]{2,1,0:T(8,128)(2,1)S(1)}, bf16[4,128,512]{2,1,0:T(8,128)(2,1)S(1)}, u32[]{:S(2)}, u32[]{:S(2)}) collective-permute-start(bf16[4,128,512]{2,1,0:T(8,128)(2,1)S(1)} %collective-permute-done.8.refs_1_), channel_id=1, source_target_pairs={{1,0},{2,3},{5,4},{6,7},{9,8},{10,11},{13,12},{14,15},{17,16},{18,... | collective-permute-start | bytes 1572872 | tf_op jit(solution)/shard_map/ppermute | solution.py:316
  39.1 6.3 %collective-permute-done.9.refs_2_ = bf16[4,128,512]{2,1,0:T(8,128)(2,1)S(1)} collective-permute-done((bf16[4,128,512]{2,1,0:T(8,128)(2,1)S(1)}, bf16[4,128,512]{2,1,0:T(8,128)(2,1)S(1)}, u32[]{:S(2)}, u32[]{:S(2)}) %collective-permute-start.9) | collective-permute-done | bytes 524320 | tf_op jit(solution)/shard_map/ppermute | solution.py:316
  45.4 3.1 %collective-permute-done.4.refs_4_.refs_6_ = bf16[512,512]{1,0:T(8,128)(2,1)S(1)} collective-permute-done((bf16[512,512]{1,0:T(8,128)(2,1)S(1)}, bf16[512,512]{1,0:T(8,128)(2,1)S(1)}, u32[]{:S(2)}, u32[]{:S(2)}) %collective-permute-start.4) | collective-permute-done | bytes 524320 | tf_op jit(solution)/shard_map/ppermute | solution.py:310
  49.2 1.8 %shard_map.86 = (f32[2,128,512]{2,1,0:T(8,128)S(1)}, bf16[2,128,512]{2,1,0:T(8,128)(2,1)S(1)}) custom-call(s32[8]{0:T(128)S(1)} %stack.32.place, bf16[640,512]{1,0:T(8,128)(2,1)S(1)} %get-tuple-element.48.refs_0_, bf16[4,128,512]{2,1,0:T(8,128)(2,1)S(1)} %collective-permute-done.2.refs_1_, bf16[640,512]{1,0:T(8,128)(2,1)S(1)} %collective-permute-done.near.refs_2_.first, ...), custom_call_target="tpu_custom_call" | custom-call | flops 1610612736 | bytes 52429 | tf_op jit(solution)/shard_map/pallas_call | solution.py:25
  51.1 1.3 %collective-permute-start.12 = (bf16[1,256,512]{2,1,0:T(8,128)(2,1)S(1)}, bf16[1,256,512]{2,1,0:T(8,128)(2,1)S(1)}, u32[]{:S(2)}, u32[]{:S(2)}) collective-permute-start(bf16[1,256,512]{2,1,0:T(8,128)(2,1)S(1)} %collective-permute-done.11.refs_4_), channel_id=1, source_target_pairs={{1,0},{2,3},{5,4},{6,7},{9,8},{10,11},{13,12},{14,15},{17,16},{18,... | collective-permute-start | bytes 786440 | tf_op jit(solution)/shard_map/ppermute | solution.py:316
  52.4 1.8 %shard_map.87 = (bf16[512,512]{1,0:T(8,128)(2,1)S(1)}, bf16[512,512]{1,0:T(8,128)(2,1)S(1)}, bf16[512,512]{1,0:T(8,128)(2,1)S(1)}, bf16[512,512]{1,0:T(8,128)(2,1)S(1)}) custom-call(s32[8]{0:T(128)S(1)} %stack.32.place, bf16[512,512]{1,0:T(8,128)(2,1)S(1)} %get-tuple-element.51.att_own, bf16[512,512]{1,0:T(8,128)(2,1)S(1)} %collective-permute-done.1.att_other, ...), custom_call_target="tpu_custom_call" | custom-call | flops 5368709 | bytes 55050 | tf_op jit(solution)/shard_map/pallas_call | solution.py:25
  54.2 2.6 %shard_map.91 = (bf16[512,512]{1,0:T(8,128)(2,1)S(1)}, f32[128,512]{1,0:T(8,128)S(1)}, f32[128,512]{1,0:T(8,128)S(1)}) custom-call(s32[8]{0:T(128)S(1)} %stack.32.place, bf16[512,512]{1,0:T(8,128)(2,1)S(1)} %copy-done, bf16[2,128,512]{2,1,0:T(8,128)(2,1)S(1)} %get-tuple-element.49.kv, f32[512,128]{1,0:T(8,128)S(1)} %get-tuple-element.50.lse, ...), custom_call_target="tpu_custom_call" | custom-call | flops 5368709 | bytes 28836 | tf_op jit(solution)/shard_map/pallas_call | solution.py:25
  56.8 1.3 %collective-permute-start.16 = (bf16[2,256,512]{2,1,0:T(8,128)(2,1)S(1)}, bf16[2,256,512]{2,1,0:T(8,128)(2,1)S(1)}, u32[]{:S(2)}, u32[]{:S(2)}) collective-permute-start(bf16[2,256,512]{2,1,0:T(8,128)(2,1)S(1)} %collective-permute-done.15.refs_0_.refs_2_.refs_4_), channel_id=1, source_target_pairs={{1,0},{2,3},{5,4},{6,7},{9,8},{10,11},{13,12},{14,15},{17,16},{18,... | collective-permute-start | bytes 1572872 | tf_op jit(solution)/shard_map/ppermute | solution.py:316
  58.8 4.8 %collective-permute-done.12.refs_5_ = bf16[1,256,512]{2,1,0:T(8,128)(2,1)S(1)} collective-permute-done((bf16[1,256,512]{2,1,0:T(8,128)(2,1)S(1)}, bf16[1,256,512]{2,1,0:T(8,128)(2,1)S(1)}, u32[]{:S(2)}, u32[]{:S(2)}) %collective-permute-start.12) | collective-permute-done | bytes 262176 | tf_op jit(solution)/shard_map/ppermute | solution.py:316
  64.7 1.6 %collective-permute-start.23 = (bf16[256,512]{1,0:T(8,128)(2,1)S(1)}, bf16[256,512]{1,0:T(8,128)(2,1)S(1)}, u32[]{:S(2)}, u32[]{:S(2)}) collective-permute-start(bf16[256,512]{1,0:T(8,128)(2,1)S(1)} %get-tuple-element.62), channel_id=1, source_target_pairs={{0,8},{4,12},{8,0},{12,4},{16,24},{20,28},{24,16},{28,20},{1,9},{5... | collective-permute-start | bytes 786440 | tf_op jit(solution)/shard_map/ppermute | solution.py:310
  66.2 1.4 %shard_map.90 = (f32[256,512]{1,0:T(8,128)S(1)}, f32[1,128,512]{2,1,0:T(8,128)S(1)}, bf16[1,128,512]{2,1,0:T(8,128)(2,1)S(1)}) custom-call(s32[8]{0:T(128)S(1)} %stack.32.place, bf16[4,128,512]{2,1,0:T(8,128)(2,1)S(1)} %collective-permute-done.7.refs_0_, bf16[4,128,512]{2,1,0:T(8,128)(2,1)S(1)} %collective-permute-done.8.refs_1_, ...), custom_call_target="tpu_custom_call" | custom-call | flops 5368709 | bytes 56361 | tf_op jit(solution)/shard_map/pallas_call | solution.py:25
  67.7 1.6 %collective-permute-start.21 = (bf16[256,512]{1,0:T(8,128)(2,1)S(1)}, bf16[256,512]{1,0:T(8,128)(2,1)S(1)}, u32[]{:S(2)}, u32[]{:S(2)}) collective-permute-start(bf16[256,512]{1,0:T(8,128)(2,1)S(1)} %get-tuple-element.87), channel_id=1, source_target_pairs={{0,16},{4,20},{8,24},{12,28},{16,0},{20,4},{24,8},{28,12},{1,17},{... | collective-permute-start | bytes 786440 | tf_op jit(solution)/shard_map/ppermute | solution.py:310
  69.3 2.2 %shard_map.92 = (bf16[512,512]{1,0:T(8,128)(2,1)S(1)}, f32[128,512]{1,0:T(8,128)S(1)}, f32[128,512]{1,0:T(8,128)S(1)}) custom-call(s32[8]{0:T(128)S(1)} %stack.32.place, bf16[512,512]{1,0:T(8,128)(2,1)S(1)} %copy-done, bf16[2,128,512]{2,1,0:T(8,128)(2,1)S(1)} %get-tuple-element.49.kv, f32[512,128]{1,0:T(8,128)S(1)} %get-tuple-element.50.lse, ...), custom_call_target="tpu_custom_call" | custom-call | flops 5368709 | bytes 35389 | tf_op jit(solution)/shard_map/pallas_call | solution.py:25
  71.5 1.3 %collective-permute-start.18 = (bf16[1,256,512]{2,1,0:T(8,128)(2,1)S(1)}, bf16[1,256,512]{2,1,0:T(8,128)(2,1)S(1)}, u32[]{:S(2)}, u32[]{:S(2)}) collective-permute-start(bf16[1,256,512]{2,1,0:T(8,128)(2,1)S(1)} %collective-permute-done.17.refs_4_), channel_id=1, source_target_pairs={{1,0},{2,3},{5,4},{6,7},{9,8},{10,11},{13,12},{14,15},{17,16},{18,... | collective-permute-start | bytes 786440 | tf_op jit(solution)/shard_map/ppermute | solution.py:316
  72.9 2.9 %collective-permute-done.16.refs_1_.refs_3_.refs_5_ = bf16[2,256,512]{2,1,0:T(8,128)(2,1)S(1)} collective-permute-done((bf16[2,256,512]{2,1,0:T(8,128)(2,1)S(1)}, bf16[2,256,512]{2,1,0:T(8,128)(2,1)S(1)}, u32[]{:S(2)}, u32[]{:S(2)}) %collective-permute-start.16) | collective-permute-done | bytes 524320 | tf_op jit(solution)/shard_map/ppermute | solution.py:316
  76.8 1.6 %collective-permute-start.24 = (bf16[512,512]{1,0:T(8,128)(2,1)S(1)}, bf16[512,512]{1,0:T(8,128)(2,1)S(1)}, u32[]{:S(2)}, u32[]{:S(2)}) collective-permute-start(bf16[512,512]{1,0:T(8,128)(2,1)S(1)} %shard_map.97), channel_id=1, source_target_pairs={{0,16},{4,20},{8,24},{12,28},{16,0},{20,4},{24,8},{28,12},{1,17},{... | collective-permute-start | bytes 1572872 | tf_op jit(solution)/shard_map/ppermute | solution.py:310
  79.4 1.6 %collective-permute-start.22 = (bf16[512,512]{1,0:T(8,128)(2,1)S(1)}, bf16[512,512]{1,0:T(8,128)(2,1)S(1)}, u32[]{:S(2)}, u32[]{:S(2)}) collective-permute-start(bf16[512,512]{1,0:T(8,128)(2,1)S(1)} %shard_map.96), channel_id=1, source_target_pairs={{0,8},{4,12},{8,0},{12,4},{16,24},{20,28},{24,16},{28,20},{1,9},{5... | collective-permute-start | bytes 1572872 | tf_op jit(solution)/shard_map/ppermute | solution.py:310
  81.0 4.2 %collective-permute-done.18.refs_5_ = bf16[1,256,512]{2,1,0:T(8,128)(2,1)S(1)} collective-permute-done((bf16[1,256,512]{2,1,0:T(8,128)(2,1)S(1)}, bf16[1,256,512]{2,1,0:T(8,128)(2,1)S(1)}, u32[]{:S(2)}, u32[]{:S(2)}) %collective-permute-start.18) | collective-permute-done | bytes 262176 | tf_op jit(solution)/shard_map/ppermute | solution.py:316
  85.2 1.1 %shard_map.93 = (f32[1,128,512]{2,1,0:T(8,128)S(1)}, bf16[1,128,512]{2,1,0:T(8,128)(2,1)S(1)}) custom-call(s32[8]{0:T(128)S(1)} %stack.32.place, bf16[2,256,512]{2,1,0:T(8,128)(2,1)S(1)} %collective-permute-done.15.refs_0_.refs_2_.refs_4_, bf16[2,256,512]{2,1,0:T(8,128)(2,1)S(1)} %collective-permute-done.16.refs_1_.refs_3_.refs_5_, ...), custom_call_target="tpu_custom_call" | custom-call | flops 5368709 | bytes 51118 | tf_op jit(solution)/shard_map/pallas_call | solution.py:25
  86.4 1.3 %collective-permute-done.19.grad_other = bf16[1,128,512]{2,1,0:T(8,128)(2,1)S(1)} collective-permute-done((bf16[1,128,512]{2,1,0:T(8,128)(2,1)S(1)}, bf16[1,128,512]{2,1,0:T(8,128)(2,1)S(1)}, u32[]{:S(2)}, u32[]{:S(2)}) %collective-permute-start.19) | collective-permute-done | bytes 131104 | tf_op jit(solution)/shard_map/ppermute | solution.py:310
  87.7 2.9 %shard_map.94 = (bf16[512,512]{1,0:T(8,128)(2,1)}, f32[128,512]{1,0:T(8,128)S(1)}, bf16[128,512]{1,0:T(8,128)(2,1)S(1)}) custom-call(s32[8]{0:T(128)S(1)} %stack.32.place, bf16[512,512]{1,0:T(8,128)(2,1)S(1)} %copy-done, bf16[2,128,512]{2,1,0:T(8,128)(2,1)S(1)} %get-tuple-element.49.kv, f32[512,128]{1,0:T(8,128)S(1)} %get-tuple-element.50.lse, ...), custom_call_target="tpu_custom_call" | custom-call | flops 5368709 | bytes 34079 | tf_op jit(solution)/shard_map/pallas_call | solution.py:25
  91.7 4.5 %collective-permute-done.20.other = bf16[128,512]{1,0:T(8,128)(2,1)S(1)} collective-permute-done((bf16[128,512]{1,0:T(8,128)(2,1)S(1)}, bf16[128,512]{1,0:T(8,128)(2,1)S(1)}, u32[]{:S(2)}, u32[]{:S(2)}) %collective-permute-start.20) | collective-permute-done | bytes 131104 | tf_op jit(solution)/shard_map/ppermute | solution.py:310
  (44 shorter events, 11.7 us)
Async XLA Ops:
  0.6 0.8 copy-start.3
  1.5 1.2 %copy-start.2 = (bf16[128,4096]{1,0:T(8,128)(2,1)S(1)}, bf16[128,4096]{1,0:T(8,128)(2,1)}, u32[]{:S(2)}) copy-start(bf16[128,4096]{1,0:T(8,128)(2,1)} %grad.1) | copy-start | bytes 3145732
  2.7 0.8 copy-start.4
  3.5 4.5 %copy-start.1 = (bf16[512,512]{1,0:T(8,128)(2,1)S(1)}, bf16[512,512]{1,0:T(8,128)(2,1)}, u32[]{:S(2)}) copy-start(bf16[512,512]{1,0:T(8,128)(2,1)} %refs_8_.1) | copy-start | bytes 1572868
  3.5 21.4 %copy-start = (bf16[512,512]{1,0:T(8,128)(2,1)S(1)}, bf16[512,512]{1,0:T(8,128)(2,1)}, u32[]{:S(2)}) copy-start(bf16[512,512]{1,0:T(8,128)(2,1)} %queries.6) | copy-start | bytes 1572868
  4.2 5.4 %collective-permute-start.2 = (bf16[4,128,512]{2,1,0:T(8,128)(2,1)S(1)}, bf16[4,128,512]{2,1,0:T(8,128)(2,1)S(1)}, u32[]{:S(2)}, u32[]{:S(2)}) collective-permute-start(bf16[4,128,512]{2,1,0:T(8,128)(2,1)S(1)} %get-tuple-element.52), channel_id=1, source_target_pairs={{0,4},{4,0},{8,12},{12,8},{16,20},{20,16},{24,28},{28,24},{1,5},{5... | collective-permute-start | bytes 1572872 | tf_op jit(solution)/shard_map/ppermute | solution.py:310
  4.7 18.2 %collective-permute-start = (bf16[640,512]{1,0:T(8,128)(2,1)S(1)}, bf16[640,512]{1,0:T(8,128)(2,1)S(1)}, u32[]{:S(2)}, u32[]{:S(2)}) collective-permute-start(bf16[640,512]{1,0:T(8,128)(2,1)S(1)} %get-tuple-element.48.refs_0_), channel_id=1, source_target_pairs={{0,1},{1,0},{2,3},{3,2},{4,5},{5,4},{6,7},{7,6},{8,9},{9,8},{10,11... | collective-permute-start | bytes 1966088 | tf_op jit(solution)/shard_map/ppermute | solution.py:310
  7.4 8.2 %collective-permute-start.7 = (bf16[4,128,512]{2,1,0:T(8,128)(2,1)S(1)}, bf16[4,128,512]{2,1,0:T(8,128)(2,1)S(1)}, u32[]{:S(2)}, u32[]{:S(2)}) collective-permute-start(bf16[4,128,512]{2,1,0:T(8,128)(2,1)S(1)} %get-tuple-element.57), channel_id=1, source_target_pairs={{1,2},{2,1},{5,6},{6,5},{9,10},{10,9},{13,14},{14,13},{17,18},{18,... | collective-permute-start | bytes 1572872 | tf_op jit(solution)/shard_map/ppermute | solution.py:313
  8.1 21.1 %collective-permute-start.5 = (bf16[512,512]{1,0:T(8,128)(2,1)S(1)}, bf16[512,512]{1,0:T(8,128)(2,1)S(1)}, u32[]{:S(2)}, u32[]{:S(2)}) collective-permute-start(bf16[512,512]{1,0:T(8,128)(2,1)S(1)} %copy-done.1), channel_id=1, source_target_pairs={{0,8},{4,12},{8,0},{12,4},{16,24},{20,28},{24,16},{28,20},{1,9},{5... | collective-permute-start | bytes 1572872 | tf_op jit(solution)/shard_map/ppermute | solution.py:310
  9.6 24.6 %collective-permute-start.3 = (bf16[4,128,512]{2,1,0:T(8,128)(2,1)S(1)}, bf16[4,128,512]{2,1,0:T(8,128)(2,1)S(1)}, u32[]{:S(2)}, u32[]{:S(2)}) collective-permute-start(bf16[4,128,512]{2,1,0:T(8,128)(2,1)S(1)} %collective-permute-done.2.refs_1_), channel_id=1, source_target_pairs={{0,1},{1,0},{2,3},{3,2},{4,5},{5,4},{6,7},{7,6},{8,9},{9,8},{10,11... | collective-permute-start | bytes 1572872 | tf_op jit(solution)/shard_map/ppermute | solution.py:310
  14.0 23.1 %collective-permute-start.6 = (bf16[512,512]{1,0:T(8,128)(2,1)S(1)}, bf16[512,512]{1,0:T(8,128)(2,1)S(1)}, u32[]{:S(2)}, u32[]{:S(2)}) collective-permute-start(bf16[512,512]{1,0:T(8,128)(2,1)S(1)} %copy-done.1), channel_id=1, source_target_pairs={{0,16},{4,20},{8,24},{12,28},{16,0},{20,4},{24,8},{28,12},{1,17},{... | collective-permute-start | bytes 1572872 | tf_op jit(solution)/shard_map/ppermute | solution.py:310
  23.0 14.1 %collective-permute-start.8 = (bf16[4,128,512]{2,1,0:T(8,128)(2,1)S(1)}, bf16[4,128,512]{2,1,0:T(8,128)(2,1)S(1)}, u32[]{:S(2)}, u32[]{:S(2)}) collective-permute-start(bf16[4,128,512]{2,1,0:T(8,128)(2,1)S(1)} %collective-permute-done.2.refs_1_), channel_id=1, source_target_pairs={{1,2},{2,1},{5,6},{6,5},{9,10},{10,9},{13,14},{14,13},{17,18},{18,... | collective-permute-start | bytes 1572872 | tf_op jit(solution)/shard_map/ppermute | solution.py:313
  23.6 21.8 %collective-permute-start.9 = (bf16[4,128,512]{2,1,0:T(8,128)(2,1)S(1)}, bf16[4,128,512]{2,1,0:T(8,128)(2,1)S(1)}, u32[]{:S(2)}, u32[]{:S(2)}) collective-permute-start(bf16[4,128,512]{2,1,0:T(8,128)(2,1)S(1)} %collective-permute-done.7.refs_0_), channel_id=1, source_target_pairs={{1,0},{2,3},{5,4},{6,7},{9,8},{10,11},{13,12},{14,15},{17,16},{18,... | collective-permute-start | bytes 1572872 | tf_op jit(solution)/shard_map/ppermute | solution.py:316
  29.2 16.3 %collective-permute-start.1 = (bf16[512,512]{1,0:T(8,128)(2,1)S(1)}, bf16[512,512]{1,0:T(8,128)(2,1)S(1)}, u32[]{:S(2)}, u32[]{:S(2)}) collective-permute-start(bf16[512,512]{1,0:T(8,128)(2,1)S(1)} %get-tuple-element.51.att_own), channel_id=1, source_target_pairs={{0,4},{4,0},{8,12},{12,8},{16,20},{20,16},{24,28},{28,24},{1,5},{5... | collective-permute-start | bytes 1572872 | tf_op jit(solution)/shard_map/ppermute | solution.py:310
  34.2 14.3 %collective-permute-start.4 = (bf16[512,512]{1,0:T(8,128)(2,1)S(1)}, bf16[512,512]{1,0:T(8,128)(2,1)S(1)}, u32[]{:S(2)}, u32[]{:S(2)}) collective-permute-start(bf16[512,512]{1,0:T(8,128)(2,1)S(1)} %copy-done.1), channel_id=1, source_target_pairs={{0,24},{4,28},{8,16},{12,20},{16,8},{20,12},{24,0},{28,4},{1,25},{... | collective-permute-start | bytes 1572872 | tf_op jit(solution)/shard_map/ppermute | solution.py:310
  37.1 11.4 %collective-permute-start.11 = (bf16[1,256,512]{2,1,0:T(8,128)(2,1)S(1)}, bf16[1,256,512]{2,1,0:T(8,128)(2,1)S(1)}, u32[]{:S(2)}, u32[]{:S(2)}) collective-permute-start(bf16[1,256,512]{2,1,0:T(8,128)(2,1)S(1)} %get-tuple-element.61), channel_id=1, source_target_pairs={{1,2},{2,1},{5,6},{6,5},{9,10},{10,9},{13,14},{14,13},{17,18},{18,... | collective-permute-start | bytes 786440 | tf_op jit(solution)/shard_map/ppermute | solution.py:313
  37.8 19.0 %collective-permute-start.10 = (bf16[4,128,512]{2,1,0:T(8,128)(2,1)S(1)}, bf16[4,128,512]{2,1,0:T(8,128)(2,1)S(1)}, u32[]{:S(2)}, u32[]{:S(2)}) collective-permute-start(bf16[4,128,512]{2,1,0:T(8,128)(2,1)S(1)} %collective-permute-done.8.refs_1_), channel_id=1, source_target_pairs={{1,0},{2,3},{5,4},{6,7},{9,8},{10,11},{13,12},{14,15},{17,16},{18,... | collective-permute-start | bytes 1572872 | tf_op jit(solution)/shard_map/ppermute | solution.py:316
  48.5 8.3 %collective-permute-start.15 = (bf16[2,256,512]{2,1,0:T(8,128)(2,1)S(1)}, bf16[2,256,512]{2,1,0:T(8,128)(2,1)S(1)}, u32[]{:S(2)}, u32[]{:S(2)}) collective-permute-start(bf16[2,256,512]{2,1,0:T(8,128)(2,1)S(1)} %get-tuple-element.73), channel_id=1, source_target_pairs={{1,2},{2,1},{5,6},{6,5},{9,10},{10,9},{13,14},{14,13},{17,18},{18,... | collective-permute-start | bytes 1572872 | tf_op jit(solution)/shard_map/ppermute | solution.py:313
  51.0 3.2 %collective-permute-start.14 = (bf16[2,128,512]{2,1,0:T(8,128)(2,1)S(1)}, bf16[2,128,512]{2,1,0:T(8,128)(2,1)S(1)}, u32[]{:S(2)}, u32[]{:S(2)}) collective-permute-start(bf16[2,128,512]{2,1,0:T(8,128)(2,1)S(1)} %get-tuple-element.54), channel_id=1, source_target_pairs={{0,4},{4,0},{8,12},{12,8},{16,20},{20,16},{24,28},{28,24},{1,5},{5... | collective-permute-start | bytes 786440 | tf_op jit(solution)/shard_map/ppermute | solution.py:310
  51.1 12.6 %collective-permute-start.12 = (bf16[1,256,512]{2,1,0:T(8,128)(2,1)S(1)}, bf16[1,256,512]{2,1,0:T(8,128)(2,1)S(1)}, u32[]{:S(2)}, u32[]{:S(2)}) collective-permute-start(bf16[1,256,512]{2,1,0:T(8,128)(2,1)S(1)} %collective-permute-done.11.refs_4_), channel_id=1, source_target_pairs={{1,0},{2,3},{5,4},{6,7},{9,8},{10,11},{13,12},{14,15},{17,16},{18,... | collective-permute-start | bytes 786440 | tf_op jit(solution)/shard_map/ppermute | solution.py:316
  56.8 18.9 %collective-permute-start.16 = (bf16[2,256,512]{2,1,0:T(8,128)(2,1)S(1)}, bf16[2,256,512]{2,1,0:T(8,128)(2,1)S(1)}, u32[]{:S(2)}, u32[]{:S(2)}) collective-permute-start(bf16[2,256,512]{2,1,0:T(8,128)(2,1)S(1)} %collective-permute-done.15.refs_0_.refs_2_.refs_4_), channel_id=1, source_target_pairs={{1,0},{2,3},{5,4},{6,7},{9,8},{10,11},{13,12},{14,15},{17,16},{18,... | collective-permute-start | bytes 1572872 | tf_op jit(solution)/shard_map/ppermute | solution.py:316
  58.1 13.4 %collective-permute-start.17 = (bf16[1,256,512]{2,1,0:T(8,128)(2,1)S(1)}, bf16[1,256,512]{2,1,0:T(8,128)(2,1)S(1)}, u32[]{:S(2)}, u32[]{:S(2)}) collective-permute-start(bf16[1,256,512]{2,1,0:T(8,128)(2,1)S(1)} %get-tuple-element.76), channel_id=1, source_target_pairs={{1,2},{2,1},{5,6},{6,5},{9,10},{10,9},{13,14},{14,13},{17,18},{18,... | collective-permute-start | bytes 786440 | tf_op jit(solution)/shard_map/ppermute | solution.py:313
  64.7 8.2 %collective-permute-start.23 = (bf16[256,512]{1,0:T(8,128)(2,1)S(1)}, bf16[256,512]{1,0:T(8,128)(2,1)S(1)}, u32[]{:S(2)}, u32[]{:S(2)}) collective-permute-start(bf16[256,512]{1,0:T(8,128)(2,1)S(1)} %get-tuple-element.62), channel_id=1, source_target_pairs={{0,8},{4,12},{8,0},{12,4},{16,24},{20,28},{24,16},{28,20},{1,9},{5... | collective-permute-start | bytes 786440 | tf_op jit(solution)/shard_map/ppermute | solution.py:310
  67.6 1.7 %collective-permute-start.13 = (bf16[1,128,512]{2,1,0:T(8,128)(2,1)S(1)}, bf16[1,128,512]{2,1,0:T(8,128)(2,1)S(1)}, u32[]{:S(2)}, u32[]{:S(2)}) collective-permute-start(bf16[1,128,512]{2,1,0:T(8,128)(2,1)S(1)} %get-tuple-element.65), channel_id=1, source_target_pairs={{0,4},{4,0},{8,12},{12,8},{16,20},{20,16},{24,28},{28,24},{1,5},{5... | collective-permute-start | bytes 393224 | tf_op jit(solution)/shard_map/ppermute | solution.py:310
  67.7 10.7 %collective-permute-start.21 = (bf16[256,512]{1,0:T(8,128)(2,1)S(1)}, bf16[256,512]{1,0:T(8,128)(2,1)S(1)}, u32[]{:S(2)}, u32[]{:S(2)}) collective-permute-start(bf16[256,512]{1,0:T(8,128)(2,1)S(1)} %get-tuple-element.87), channel_id=1, source_target_pairs={{0,16},{4,20},{8,24},{12,28},{16,0},{20,4},{24,8},{28,12},{1,17},{... | collective-permute-start | bytes 786440 | tf_op jit(solution)/shard_map/ppermute | solution.py:310
  71.5 13.6 %collective-permute-start.18 = (bf16[1,256,512]{2,1,0:T(8,128)(2,1)S(1)}, bf16[1,256,512]{2,1,0:T(8,128)(2,1)S(1)}, u32[]{:S(2)}, u32[]{:S(2)}) collective-permute-start(bf16[1,256,512]{2,1,0:T(8,128)(2,1)S(1)} %collective-permute-done.17.refs_4_), channel_id=1, source_target_pairs={{1,0},{2,3},{5,4},{6,7},{9,8},{10,11},{13,12},{14,15},{17,16},{18,... | collective-permute-start | bytes 786440 | tf_op jit(solution)/shard_map/ppermute | solution.py:316
  76.8 19.4 %collective-permute-start.24 = (bf16[512,512]{1,0:T(8,128)(2,1)S(1)}, bf16[512,512]{1,0:T(8,128)(2,1)S(1)}, u32[]{:S(2)}, u32[]{:S(2)}) collective-permute-start(bf16[512,512]{1,0:T(8,128)(2,1)S(1)} %shard_map.97), channel_id=1, source_target_pairs={{0,16},{4,20},{8,24},{12,28},{16,0},{20,4},{24,8},{28,12},{1,17},{... | collective-permute-start | bytes 1572872 | tf_op jit(solution)/shard_map/ppermute | solution.py:310
  79.4 16.8 %collective-permute-start.22 = (bf16[512,512]{1,0:T(8,128)(2,1)S(1)}, bf16[512,512]{1,0:T(8,128)(2,1)S(1)}, u32[]{:S(2)}, u32[]{:S(2)}) collective-permute-start(bf16[512,512]{1,0:T(8,128)(2,1)S(1)} %shard_map.96), channel_id=1, source_target_pairs={{0,8},{4,12},{8,0},{12,4},{16,24},{20,28},{24,16},{28,20},{1,9},{5... | collective-permute-start | bytes 1572872 | tf_op jit(solution)/shard_map/ppermute | solution.py:310
  86.3 1.4 %collective-permute-start.19 = (bf16[1,128,512]{2,1,0:T(8,128)(2,1)S(1)}, bf16[1,128,512]{2,1,0:T(8,128)(2,1)S(1)}, u32[]{:S(2)}, u32[]{:S(2)}) collective-permute-start(bf16[1,128,512]{2,1,0:T(8,128)(2,1)S(1)} %get-tuple-element.79), channel_id=1, source_target_pairs={{0,4},{4,0},{8,12},{12,8},{16,20},{20,16},{24,28},{28,24},{1,5},{5... | collective-permute-start | bytes 393224 | tf_op jit(solution)/shard_map/ppermute | solution.py:310
  90.6 5.5 %collective-permute-start.20 = (bf16[128,512]{1,0:T(8,128)(2,1)S(1)}, bf16[128,512]{1,0:T(8,128)(2,1)S(1)}, u32[]{:S(2)}, u32[]{:S(2)}) collective-permute-start(bf16[128,512]{1,0:T(8,128)(2,1)S(1)} %get-tuple-element.84), channel_id=1, source_target_pairs={{0,1},{1,0},{2,3},{3,2},{4,5},{5,4},{6,7},{7,6},{8,9},{9,8},{10,11... | collective-permute-start | bytes 393224 | tf_op jit(solution)/shard_map/ppermute | solution.py:310

commit v3 on v2

--- a/solution.py
+++ b/solution.py
@@ -99,9 +99,9 @@
         early_q, early_k, early_v = refs[:3]
         refs = refs[3:]
     if final:
-        grad_q, keep, send, dk, dv, ds_all, p_all = refs
-    else:
-        grad_q, dk, dv, ds_all, p_all = refs
+        grad_q, keep, send, dk, dv = refs
+    else:
+        grad_q, dk, dv = refs
     if first:
         dk[...] = jnp.zeros_like(dk)
         dv[...] = jnp.zeros_like(dv)
@@ -119,28 +119,26 @@
         rows = pl.ds(j * size, size)
         keys = -(-(j + 1) * size // BLOCK) * BLOCK
         early = keys - BLOCK
-        grads = []
+        columns = [pl.ds(h * HEAD_DIM, HEAD_DIM) for h in range(heads)]
+        lhs = [queries[rows, cols] for cols in columns]
+        grads = [
+            (grad_own[slot, :, cols] + grad_other[slot, :, cols].astype(F32)).astype(BF16)
+            for cols in columns
+        ]
+        scores = [dot(value, kv[0, :, :keys], 1, 0) for value in lhs]
+        dprobs = [dot(value, kv[1, :, :keys], 1, 0) for value in grads]
+        halves, dscores = [], []
         for h in range(heads):
-            cols = pl.ds(h * HEAD_DIM, HEAD_DIM)
-            grad = grad_own[slot, :, cols] + grad_other[slot, :, cols].astype(F32)
-            grad = grad.astype(BF16)
-            grads.append(grad)
-            scores = dot(queries[rows, cols], kv[0, :, :keys], 1, 0) * SCALE2
-            probs = jnp.exp2(scores - lse[rows, h : h + 1])
+            probs = jnp.exp2(scores[h] * SCALE2 - lse[rows, h : h + 1])
             last = jnp.where(col + early <= row + j * size, probs[:, early:], 0.0)
             probs = jnp.concatenate([probs[:, :early], last], axis=1) if early else last
-            dprobs = dot(grad, kv[1, :, :keys], 1, 0)
-            delta = jnp.sum(probs * dprobs, axis=1, keepdims=True)
-            dscores = (probs * (dprobs - delta) * SCALE).astype(BF16)
-            grad_q[rows, cols] = dot(dscores, kv[0, :, :keys], 1, 1).astype(BF16)
-            ds_all[pl.ds(h * size, size), :keys] = dscores
-            p_all[pl.ds(h * size, size), :keys] = probs.astype(BF16)
-        stacked_q = jnp.concatenate(
-            [queries[rows, h * HEAD_DIM : (h + 1) * HEAD_DIM] for h in range(heads)], axis=0
-        )
-        stacked_g = jnp.concatenate(grads, axis=0)
-        dk[:, :keys] += dot(stacked_q, ds_all[:, :keys], 0, 0)
-        dv[:, :keys] += dot(stacked_g, p_all[:, :keys], 0, 0)
+            delta = jnp.sum(probs * dprobs[h], axis=1, keepdims=True)
+            dscores.append((probs * (dprobs[h] - delta) * SCALE).astype(BF16))
+            halves.append(probs.astype(BF16))
+        for h, cols in enumerate(columns):
+            grad_q[rows, cols] = dot(dscores[h], kv[0, :, :keys], 1, 1).astype(BF16)
+        dk[:, :keys] += dot(jnp.concatenate(lhs, axis=0), jnp.concatenate(dscores, axis=0), 0, 0)
+        dv[:, :keys] += dot(jnp.concatenate(grads, axis=0), jnp.concatenate(halves, axis=0), 0, 0)
 
     def step(slot, carry):
         for j in range(length // size):
@@ -232,31 +230,30 @@
 
 
 def middle_kernel(count, place, *refs):
-    middle, late, weights = refs[:4], refs[4:6], refs[6 : 6 + count]
-    total, own, give = refs[6 + count :]
-    rows = own.shape[1]
-    value = None
+    middle, late, weights, out = refs[:4], refs[4:6], refs[6 : 6 + count], refs[-1]
+    total = None
     for c, weight in enumerate(weights):
         product = dot(middle_piece(place, middle, c), weight[...], 1, 0)
-        value = product if value is None else value + product
-    own[0] = value[:rows]
-    give[0] = value[rows:].astype(BF16)
-    value = None
+        total = product if total is None else total + product
+    out[0] = total
+    total = None
     for i in range(late[0].shape[0]):
         product = dot(late_piece(place, late, i, i), weights[i][...], 1, 0)
-        value = product if value is None else value + product
-    total[...] = value
+        total = product if total is None else total + product
+    out[1] = total
 
 
 def late_kernel(chunks, place, *refs):
     count = len(chunks)
-    late, weights, (early, own, give) = refs[: 2 * count], refs[2 * count : 3 * count], refs[3 * count :]
-    total = early[...]
+    late, weights = refs[: 2 * count], refs[2 * count : 3 * count]
+    early, own, give = refs[3 * count :]
+    total = early[1]
     for c, (i, j) in enumerate(chunks):
         total += dot(late_piece(place, late[2 * c : 2 * c + 2], i, j), weights[c][...], 1, 0)
     rows = own.shape[1]
-    own[0] = total[:rows]
-    give[0] = total[rows:].astype(BF16)
+    for q, value in enumerate((early[0], total)):
+        own[q] = value[:rows]
+        give[q] = value[rows:].astype(BF16)
 
 
 def term_kernel(c, i, j, late, spans, place, att_own, att_other, partial, *refs):
@@ -402,10 +399,7 @@
     def backward(first, final, base, own, other, carry):
         state = [shape((HEAD_DIM, length), F32)] * 2
         ends = [shape((2 * half, length), F32), shape((2 * half, length), BF16)]
-        size = (width // HEAD_DIM * rows, length)
-        scratch = [pltpu.VMEM(size, BF16)] * 2
-        if final:
-            scratch = [pltpu.VMEM((HEAD_DIM, length), F32)] * 2 + scratch
+        scratch = [pltpu.VMEM((HEAD_DIM, length), F32)] * 2 if final else []
         return call(
             functools.partial(backward_kernel, first, final, base),
             [shape((length, width), BF16)] + (ends if final else state),
@@ -451,35 +445,28 @@
         return found[0]
 
     terms = [term(0)]
+    total = place
     if tensor == 4:
-        total, grad_own, grad_give = call(
+        (total,) = call(
             functools.partial(middle_kernel, chips),
-            [
-                shape((2 * rows, width), F32),
-                shape((1, rows, width), F32),
-                shape((1, rows, width), BF16),
-            ],
+            [shape((2, 2 * rows, width), F32)],
             [tie(place, terms[0])] + middle + late[0][2] + weights,
             flops,
             scalars=1,
         )
+    terms += [term(c, total) for c in range(1, chips - 1)]
+
+    if tensor == 4:
+        ends = late[sizes[0] :]
+        grad_own, grad_give = call(
+            functools.partial(late_kernel, [item[:2] for item in ends]),
+            [shape((2, rows, width), F32), shape((2, rows, width), BF16)],
+            [place] + sum([item[2] for item in ends], []) + weights[sizes[0] :] + [total],
+            flops,
+            scalars=1,
+        )
         grad_other = swap(grad_give, "dp", 1)
-        done = backward(False, False, early, grad_own, grad_other, list(done))
-    terms += [term(c, done[1]) for c in range(1, chips - 1)]
-
-    if tensor == 4:
-        (grad_own, grad_give) = call(
-            functools.partial(late_kernel, [item[:2] for item in late[sizes[0] :]]),
-            [shape((1, rows, width), F32), shape((1, rows, width), BF16)],
-            [tie(place, done[1])]
-            + sum([item[2] for item in late[sizes[0] :]], [])
-            + weights[sizes[0] :]
-            + [total],
-            flops,
-            scalars=1,
-        )
-        grad_other = swap(grad_give, "dp", 1)
-        done = backward(False, True, early + 1, grad_own, grad_other, list(done))
+        done = backward(False, True, early, grad_own, grad_other, list(done))
     grad_q, keep, send = done
     grad_k, grad_v, grad_weight = call(
         finish_kernel,

time: 97.6 us -> 94.3 us (0.966)
  Pallas kernels: 23.8 us -> 21.3 us
  waiting for transfers between devices: 39.7 us -> 37.5 us
  starting transfers between devices: 29.9 us -> 31.3 us
    ppermute x15 -> x14, waiting for transfers between devices: 21.4 us -> 17.6 us  [swap(): lax.ppermute(value, axis, [(i, i ^ mask) for i in range(lax.axis_size(axi...]
    pallas_call x15 -> x14, Pallas kernels: 23.8 us -> 21.3 us  [call(): pl.pallas_call(kernel, out_shape=tuple(outs), in_specs=[SMEM] * scalars +...]
    ppermute x5, waiting for transfers between devices: 18.3 us -> 19.9 us  [outward(): return lax.ppermute(value, 'tensor', [(1, 0), (2, 3)])]
    ppermute x15 -> x14, starting transfers between devices: 20 us -> 21.3 us  [swap(): lax.ppermute(value, axis, [(i, i ^ mask) for i in range(lax.axis_size(axi...]
  transfers between devices with their start and end apart: 25 -> 24, of which waited for: 9 -> 9; matrix products, arithmetic and copies ran while one was open for 0% -> 0% of each run, Pallas kernels for 23% -> 21%
where the time goes in v3:
time: 94.3 us; the launch traced here: 93.9 us
  waiting for transfers between devices  37.5 us (40%)
  starting transfers between devices  31.3 us (33%)
  Pallas kernels  21.3 us (23%)
  local copies, waits for them, and re-layouts  2.87 us (3%)
    ppermute x14, starting transfers between devices, swap(): lax.ppermute(value, axis, [(i, i ^ mask) for i in range(lax.axis_size(axi...  21.3 us
    pallas_call x14, Pallas kernels, call(): pl.pallas_call(kernel, out_shape=tuple(outs), in_specs=[SMEM] * scalars +...  21.3 us
    ppermute x5, waiting for transfers between devices, outward(): return lax.ppermute(value, 'tensor', [(1, 0), (2, 3)])  19.9 us
    ppermute x14, waiting for transfers between devices, swap(): lax.ppermute(value, axis, [(i, i ^ mask) for i in range(lax.axis_size(axi...  17.6 us
    ppermute x5, starting transfers between devices, outward(): return lax.ppermute(value, 'tensor', [(1, 0), (2, 3)])  6.63 us
    ppermute x5, starting transfers between devices, across(): return lax.ppermute(value, 'tensor', [(1, 2), (2, 1)])  3.41 us
    unnamed x10, local copies, waits for them, and re-layouts  2.78 us
  transfers between devices with their start and end apart: 24, of which 9 were waited for; matrix products, arithmetic and copies ran while one was open for 0% of the time, Pallas kernels for 21%

profile of v3, /device:TPU:0, one launch (start us, length us, event | category | flops | bytes accessed | tf_op | source)
XLA Modules:
  0.0 93.9 jit_solution(14354807645118506214)
XLA Ops:
  1.5 1.2 %copy-done.2 = bf16[128,4096]{1,0:T(8,128)(2,1)S(1)} copy-done((bf16[128,4096]{1,0:T(8,128)(2,1)S(1)}, bf16[128,4096]{1,0:T(8,128)(2,1)}, u32[]{:S(2)}) %copy-start.2) | copy-done | bytes 1048600
  4.7 2.6 %collective-permute-start = (bf16[640,512]{1,0:T(8,128)(2,1)S(1)}, bf16[640,512]{1,0:T(8,128)(2,1)S(1)}, u32[]{:S(2)}, u32[]{:S(2)}) collective-permute-start(bf16[640,512]{1,0:T(8,128)(2,1)S(1)} %get-tuple-element.42.refs_0_), channel_id=1, source_target_pairs={{0,1},{1,0},{2,3},{3,2},{4,5},{5,4},{6,7},{7,6},{8,9},{9,8},{10,11... | collective-permute-start | bytes 1966088 | tf_op jit(solution)/shard_map/ppermute | solution.py:307
  8.1 1.6 %collective-permute-start.8 = (bf16[512,512]{1,0:T(8,128)(2,1)S(1)}, bf16[512,512]{1,0:T(8,128)(2,1)S(1)}, u32[]{:S(2)}, u32[]{:S(2)}) collective-permute-start(bf16[512,512]{1,0:T(8,128)(2,1)S(1)} %copy-done.1), channel_id=1, source_target_pairs={{0,8},{4,12},{8,0},{12,4},{16,24},{20,28},{24,16},{28,20},{1,9},{5... | collective-permute-start | bytes 1572872 | tf_op jit(solution)/shard_map/ppermute | solution.py:307
  9.6 4.4 %collective-permute-start.2 = (bf16[4,128,512]{2,1,0:T(8,128)(2,1)S(1)}, bf16[4,128,512]{2,1,0:T(8,128)(2,1)S(1)}, u32[]{:S(2)}, u32[]{:S(2)}) collective-permute-start(bf16[4,128,512]{2,1,0:T(8,128)(2,1)S(1)} %collective-permute-done.1.refs_1_), channel_id=1, source_target_pairs={{0,1},{1,0},{2,3},{3,2},{4,5},{5,4},{6,7},{7,6},{8,9},{9,8},{10,11... | collective-permute-start | bytes 1572872 | tf_op jit(solution)/shard_map/ppermute | solution.py:307
  14.0 1.5 %collective-permute-start.9 = (bf16[512,512]{1,0:T(8,128)(2,1)S(1)}, bf16[512,512]{1,0:T(8,128)(2,1)S(1)}, u32[]{:S(2)}, u32[]{:S(2)}) collective-permute-start(bf16[512,512]{1,0:T(8,128)(2,1)S(1)} %copy-done.1), channel_id=1, source_target_pairs={{0,16},{4,20},{8,24},{12,28},{16,0},{20,4},{24,8},{28,12},{1,17},{... | collective-permute-start | bytes 1572872 | tf_op jit(solution)/shard_map/ppermute | solution.py:307
  15.5 7.4 %collective-permute-done.near.first.refs_2_ = bf16[640,512]{1,0:T(8,128)(2,1)S(1)} collective-permute-done((bf16[640,512]{1,0:T(8,128)(2,1)S(1)}, bf16[640,512]{1,0:T(8,128)(2,1)S(1)}, u32[]{:S(2)}, u32[]{:S(2)}) %collective-permute-start) | collective-permute-done | bytes 655392 | tf_op jit(solution)/shard_map/ppermute | solution.py:307
  23.6 1.3 %collective-permute-start.4 = (bf16[4,128,512]{2,1,0:T(8,128)(2,1)S(1)}, bf16[4,128,512]{2,1,0:T(8,128)(2,1)S(1)}, u32[]{:S(2)}, u32[]{:S(2)}) collective-permute-start(bf16[4,128,512]{2,1,0:T(8,128)(2,1)S(1)} %collective-permute-done.3.refs_0_), channel_id=1, source_target_pairs={{1,0},{2,3},{5,4},{6,7},{9,8},{10,11},{13,12},{14,15},{17,16},{18,... | collective-permute-start | bytes 1572872 | tf_op jit(solution)/shard_map/ppermute | solution.py:313
  25.0 4.2 %shard_map.85 = (bf16[2,128,512]{2,1,0:T(8,128)(2,1)S(1)}, bf16[512,512]{1,0:T(8,128)(2,1)S(1)}, f32[512,128]{1,0:T(8,128)S(1)}) custom-call(s32[8]{0:T(128)S(1)} %stack.32.place, bf16[512,512]{1,0:T(8,128)(2,1)S(1)} %copy-done, bf16[64,512]{1,0:T(8,128)(2,1)S(1)} %bitcast.12, bf16[64,512]{1,0:T(8,128)(2,1)S(1)} %bitcast.14, ...), custom_call_target="tpu_custom_call" | custom-call | flops 5368709 | bytes 23593 | tf_op jit(solution)/shard_map/pallas_call | solution.py:25
  29.2 2.9 %collective-permute-start.5 = (bf16[512,512]{1,0:T(8,128)(2,1)S(1)}, bf16[512,512]{1,0:T(8,128)(2,1)S(1)}, u32[]{:S(2)}, u32[]{:S(2)}) collective-permute-start(bf16[512,512]{1,0:T(8,128)(2,1)S(1)} %copy-done.1), channel_id=1, source_target_pairs={{0,24},{4,28},{8,16},{12,20},{16,8},{20,12},{24,0},{28,4},{1,25},{... | collective-permute-start | bytes 1572872 | tf_op jit(solution)/shard_map/ppermute | solution.py:307
  32.0 2.1 %collective-permute-done.2.second.refs_3_ = bf16[4,128,512]{2,1,0:T(8,128)(2,1)S(1)} collective-permute-done((bf16[4,128,512]{2,1,0:T(8,128)(2,1)S(1)}, bf16[4,128,512]{2,1,0:T(8,128)(2,1)S(1)}, u32[]{:S(2)}, u32[]{:S(2)}) %collective-permute-start.2) | collective-permute-done | bytes 524320 | tf_op jit(solution)/shard_map/ppermute | solution.py:307
  35.0 1.3 %collective-permute-start.12 = (bf16[4,128,512]{2,1,0:T(8,128)(2,1)S(1)}, bf16[4,128,512]{2,1,0:T(8,128)(2,1)S(1)}, u32[]{:S(2)}, u32[]{:S(2)}) collective-permute-start(bf16[4,128,512]{2,1,0:T(8,128)(2,1)S(1)} %collective-permute-done.7.refs_1_), channel_id=1, source_target_pairs={{1,0},{2,3},{5,4},{6,7},{9,8},{10,11},{13,12},{14,15},{17,16},{18,... | collective-permute-start | bytes 1572872 | tf_op jit(solution)/shard_map/ppermute | solution.py:313
  36.3 9.2 %collective-permute-done.4.refs_2_ = bf16[4,128,512]{2,1,0:T(8,128)(2,1)S(1)} collective-permute-done((bf16[4,128,512]{2,1,0:T(8,128)(2,1)S(1)}, bf16[4,128,512]{2,1,0:T(8,128)(2,1)S(1)}, u32[]{:S(2)}, u32[]{:S(2)}) %collective-permute-start.4) | collective-permute-done | bytes 524320 | tf_op jit(solution)/shard_map/ppermute | solution.py:313
  46.1 1.8 %shard_map.87 = (f32[2,128,512]{2,1,0:T(8,128)S(1)}, bf16[2,128,512]{2,1,0:T(8,128)(2,1)S(1)}) custom-call(s32[8]{0:T(128)S(1)} %stack.32.place, bf16[640,512]{1,0:T(8,128)(2,1)S(1)} %get-tuple-element.42.refs_0_, bf16[4,128,512]{2,1,0:T(8,128)(2,1)S(1)} %collective-permute-done.1.refs_1_, bf16[640,512]{1,0:T(8,128)(2,1)S(1)} %collective-permute-done.near.first.refs_2_, ...), custom_call_target="tpu_custom_call" | custom-call | flops 1610612736 | bytes 52429 | tf_op jit(solution)/shard_map/pallas_call | solution.py:25
  48.0 1.3 %collective-permute-start.17 = (bf16[1,256,512]{2,1,0:T(8,128)(2,1)S(1)}, bf16[1,256,512]{2,1,0:T(8,128)(2,1)S(1)}, u32[]{:S(2)}, u32[]{:S(2)}) collective-permute-start(bf16[1,256,512]{2,1,0:T(8,128)(2,1)S(1)} %collective-permute-done.10.refs_4_), channel_id=1, source_target_pairs={{1,0},{2,3},{5,4},{6,7},{9,8},{10,11},{13,12},{14,15},{17,16},{18,... | collective-permute-start | bytes 786440 | tf_op jit(solution)/shard_map/ppermute | solution.py:313
  49.3 1.8 %shard_map.88 = (bf16[512,512]{1,0:T(8,128)(2,1)S(1)}, bf16[512,512]{1,0:T(8,128)(2,1)S(1)}, bf16[512,512]{1,0:T(8,128)(2,1)S(1)}, bf16[512,512]{1,0:T(8,128)(2,1)S(1)}) custom-call(s32[8]{0:T(128)S(1)} %stack.32.place, bf16[512,512]{1,0:T(8,128)(2,1)S(1)} %get-tuple-element.49.att_own, bf16[512,512]{1,0:T(8,128)(2,1)S(1)} %collective-permute-done.6.att_other, ...), custom_call_target="tpu_custom_call" | custom-call | flops 5368709 | bytes 55050 | tf_op jit(solution)/shard_map/pallas_call | solution.py:25
  51.2 1.8 %shard_map.89 = (bf16[512,512]{1,0:T(8,128)(2,1)S(1)}, f32[128,512]{1,0:T(8,128)S(1)}, f32[128,512]{1,0:T(8,128)S(1)}) custom-call(s32[8]{0:T(128)S(1)} %stack.32.place, bf16[512,512]{1,0:T(8,128)(2,1)S(1)} %copy-done, bf16[2,128,512]{2,1,0:T(8,128)(2,1)S(1)} %get-tuple-element.43.kv, f32[512,128]{1,0:T(8,128)S(1)} %get-tuple-element.44.lse, ...), custom_call_target="tpu_custom_call" | custom-call | flops 5368709 | bytes 28836 | tf_op jit(solution)/shard_map/pallas_call | solution.py:25
  53.0 3.5 %collective-permute-done.12.refs_3_ = bf16[4,128,512]{2,1,0:T(8,128)(2,1)S(1)} collective-permute-done((bf16[4,128,512]{2,1,0:T(8,128)(2,1)S(1)}, bf16[4,128,512]{2,1,0:T(8,128)(2,1)S(1)}, u32[]{:S(2)}, u32[]{:S(2)}) %collective-permute-start.12) | collective-permute-done | bytes 524320 | tf_op jit(solution)/shard_map/ppermute | solution.py:313
  56.5 1.3 %collective-permute-start.14 = (bf16[2,256,512]{2,1,0:T(8,128)(2,1)S(1)}, bf16[2,256,512]{2,1,0:T(8,128)(2,1)S(1)}, u32[]{:S(2)}, u32[]{:S(2)}) collective-permute-start(bf16[2,256,512]{2,1,0:T(8,128)(2,1)S(1)} %collective-permute-done.11.refs_0_.refs_2_.refs_4_), channel_id=1, source_target_pairs={{1,0},{2,3},{5,4},{6,7},{9,8},{10,11},{13,12},{14,15},{17,16},{18,... | collective-permute-start | bytes 1572872 | tf_op jit(solution)/shard_map/ppermute | solution.py:313
  58.4 3.7 %collective-permute-done.17.refs_5_ = bf16[1,256,512]{2,1,0:T(8,128)(2,1)S(1)} collective-permute-done((bf16[1,256,512]{2,1,0:T(8,128)(2,1)S(1)}, bf16[1,256,512]{2,1,0:T(8,128)(2,1)S(1)}, u32[]{:S(2)}, u32[]{:S(2)}) %collective-permute-start.17) | collective-permute-done | bytes 262176 | tf_op jit(solution)/shard_map/ppermute | solution.py:313
  63.1 1.9 %collective-permute-start.20 = (bf16[256,512]{1,0:T(8,128)(2,1)S(1)}, bf16[256,512]{1,0:T(8,128)(2,1)S(1)}, u32[]{:S(2)}, u32[]{:S(2)}) collective-permute-start(bf16[256,512]{1,0:T(8,128)(2,1)S(1)} %get-tuple-element.75), channel_id=1, source_target_pairs={{0,16},{4,20},{8,24},{12,28},{16,0},{20,4},{24,8},{28,12},{1,17},{... | collective-permute-start | bytes 786440 | tf_op jit(solution)/shard_map/ppermute | solution.py:307
  65.0 1.5 %collective-permute-start.22 = (bf16[256,512]{1,0:T(8,128)(2,1)S(1)}, bf16[256,512]{1,0:T(8,128)(2,1)S(1)}, u32[]{:S(2)}, u32[]{:S(2)}) collective-permute-start(bf16[256,512]{1,0:T(8,128)(2,1)S(1)} %get-tuple-element.63), channel_id=1, source_target_pairs={{0,8},{4,12},{8,0},{12,4},{16,24},{20,28},{24,16},{28,20},{1,9},{5... | collective-permute-start | bytes 786440 | tf_op jit(solution)/shard_map/ppermute | solution.py:307
  66.5 1.4 %shard_map.91.refs_9_ = f32[2,256,512]{2,1,0:T(8,128)S(1)} custom-call(s32[8]{0:T(128)S(1)} %stack.32.place, bf16[4,128,512]{2,1,0:T(8,128)(2,1)S(1)} %collective-permute-done.3.refs_0_, bf16[4,128,512]{2,1,0:T(8,128)(2,1)S(1)} %collective-permute-done.7.refs_1_, bf16[4,128,512]{2,1,0:T(8,128)(2,1)S(1)} %collective-permute-done.4.refs_2_, ...), custom_call_target="tpu_custom_call" | custom-call | flops 5368709 | bytes 57672 | tf_op jit(solution)/shard_map/pallas_call | solution.py:25
  67.9 1.5 %collective-permute-start.16 = (bf16[1,256,512]{2,1,0:T(8,128)(2,1)S(1)}, bf16[1,256,512]{2,1,0:T(8,128)(2,1)S(1)}, u32[]{:S(2)}, u32[]{:S(2)}) collective-permute-start(bf16[1,256,512]{2,1,0:T(8,128)(2,1)S(1)} %collective-permute-done.15.refs_4_), channel_id=1, source_target_pairs={{1,0},{2,3},{5,4},{6,7},{9,8},{10,11},{13,12},{14,15},{17,16},{18,... | collective-permute-start | bytes 786440 | tf_op jit(solution)/shard_map/ppermute | solution.py:313
  69.4 1.9 %collective-permute-done.20.refs_6_ = bf16[256,512]{1,0:T(8,128)(2,1)S(1)} collective-permute-done((bf16[256,512]{1,0:T(8,128)(2,1)S(1)}, bf16[256,512]{1,0:T(8,128)(2,1)S(1)}, u32[]{:S(2)}, u32[]{:S(2)}) %collective-permute-start.20) | collective-permute-done | bytes 262176 | tf_op jit(solution)/shard_map/ppermute | solution.py:307
  71.3 3.6 %collective-permute-done.14.refs_1_.refs_3_.refs_5_ = bf16[2,256,512]{2,1,0:T(8,128)(2,1)S(1)} collective-permute-done((bf16[2,256,512]{2,1,0:T(8,128)(2,1)S(1)}, bf16[2,256,512]{2,1,0:T(8,128)(2,1)S(1)}, u32[]{:S(2)}, u32[]{:S(2)}) %collective-permute-start.14) | collective-permute-done | bytes 524320 | tf_op jit(solution)/shard_map/ppermute | solution.py:313
  75.0 1.0 %shard_map.95 = bf16[512,512]{1,0:T(8,128)(2,1)S(1)} custom-call(s32[8]{0:T(128)S(1)} %stack.32.place, bf16[512,512]{1,0:T(8,128)(2,1)S(1)} %get-tuple-element.49.att_own, bf16[512,512]{1,0:T(8,128)(2,1)S(1)} %collective-permute-done.6.att_other, bf16[512,512]{1,0:T(8,128)(2,1)S(1)} %get-tuple-element.74.partial, ...), custom_call_target="tpu_custom_call" | custom-call | flops 1610612736 | bytes 55050 | tf_op jit(solution)/shard_map/pallas_call | solution.py:25
  76.0 2.6 %collective-permute-start.21 = (bf16[512,512]{1,0:T(8,128)(2,1)S(1)}, bf16[512,512]{1,0:T(8,128)(2,1)S(1)}, u32[]{:S(2)}, u32[]{:S(2)}) collective-permute-start(bf16[512,512]{1,0:T(8,128)(2,1)S(1)} %shard_map.95), channel_id=1, source_target_pairs={{0,8},{4,12},{8,0},{12,4},{16,24},{20,28},{24,16},{28,20},{1,9},{5... | collective-permute-start | bytes 1572872 | tf_op jit(solution)/shard_map/ppermute | solution.py:307
  79.7 1.6 %collective-permute-start.23 = (bf16[512,512]{1,0:T(8,128)(2,1)S(1)}, bf16[512,512]{1,0:T(8,128)(2,1)S(1)}, u32[]{:S(2)}, u32[]{:S(2)}) collective-permute-start(bf16[512,512]{1,0:T(8,128)(2,1)S(1)} %shard_map.96), channel_id=1, source_target_pairs={{0,16},{4,20},{8,24},{12,28},{16,0},{20,4},{24,8},{28,12},{1,17},{... | collective-permute-start | bytes 1572872 | tf_op jit(solution)/shard_map/ppermute | solution.py:307
  81.2 1.1 %shard_map.92 = (f32[2,128,512]{2,1,0:T(8,128)S(1)}, bf16[2,128,512]{2,1,0:T(8,128)(2,1)S(1)}) custom-call(s32[8]{0:T(128)S(1)} %stack.32.place, bf16[2,256,512]{2,1,0:T(8,128)(2,1)S(1)} %collective-permute-done.11.refs_0_.refs_2_.refs_4_, bf16[2,256,512]{2,1,0:T(8,128)(2,1)S(1)} %collective-permute-done.14.refs_1_.refs_3_.refs_5_, ...), custom_call_target="tpu_custom_call" | custom-call | flops 5368709 | bytes 60293 | tf_op jit(solution)/shard_map/pallas_call | solution.py:25
  82.4 1.5 %collective-permute-done.18.grad_other = bf16[2,128,512]{2,1,0:T(8,128)(2,1)S(1)} collective-permute-done((bf16[2,128,512]{2,1,0:T(8,128)(2,1)S(1)}, bf16[2,128,512]{2,1,0:T(8,128)(2,1)S(1)}, u32[]{:S(2)}, u32[]{:S(2)}) %collective-permute-start.18) | collective-permute-done | bytes 262176 | tf_op jit(solution)/shard_map/ppermute | solution.py:307
  84.0 3.4 %shard_map.93 = (bf16[512,512]{1,0:T(8,128)(2,1)}, f32[128,512]{1,0:T(8,128)S(1)}, bf16[128,512]{1,0:T(8,128)(2,1)S(1)}) custom-call(s32[8]{0:T(128)S(1)} %stack.32.place, bf16[512,512]{1,0:T(8,128)(2,1)S(1)} %copy-done, bf16[2,128,512]{2,1,0:T(8,128)(2,1)S(1)} %get-tuple-element.43.kv, f32[512,128]{1,0:T(8,128)S(1)} %get-tuple-element.44.lse, ...), custom_call_target="tpu_custom_call" | custom-call | flops 5368709 | bytes 38011 | tf_op jit(solution)/shard_map/pallas_call | solution.py:25
  88.4 4.5 %collective-permute-done.19.other = bf16[128,512]{1,0:T(8,128)(2,1)S(1)} collective-permute-done((bf16[128,512]{1,0:T(8,128)(2,1)S(1)}, bf16[128,512]{1,0:T(8,128)(2,1)S(1)}, u32[]{:S(2)}, u32[]{:S(2)}) %collective-permute-start.19) | collective-permute-done | bytes 131104 | tf_op jit(solution)/shard_map/ppermute | solution.py:307
  (41 shorter events, 10.5 us)
Async XLA Ops:
  0.6 0.8 copy-start.3
  1.5 1.2 %copy-start.2 = (bf16[128,4096]{1,0:T(8,128)(2,1)S(1)}, bf16[128,4096]{1,0:T(8,128)(2,1)}, u32[]{:S(2)}) copy-start(bf16[128,4096]{1,0:T(8,128)(2,1)} %grad.1) | copy-start | bytes 3145732
  2.7 0.8 copy-start.4
  3.5 4.5 %copy-start.1 = (bf16[512,512]{1,0:T(8,128)(2,1)S(1)}, bf16[512,512]{1,0:T(8,128)(2,1)}, u32[]{:S(2)}) copy-start(bf16[512,512]{1,0:T(8,128)(2,1)} %refs_8_.1) | copy-start | bytes 1572868
  3.5 21.4 %copy-start = (bf16[512,512]{1,0:T(8,128)(2,1)S(1)}, bf16[512,512]{1,0:T(8,128)(2,1)}, u32[]{:S(2)}) copy-start(bf16[512,512]{1,0:T(8,128)(2,1)} %queries.4) | copy-start | bytes 1572868
  4.2 5.4 %collective-permute-start.1 = (bf16[4,128,512]{2,1,0:T(8,128)(2,1)S(1)}, bf16[4,128,512]{2,1,0:T(8,128)(2,1)S(1)}, u32[]{:S(2)}, u32[]{:S(2)}) collective-permute-start(bf16[4,128,512]{2,1,0:T(8,128)(2,1)S(1)} %get-tuple-element.45), channel_id=1, source_target_pairs={{0,4},{4,0},{8,12},{12,8},{16,20},{20,16},{24,28},{28,24},{1,5},{5... | collective-permute-start | bytes 1572872 | tf_op jit(solution)/shard_map/ppermute | solution.py:307
  4.7 18.2 %collective-permute-start = (bf16[640,512]{1,0:T(8,128)(2,1)S(1)}, bf16[640,512]{1,0:T(8,128)(2,1)S(1)}, u32[]{:S(2)}, u32[]{:S(2)}) collective-permute-start(bf16[640,512]{1,0:T(8,128)(2,1)S(1)} %get-tuple-element.42.refs_0_), channel_id=1, source_target_pairs={{0,1},{1,0},{2,3},{3,2},{4,5},{5,4},{6,7},{7,6},{8,9},{9,8},{10,11... | collective-permute-start | bytes 1966088 | tf_op jit(solution)/shard_map/ppermute | solution.py:307
  7.4 8.2 %collective-permute-start.3 = (bf16[4,128,512]{2,1,0:T(8,128)(2,1)S(1)}, bf16[4,128,512]{2,1,0:T(8,128)(2,1)S(1)}, u32[]{:S(2)}, u32[]{:S(2)}) collective-permute-start(bf16[4,128,512]{2,1,0:T(8,128)(2,1)S(1)} %get-tuple-element.47), channel_id=1, source_target_pairs={{1,2},{2,1},{5,6},{6,5},{9,10},{10,9},{13,14},{14,13},{17,18},{18,... | collective-permute-start | bytes 1572872 | tf_op jit(solution)/shard_map/ppermute | solution.py:310
  8.1 21.1 %collective-permute-start.8 = (bf16[512,512]{1,0:T(8,128)(2,1)S(1)}, bf16[512,512]{1,0:T(8,128)(2,1)S(1)}, u32[]{:S(2)}, u32[]{:S(2)}) collective-permute-start(bf16[512,512]{1,0:T(8,128)(2,1)S(1)} %copy-done.1), channel_id=1, source_target_pairs={{0,8},{4,12},{8,0},{12,4},{16,24},{20,28},{24,16},{28,20},{1,9},{5... | collective-permute-start | bytes 1572872 | tf_op jit(solution)/shard_map/ppermute | solution.py:307
  9.6 24.6 %collective-permute-start.2 = (bf16[4,128,512]{2,1,0:T(8,128)(2,1)S(1)}, bf16[4,128,512]{2,1,0:T(8,128)(2,1)S(1)}, u32[]{:S(2)}, u32[]{:S(2)}) collective-permute-start(bf16[4,128,512]{2,1,0:T(8,128)(2,1)S(1)} %collective-permute-done.1.refs_1_), channel_id=1, source_target_pairs={{0,1},{1,0},{2,3},{3,2},{4,5},{5,4},{6,7},{7,6},{8,9},{9,8},{10,11... | collective-permute-start | bytes 1572872 | tf_op jit(solution)/shard_map/ppermute | solution.py:307
  14.0 20.3 %collective-permute-start.9 = (bf16[512,512]{1,0:T(8,128)(2,1)S(1)}, bf16[512,512]{1,0:T(8,128)(2,1)S(1)}, u32[]{:S(2)}, u32[]{:S(2)}) collective-permute-start(bf16[512,512]{1,0:T(8,128)(2,1)S(1)} %copy-done.1), channel_id=1, source_target_pairs={{0,16},{4,20},{8,24},{12,28},{16,0},{20,4},{24,8},{28,12},{1,17},{... | collective-permute-start | bytes 1572872 | tf_op jit(solution)/shard_map/ppermute | solution.py:307
  23.0 11.3 %collective-permute-start.7 = (bf16[4,128,512]{2,1,0:T(8,128)(2,1)S(1)}, bf16[4,128,512]{2,1,0:T(8,128)(2,1)S(1)}, u32[]{:S(2)}, u32[]{:S(2)}) collective-permute-start(bf16[4,128,512]{2,1,0:T(8,128)(2,1)S(1)} %collective-permute-done.1.refs_1_), channel_id=1, source_target_pairs={{1,2},{2,1},{5,6},{6,5},{9,10},{10,9},{13,14},{14,13},{17,18},{18,... | collective-permute-start | bytes 1572872 | tf_op jit(solution)/shard_map/ppermute | solution.py:310
  23.6 21.8 %collective-permute-start.4 = (bf16[4,128,512]{2,1,0:T(8,128)(2,1)S(1)}, bf16[4,128,512]{2,1,0:T(8,128)(2,1)S(1)}, u32[]{:S(2)}, u32[]{:S(2)}) collective-permute-start(bf16[4,128,512]{2,1,0:T(8,128)(2,1)S(1)} %collective-permute-done.3.refs_0_), channel_id=1, source_target_pairs={{1,0},{2,3},{5,4},{6,7},{9,8},{10,11},{13,12},{14,15},{17,16},{18,... | collective-permute-start | bytes 1572872 | tf_op jit(solution)/shard_map/ppermute | solution.py:313
  29.2 16.3 %collective-permute-start.5 = (bf16[512,512]{1,0:T(8,128)(2,1)S(1)}, bf16[512,512]{1,0:T(8,128)(2,1)S(1)}, u32[]{:S(2)}, u32[]{:S(2)}) collective-permute-start(bf16[512,512]{1,0:T(8,128)(2,1)S(1)} %copy-done.1), channel_id=1, source_target_pairs={{0,24},{4,28},{8,16},{12,20},{16,8},{20,12},{24,0},{28,4},{1,25},{... | collective-permute-start | bytes 1572872 | tf_op jit(solution)/shard_map/ppermute | solution.py:307
  34.2 11.2 %collective-permute-start.6 = (bf16[512,512]{1,0:T(8,128)(2,1)S(1)}, bf16[512,512]{1,0:T(8,128)(2,1)S(1)}, u32[]{:S(2)}, u32[]{:S(2)}) collective-permute-start(bf16[512,512]{1,0:T(8,128)(2,1)S(1)} %get-tuple-element.49.att_own), channel_id=1, source_target_pairs={{0,4},{4,0},{8,12},{12,8},{16,20},{20,16},{24,28},{28,24},{1,5},{5... | collective-permute-start | bytes 1572872 | tf_op jit(solution)/shard_map/ppermute | solution.py:307
  34.3 11.1 %collective-permute-start.10 = (bf16[1,256,512]{2,1,0:T(8,128)(2,1)S(1)}, bf16[1,256,512]{2,1,0:T(8,128)(2,1)S(1)}, u32[]{:S(2)}, u32[]{:S(2)}) collective-permute-start(bf16[1,256,512]{2,1,0:T(8,128)(2,1)S(1)} %get-tuple-element.52), channel_id=1, source_target_pairs={{1,2},{2,1},{5,6},{6,5},{9,10},{10,9},{13,14},{14,13},{17,18},{18,... | collective-permute-start | bytes 786440 | tf_op jit(solution)/shard_map/ppermute | solution.py:310
  35.0 21.5 %collective-permute-start.12 = (bf16[4,128,512]{2,1,0:T(8,128)(2,1)S(1)}, bf16[4,128,512]{2,1,0:T(8,128)(2,1)S(1)}, u32[]{:S(2)}, u32[]{:S(2)}) collective-permute-start(bf16[4,128,512]{2,1,0:T(8,128)(2,1)S(1)} %collective-permute-done.7.refs_1_), channel_id=1, source_target_pairs={{1,0},{2,3},{5,4},{6,7},{9,8},{10,11},{13,12},{14,15},{17,16},{18,... | collective-permute-start | bytes 1572872 | tf_op jit(solution)/shard_map/ppermute | solution.py:313
  45.4 11.0 %collective-permute-start.11 = (bf16[2,256,512]{2,1,0:T(8,128)(2,1)S(1)}, bf16[2,256,512]{2,1,0:T(8,128)(2,1)S(1)}, u32[]{:S(2)}, u32[]{:S(2)}) collective-permute-start(bf16[2,256,512]{2,1,0:T(8,128)(2,1)S(1)} %get-tuple-element.53), channel_id=1, source_target_pairs={{1,2},{2,1},{5,6},{6,5},{9,10},{10,9},{13,14},{14,13},{17,18},{18,... | collective-permute-start | bytes 1572872 | tf_op jit(solution)/shard_map/ppermute | solution.py:310
  47.9 3.2 %collective-permute-start.13 = (bf16[2,128,512]{2,1,0:T(8,128)(2,1)S(1)}, bf16[2,128,512]{2,1,0:T(8,128)(2,1)S(1)}, u32[]{:S(2)}, u32[]{:S(2)}) collective-permute-start(bf16[2,128,512]{2,1,0:T(8,128)(2,1)S(1)} %get-tuple-element.55), channel_id=1, source_target_pairs={{0,4},{4,0},{8,12},{12,8},{16,20},{20,16},{24,28},{28,24},{1,5},{5... | collective-permute-start | bytes 786440 | tf_op jit(solution)/shard_map/ppermute | solution.py:307
  48.0 14.1 %collective-permute-start.17 = (bf16[1,256,512]{2,1,0:T(8,128)(2,1)S(1)}, bf16[1,256,512]{2,1,0:T(8,128)(2,1)S(1)}, u32[]{:S(2)}, u32[]{:S(2)}) collective-permute-start(bf16[1,256,512]{2,1,0:T(8,128)(2,1)S(1)} %collective-permute-done.10.refs_4_), channel_id=1, source_target_pairs={{1,0},{2,3},{5,4},{6,7},{9,8},{10,11},{13,12},{14,15},{17,16},{18,... | collective-permute-start | bytes 786440 | tf_op jit(solution)/shard_map/ppermute | solution.py:313
  56.5 18.5 %collective-permute-start.14 = (bf16[2,256,512]{2,1,0:T(8,128)(2,1)S(1)}, bf16[2,256,512]{2,1,0:T(8,128)(2,1)S(1)}, u32[]{:S(2)}, u32[]{:S(2)}) collective-permute-start(bf16[2,256,512]{2,1,0:T(8,128)(2,1)S(1)} %collective-permute-done.11.refs_0_.refs_2_.refs_4_), channel_id=1, source_target_pairs={{1,0},{2,3},{5,4},{6,7},{9,8},{10,11},{13,12},{14,15},{17,16},{18,... | collective-permute-start | bytes 1572872 | tf_op jit(solution)/shard_map/ppermute | solution.py:313
  57.8 10.2 %collective-permute-start.15 = (bf16[1,256,512]{2,1,0:T(8,128)(2,1)S(1)}, bf16[1,256,512]{2,1,0:T(8,128)(2,1)S(1)}, u32[]{:S(2)}, u32[]{:S(2)}) collective-permute-start(bf16[1,256,512]{2,1,0:T(8,128)(2,1)S(1)} %get-tuple-element.62), channel_id=1, source_target_pairs={{1,2},{2,1},{5,6},{6,5},{9,10},{10,9},{13,14},{14,13},{17,18},{18,... | collective-permute-start | bytes 786440 | tf_op jit(solution)/shard_map/ppermute | solution.py:310
  63.1 8.2 %collective-permute-start.20 = (bf16[256,512]{1,0:T(8,128)(2,1)S(1)}, bf16[256,512]{1,0:T(8,128)(2,1)S(1)}, u32[]{:S(2)}, u32[]{:S(2)}) collective-permute-start(bf16[256,512]{1,0:T(8,128)(2,1)S(1)} %get-tuple-element.75), channel_id=1, source_target_pairs={{0,16},{4,20},{8,24},{12,28},{16,0},{20,4},{24,8},{28,12},{1,17},{... | collective-permute-start | bytes 786440 | tf_op jit(solution)/shard_map/ppermute | solution.py:307
  65.0 13.6 %collective-permute-start.22 = (bf16[256,512]{1,0:T(8,128)(2,1)S(1)}, bf16[256,512]{1,0:T(8,128)(2,1)S(1)}, u32[]{:S(2)}, u32[]{:S(2)}) collective-permute-start(bf16[256,512]{1,0:T(8,128)(2,1)S(1)} %get-tuple-element.63), channel_id=1, source_target_pairs={{0,8},{4,12},{8,0},{12,4},{16,24},{20,28},{24,16},{28,20},{1,9},{5... | collective-permute-start | bytes 786440 | tf_op jit(solution)/shard_map/ppermute | solution.py:307
  67.9 13.3 %collective-permute-start.16 = (bf16[1,256,512]{2,1,0:T(8,128)(2,1)S(1)}, bf16[1,256,512]{2,1,0:T(8,128)(2,1)S(1)}, u32[]{:S(2)}, u32[]{:S(2)}) collective-permute-start(bf16[1,256,512]{2,1,0:T(8,128)(2,1)S(1)} %collective-permute-done.15.refs_4_), channel_id=1, source_target_pairs={{1,0},{2,3},{5,4},{6,7},{9,8},{10,11},{13,12},{14,15},{17,16},{18,... | collective-permute-start | bytes 786440 | tf_op jit(solution)/shard_map/ppermute | solution.py:313
  76.0 16.9 %collective-permute-start.21 = (bf16[512,512]{1,0:T(8,128)(2,1)S(1)}, bf16[512,512]{1,0:T(8,128)(2,1)S(1)}, u32[]{:S(2)}, u32[]{:S(2)}) collective-permute-start(bf16[512,512]{1,0:T(8,128)(2,1)S(1)} %shard_map.95), channel_id=1, source_target_pairs={{0,8},{4,12},{8,0},{12,4},{16,24},{20,28},{24,16},{28,20},{1,9},{5... | collective-permute-start | bytes 1572872 | tf_op jit(solution)/shard_map/ppermute | solution.py:307
  79.7 13.3 %collective-permute-start.23 = (bf16[512,512]{1,0:T(8,128)(2,1)S(1)}, bf16[512,512]{1,0:T(8,128)(2,1)S(1)}, u32[]{:S(2)}, u32[]{:S(2)}) collective-permute-start(bf16[512,512]{1,0:T(8,128)(2,1)S(1)} %shard_map.96), channel_id=1, source_target_pairs={{0,16},{4,20},{8,24},{12,28},{16,0},{20,4},{24,8},{28,12},{1,17},{... | collective-permute-start | bytes 1572872 | tf_op jit(solution)/shard_map/ppermute | solution.py:307
  82.4 1.6 %collective-permute-start.18 = (bf16[2,128,512]{2,1,0:T(8,128)(2,1)S(1)}, bf16[2,128,512]{2,1,0:T(8,128)(2,1)S(1)}, u32[]{:S(2)}, u32[]{:S(2)}) collective-permute-start(bf16[2,128,512]{2,1,0:T(8,128)(2,1)S(1)} %get-tuple-element.66), channel_id=1, source_target_pairs={{0,4},{4,0},{8,12},{12,8},{16,20},{20,16},{24,28},{28,24},{1,5},{5... | collective-permute-start | bytes 786440 | tf_op jit(solution)/shard_map/ppermute | solution.py:307
  87.4 5.5 %collective-permute-start.19 = (bf16[128,512]{1,0:T(8,128)(2,1)S(1)}, bf16[128,512]{1,0:T(8,128)(2,1)S(1)}, u32[]{:S(2)}, u32[]{:S(2)}) collective-permute-start(bf16[128,512]{1,0:T(8,128)(2,1)S(1)} %get-tuple-element.71), channel_id=1, source_target_pairs={{0,1},{1,0},{2,3},{3,2},{4,5},{5,4},{6,7},{7,6},{8,9},{9,8},{10,11... | collective-permute-start | bytes 393224 | tf_op jit(solution)/shard_map/ppermute | solution.py:307

commit v4 on v3

--- a/solution.py
+++ b/solution.py
@@ -256,9 +256,8 @@
         give[q] = value[rows:].astype(BF16)
 
 
-def term_kernel(c, i, j, late, spans, place, att_own, att_other, partial, *refs):
-    blocks, received = refs[:late], refs[late : late + len(spans)]
-    outs = refs[late + len(spans) :]
+def term_kernel(c, i, j, late, count, place, att_own, att_other, partial, *refs):
+    blocks, received, outs = refs[:late], refs[late : late + count], refs[late + count :]
     total = partial[...].astype(F32)
     if late:
         values = [middle_piece(place, blocks[:4], c), late_piece(place, blocks[4:], i, j)]
@@ -266,18 +265,9 @@
         slots = [place[place.shape[0] - 2], place[place.shape[0] - 1]]
         for slot, value in zip(slots, values):
             total = total + dot(value, attended_rows(att_own, att_other, slot, rows), 0, 0)
-    middle = total.shape[0] // 2
-    sides = [total[:middle], total[middle:]]
-    for ref, span in zip(received, spans):
-        for side in span:
-            part = ref[...] if len(span) == 1 else ref[side * middle : (side + 1) * middle]
-            sides[side] = sides[side] + part.astype(F32)
-    if len(outs) == 2:
-        for out, side in zip(outs, sides):
-            out[...] = side.astype(out.dtype)
-    else:
-        outs[0][:middle] = sides[0].astype(outs[0].dtype)
-        outs[0][middle:] = sides[1].astype(outs[0].dtype)
+    for ref in received:
+        total = total + ref[...].astype(F32)
+    outs[0][...] = total.astype(outs[0].dtype)
 
 
 def tie(value, *others):
@@ -328,7 +318,7 @@
     near = [swap(own_kv, "tensor", 1), swap(taken, "tensor", 1)]
     weights = {0: out_weight}
     for s in reversed(order[:-1]):
-        operand = tie(out_weight, near[0]) if s & (s - 1) else out_weight
+        operand = tie(out_weight, near[0]) if s > 1 else out_weight
         weights[s] = swap(operand, "dp", 2 * s)
     weights = [weights[s] for s in order]
 
@@ -338,8 +328,8 @@
     flops = 4 * length * depth * width // 100
     if tensor == 4:
         middle_own = across(own)
-        direct = [w for s, w in zip(order, weights) if s & (s - 1) == 0]
-        middle_taken = across(tie(taken, middle_own, near[0]))
+        direct = [w for s, w in zip(order, weights) if s < 2]
+        middle_taken = across(taken)
         hold = []
         kv, attended, lse = call(
             forward_kernel,
@@ -362,7 +352,7 @@
             near,
             400 * flops,
         )
-        after = [[middle_taken, attended, *direct], [in_own, weights[0], att_other], []]
+        after = [[middle_taken, attended, *weights[1:]], [in_own, *weights, att_other], []]
         for side in range(len(sizes)):
             second.append(across(tie(relay[side], *after[side], *second[-1:])))
     else:
@@ -424,25 +414,23 @@
 
     def term(c, *others, kind=BF16):
         s = order[c]
-        low, high = s & -s, 1 << s.bit_length() >> 1
-        spans, extra = zip(*received[s]) if received[s] and s else ((), ())
-        shapes = [(depth, width)] if low == high else [(depth // 2, width)] * 2
-        found = call(
-            functools.partial(term_kernel, c, *late[c][:2], len(middle + late[c][2]), spans),
-            [shape(size, kind) for size in shapes],
+        extra = received[s] if s else []
+        (found,) = call(
+            functools.partial(
+                term_kernel, c, *late[c][:2], len(middle + late[c][2]), len(extra)
+            ),
+            [shape((depth, width), kind)],
             [tie(place, *others), attended, att_other, partials[c]]
             + middle
             + late[c][2]
-            + list(extra),
+            + extra,
             300 * flops,
             scalars=1,
         )
-        if len(found) == 2:
-            received[s ^ low].append(((0,), swap(found[0], "dp", 2 * low)))
-            received[s ^ high].append(((1,), swap(found[1], "dp", 2 * high)))
-        elif s:
-            received[0].append(((0, 1), swap(found[0], "dp", 2 * s)))
-        return found[0]
+        if s:
+            low = s & -s
+            received[s ^ low].append(swap(found, "dp", 2 * low))
+        return found
 
     terms = [term(0)]
     total = place
@@ -472,7 +460,7 @@
         finish_kernel,
         [shape((half, length), BF16)] * 2 + [shape((depth, width), BF16)],
         [keep, swap(send, "tensor", 1), term(chips - 1, kind=F32)]
-        + [value for _, value in received[0]],
+        + received[0],
         flops,
     )
     return grad_q, grad_k.T, grad_v.T, grad_weight

time: 94.3 us -> 103 us (1.092)
  waiting for transfers between devices: 37.5 us -> 49.1 us
  starting transfers between devices: 31.3 us -> 28.3 us
    ppermute x14 -> x13, waiting for transfers between devices: 17.6 us -> 31.4 us  [swap(): lax.ppermute(value, axis, [(i, i ^ mask) for i in range(lax.axis_size(axi...]
    ppermute x14 -> x13, starting transfers between devices: 21.3 us -> 18.3 us  [swap(): lax.ppermute(value, axis, [(i, i ^ mask) for i in range(lax.axis_size(axi...]
    ppermute x5, waiting for transfers between devices: 19.9 us -> 17.7 us  [outward(): return lax.ppermute(value, 'tensor', [(1, 0), (2, 3)])]
  transfers between devices with their start and end apart: 24 -> 23, of which waited for: 9 -> 9; matrix products, arithmetic and copies ran while one was open for 0% -> 0% of each run, Pallas kernels for 21% -> 19%
where the time goes in v4:
time: 103 us
  waiting for transfers between devices  49.1 us (48%)
  starting transfers between devices  28.3 us (27%)
  Pallas kernels  21.3 us (21%)
  local copies, waits for them, and re-layouts  2.87 us (3%)
    ppermute x13, waiting for transfers between devices, swap(): lax.ppermute(value, axis, [(i, i ^ mask) for i in range(lax.axis_size(axi...  31.4 us
    pallas_call x14, Pallas kernels, call(): pl.pallas_call(kernel, out_shape=tuple(outs), in_specs=[SMEM] * scalars +...  21.3 us
    ppermute x13, starting transfers between devices, swap(): lax.ppermute(value, axis, [(i, i ^ mask) for i in range(lax.axis_size(axi...  18.3 us
    ppermute x5, waiting for transfers between devices, outward(): return lax.ppermute(value, 'tensor', [(1, 0), (2, 3)])  17.7 us
    ppermute x5, starting transfers between devices, outward(): return lax.ppermute(value, 'tensor', [(1, 0), (2, 3)])  6.62 us
    ppermute x5, starting transfers between devices, across(): return lax.ppermute(value, 'tensor', [(1, 2), (2, 1)])  3.39 us
    unnamed x10, local copies, waits for them, and re-layouts  2.78 us
  transfers between devices with their start and end apart: 23, of which 9 were waited for; matrix products, arithmetic and copies ran while one was open for 0% of the time, Pallas kernels for 19%

profile of v4, /device:TPU:0, one launch (start us, length us, event | category | flops | bytes accessed | tf_op | source)
XLA Modules:
  0.0 102.6 jit_solution(6932964071989242374)
XLA Ops:
  1.5 1.2 %copy-done.2 = bf16[128,4096]{1,0:T(8,128)(2,1)S(1)} copy-done((bf16[128,4096]{1,0:T(8,128)(2,1)S(1)}, bf16[128,4096]{1,0:T(8,128)(2,1)}, u32[]{:S(2)}) %copy-start.2) | copy-done | bytes 1048600
  4.7 2.6 %collective-permute-start = (bf16[640,512]{1,0:T(8,128)(2,1)S(1)}, bf16[640,512]{1,0:T(8,128)(2,1)S(1)}, u32[]{:S(2)}, u32[]{:S(2)}) collective-permute-start(bf16[640,512]{1,0:T(8,128)(2,1)S(1)} %get-tuple-element.39.refs_0_), channel_id=1, source_target_pairs={{0,1},{1,0},{2,3},{3,2},{4,5},{5,4},{6,7},{7,6},{8,9},{9,8},{10,11... | collective-permute-start | bytes 1966088 | tf_op jit(solution)/shard_map/ppermute | solution.py:297
  8.1 1.6 %collective-permute-start.6 = (bf16[512,512]{1,0:T(8,128)(2,1)S(1)}, bf16[512,512]{1,0:T(8,128)(2,1)S(1)}, u32[]{:S(2)}, u32[]{:S(2)}) collective-permute-start(bf16[512,512]{1,0:T(8,128)(2,1)S(1)} %copy-done.1), channel_id=1, source_target_pairs={{0,8},{4,12},{8,0},{12,4},{16,24},{20,28},{24,16},{28,20},{1,9},{5... | collective-permute-start | bytes 1572872 | tf_op jit(solution)/shard_map/ppermute | solution.py:297
  9.6 4.4 %collective-permute-start.2 = (bf16[4,128,512]{2,1,0:T(8,128)(2,1)S(1)}, bf16[4,128,512]{2,1,0:T(8,128)(2,1)S(1)}, u32[]{:S(2)}, u32[]{:S(2)}) collective-permute-start(bf16[4,128,512]{2,1,0:T(8,128)(2,1)S(1)} %collective-permute-done.1.refs_1_), channel_id=1, source_target_pairs={{0,1},{1,0},{2,3},{3,2},{4,5},{5,4},{6,7},{7,6},{8,9},{9,8},{10,11... | collective-permute-start | bytes 1572872 | tf_op jit(solution)/shard_map/ppermute | solution.py:297
  14.7 8.3 %collective-permute-done.near.first.refs_2_ = bf16[640,512]{1,0:T(8,128)(2,1)S(1)} collective-permute-done((bf16[640,512]{1,0:T(8,128)(2,1)S(1)}, bf16[640,512]{1,0:T(8,128)(2,1)S(1)}, u32[]{:S(2)}, u32[]{:S(2)}) %collective-permute-start) | collective-permute-done | bytes 655392 | tf_op jit(solution)/shard_map/ppermute | solution.py:297
  23.0 1.9 %collective-permute-start.7 = (bf16[512,512]{1,0:T(8,128)(2,1)S(1)}, bf16[512,512]{1,0:T(8,128)(2,1)S(1)}, u32[]{:S(2)}, u32[]{:S(2)}) collective-permute-start(bf16[512,512]{1,0:T(8,128)(2,1)S(1)} %copy-done.1), channel_id=1, source_target_pairs={{0,16},{4,20},{8,24},{12,28},{16,0},{20,4},{24,8},{28,12},{1,17},{... | collective-permute-start | bytes 1572872 | tf_op jit(solution)/shard_map/ppermute | solution.py:297
  24.8 1.3 %collective-permute-start.4 = (bf16[4,128,512]{2,1,0:T(8,128)(2,1)S(1)}, bf16[4,128,512]{2,1,0:T(8,128)(2,1)S(1)}, u32[]{:S(2)}, u32[]{:S(2)}) collective-permute-start(bf16[4,128,512]{2,1,0:T(8,128)(2,1)S(1)} %collective-permute-done.3.refs_0_), channel_id=1, source_target_pairs={{1,0},{2,3},{5,4},{6,7},{9,8},{10,11},{13,12},{14,15},{17,16},{18,... | collective-permute-start | bytes 1572872 | tf_op jit(solution)/shard_map/ppermute | solution.py:303
  26.1 4.2 %shard_map.85 = (bf16[2,128,512]{2,1,0:T(8,128)(2,1)S(1)}, bf16[512,512]{1,0:T(8,128)(2,1)S(1)}, f32[512,128]{1,0:T(8,128)S(1)}) custom-call(s32[8]{0:T(128)S(1)} %stack.32.place, bf16[512,512]{1,0:T(8,128)(2,1)S(1)} %copy-done, bf16[64,512]{1,0:T(8,128)(2,1)S(1)} %bitcast.12, bf16[64,512]{1,0:T(8,128)(2,1)S(1)} %bitcast.14, ...), custom_call_target="tpu_custom_call" | custom-call | flops 5368709 | bytes 23593 | tf_op jit(solution)/shard_map/pallas_call | solution.py:25
  30.3 1.5 %collective-permute-start.5 = (bf16[512,512]{1,0:T(8,128)(2,1)S(1)}, bf16[512,512]{1,0:T(8,128)(2,1)S(1)}, u32[]{:S(2)}, u32[]{:S(2)}) collective-permute-start(bf16[512,512]{1,0:T(8,128)(2,1)S(1)} %copy-done.1), channel_id=1, source_target_pairs={{0,24},{4,28},{8,16},{12,20},{16,8},{20,12},{24,0},{28,4},{1,25},{... | collective-permute-start | bytes 1572872 | tf_op jit(solution)/shard_map/ppermute | solution.py:297
  31.8 2.3 %collective-permute-done.2.second.refs_3_ = bf16[4,128,512]{2,1,0:T(8,128)(2,1)S(1)} collective-permute-done((bf16[4,128,512]{2,1,0:T(8,128)(2,1)S(1)}, bf16[4,128,512]{2,1,0:T(8,128)(2,1)S(1)}, u32[]{:S(2)}, u32[]{:S(2)}) %collective-permute-start.2) | collective-permute-done | bytes 524320 | tf_op jit(solution)/shard_map/ppermute | solution.py:297
  34.3 13.3 %collective-permute-done.7.refs_6_.refs_8_.refs_7_ = bf16[512,512]{1,0:T(8,128)(2,1)S(1)} collective-permute-done((bf16[512,512]{1,0:T(8,128)(2,1)S(1)}, bf16[512,512]{1,0:T(8,128)(2,1)S(1)}, u32[]{:S(2)}, u32[]{:S(2)}) %collective-permute-start.7) | collective-permute-done | bytes 524320 | tf_op jit(solution)/shard_map/ppermute | solution.py:297
  48.3 1.3 %collective-permute-start.12 = (bf16[4,128,512]{2,1,0:T(8,128)(2,1)S(1)}, bf16[4,128,512]{2,1,0:T(8,128)(2,1)S(1)}, u32[]{:S(2)}, u32[]{:S(2)}) collective-permute-start(bf16[4,128,512]{2,1,0:T(8,128)(2,1)S(1)} %collective-permute-done.9.refs_1_), channel_id=1, source_target_pairs={{1,0},{2,3},{5,4},{6,7},{9,8},{10,11},{13,12},{14,15},{17,16},{18,... | collective-permute-start | bytes 1572872 | tf_op jit(solution)/shard_map/ppermute | solution.py:303
  50.3 1.8 %shard_map.87 = (f32[2,128,512]{2,1,0:T(8,128)S(1)}, bf16[2,128,512]{2,1,0:T(8,128)(2,1)S(1)}) custom-call(s32[8]{0:T(128)S(1)} %stack.32.place, bf16[640,512]{1,0:T(8,128)(2,1)S(1)} %get-tuple-element.39.refs_0_, bf16[4,128,512]{2,1,0:T(8,128)(2,1)S(1)} %collective-permute-done.1.refs_1_, bf16[640,512]{1,0:T(8,128)(2,1)S(1)} %collective-permute-done.near.first.refs_2_, ...), custom_call_target="tpu_custom_call" | custom-call | flops 1610612736 | bytes 52429 | tf_op jit(solution)/shard_map/pallas_call | solution.py:25
  52.2 1.3 %collective-permute-start.17 = (bf16[1,256,512]{2,1,0:T(8,128)(2,1)S(1)}, bf16[1,256,512]{2,1,0:T(8,128)(2,1)S(1)}, u32[]{:S(2)}, u32[]{:S(2)}) collective-permute-start(bf16[1,256,512]{2,1,0:T(8,128)(2,1)S(1)} %collective-permute-done.10.refs_4_), channel_id=1, source_target_pairs={{1,0},{2,3},{5,4},{6,7},{9,8},{10,11},{13,12},{14,15},{17,16},{18,... | collective-permute-start | bytes 786440 | tf_op jit(solution)/shard_map/ppermute | solution.py:303
  53.5 1.8 %shard_map.88 = (bf16[512,512]{1,0:T(8,128)(2,1)S(1)}, bf16[512,512]{1,0:T(8,128)(2,1)S(1)}, bf16[512,512]{1,0:T(8,128)(2,1)S(1)}, bf16[512,512]{1,0:T(8,128)(2,1)S(1)}) custom-call(s32[8]{0:T(128)S(1)} %stack.32.place, bf16[512,512]{1,0:T(8,128)(2,1)S(1)} %get-tuple-element.46.att_own, bf16[512,512]{1,0:T(8,128)(2,1)S(1)} %collective-permute-done.8.att_other, ...), custom_call_target="tpu_custom_call" | custom-call | flops 5368709 | bytes 55050 | tf_op jit(solution)/shard_map/pallas_call | solution.py:25
  55.3 1.8 %shard_map.89 = (bf16[512,512]{1,0:T(8,128)(2,1)S(1)}, f32[128,512]{1,0:T(8,128)S(1)}, f32[128,512]{1,0:T(8,128)S(1)}) custom-call(s32[8]{0:T(128)S(1)} %stack.32.place, bf16[512,512]{1,0:T(8,128)(2,1)S(1)} %copy-done, bf16[2,128,512]{2,1,0:T(8,128)(2,1)S(1)} %get-tuple-element.40.kv, f32[512,128]{1,0:T(8,128)S(1)} %get-tuple-element.41.lse, ...), custom_call_target="tpu_custom_call" | custom-call | flops 5368709 | bytes 28836 | tf_op jit(solution)/shard_map/pallas_call | solution.py:25
  57.2 5.7 %collective-permute-done.12.refs_3_ = bf16[4,128,512]{2,1,0:T(8,128)(2,1)S(1)} collective-permute-done((bf16[4,128,512]{2,1,0:T(8,128)(2,1)S(1)}, bf16[4,128,512]{2,1,0:T(8,128)(2,1)S(1)}, u32[]{:S(2)}, u32[]{:S(2)}) %collective-permute-start.12) | collective-permute-done | bytes 524320 | tf_op jit(solution)/shard_map/ppermute | solution.py:303
  62.9 1.3 %collective-permute-start.14 = (bf16[2,256,512]{2,1,0:T(8,128)(2,1)S(1)}, bf16[2,256,512]{2,1,0:T(8,128)(2,1)S(1)}, u32[]{:S(2)}, u32[]{:S(2)}) collective-permute-start(bf16[2,256,512]{2,1,0:T(8,128)(2,1)S(1)} %collective-permute-done.11.refs_0_.refs_2_.refs_4_), channel_id=1, source_target_pairs={{1,0},{2,3},{5,4},{6,7},{9,8},{10,11},{13,12},{14,15},{17,16},{18,... | collective-permute-start | bytes 1572872 | tf_op jit(solution)/shard_map/ppermute | solution.py:303
  64.2 7.0 %collective-permute-done.17.refs_5_ = bf16[1,256,512]{2,1,0:T(8,128)(2,1)S(1)} collective-permute-done((bf16[1,256,512]{2,1,0:T(8,128)(2,1)S(1)}, bf16[1,256,512]{2,1,0:T(8,128)(2,1)S(1)}, u32[]{:S(2)}, u32[]{:S(2)}) %collective-permute-start.17) | collective-permute-done | bytes 262176 | tf_op jit(solution)/shard_map/ppermute | solution.py:303
  72.2 1.6 %collective-permute-start.21 = (bf16[512,512]{1,0:T(8,128)(2,1)S(1)}, bf16[512,512]{1,0:T(8,128)(2,1)S(1)}, u32[]{:S(2)}, u32[]{:S(2)}) collective-permute-start(bf16[512,512]{1,0:T(8,128)(2,1)S(1)} %shard_map.90), channel_id=1, source_target_pairs={{0,8},{4,12},{8,0},{12,4},{16,24},{20,28},{24,16},{28,20},{1,9},{5... | collective-permute-start | bytes 1572872 | tf_op jit(solution)/shard_map/ppermute | solution.py:297
  74.5 1.4 %shard_map.91.refs_9_ = f32[2,256,512]{2,1,0:T(8,128)S(1)} custom-call(s32[8]{0:T(128)S(1)} %stack.32.place, bf16[4,128,512]{2,1,0:T(8,128)(2,1)S(1)} %collective-permute-done.3.refs_0_, bf16[4,128,512]{2,1,0:T(8,128)(2,1)S(1)} %collective-permute-done.9.refs_1_, bf16[4,128,512]{2,1,0:T(8,128)(2,1)S(1)} %collective-permute-done.4.refs_2_, ...), custom_call_target="tpu_custom_call" | custom-call | flops 5368709 | bytes 57672 | tf_op jit(solution)/shard_map/pallas_call | solution.py:25
  75.9 1.5 %collective-permute-start.16 = (bf16[1,256,512]{2,1,0:T(8,128)(2,1)S(1)}, bf16[1,256,512]{2,1,0:T(8,128)(2,1)S(1)}, u32[]{:S(2)}, u32[]{:S(2)}) collective-permute-start(bf16[1,256,512]{2,1,0:T(8,128)(2,1)S(1)} %collective-permute-done.15.refs_4_), channel_id=1, source_target_pairs={{1,0},{2,3},{5,4},{6,7},{9,8},{10,11},{13,12},{14,15},{17,16},{18,... | collective-permute-start | bytes 786440 | tf_op jit(solution)/shard_map/ppermute | solution.py:303
  77.3 4.9 %collective-permute-done.14.refs_1_.refs_3_.refs_5_ = bf16[2,256,512]{2,1,0:T(8,128)(2,1)S(1)} collective-permute-done((bf16[2,256,512]{2,1,0:T(8,128)(2,1)S(1)}, bf16[2,256,512]{2,1,0:T(8,128)(2,1)S(1)}, u32[]{:S(2)}, u32[]{:S(2)}) %collective-permute-start.14) | collective-permute-done | bytes 524320 | tf_op jit(solution)/shard_map/ppermute | solution.py:303
  82.3 1.0 shard_map.95
  83.3 2.4 %collective-permute-start.20 = (bf16[512,512]{1,0:T(8,128)(2,1)S(1)}, bf16[512,512]{1,0:T(8,128)(2,1)S(1)}, u32[]{:S(2)}, u32[]{:S(2)}) collective-permute-start(bf16[512,512]{1,0:T(8,128)(2,1)S(1)} %shard_map.95), channel_id=1, source_target_pairs={{0,8},{4,12},{8,0},{12,4},{16,24},{20,28},{24,16},{28,20},{1,9},{5... | collective-permute-start | bytes 1572872 | tf_op jit(solution)/shard_map/ppermute | solution.py:297
  85.7 1.4 %collective-permute-done.21.refs_6_ = bf16[512,512]{1,0:T(8,128)(2,1)S(1)} collective-permute-done((bf16[512,512]{1,0:T(8,128)(2,1)S(1)}, bf16[512,512]{1,0:T(8,128)(2,1)S(1)}, u32[]{:S(2)}, u32[]{:S(2)}) %collective-permute-start.21) | collective-permute-done | bytes 524320 | tf_op jit(solution)/shard_map/ppermute | solution.py:297
  87.1 1.0 %shard_map.96 = bf16[512,512]{1,0:T(8,128)(2,1)S(1)} custom-call(s32[8]{0:T(128)S(1)} %stack.32.place, bf16[512,512]{1,0:T(8,128)(2,1)S(1)} %get-tuple-element.46.att_own, bf16[512,512]{1,0:T(8,128)(2,1)S(1)} %collective-permute-done.8.att_other, bf16[512,512]{1,0:T(8,128)(2,1)S(1)} %get-tuple-element.70.partial, ...), custom_call_target="tpu_custom_call" | custom-call | flops 1610612736 | bytes 57672 | tf_op jit(solution)/shard_map/pallas_call | solution.py:25
  88.2 1.7 %collective-permute-start.22 = (bf16[512,512]{1,0:T(8,128)(2,1)S(1)}, bf16[512,512]{1,0:T(8,128)(2,1)S(1)}, u32[]{:S(2)}, u32[]{:S(2)}) collective-permute-start(bf16[512,512]{1,0:T(8,128)(2,1)S(1)} %shard_map.96), channel_id=1, source_target_pairs={{0,16},{4,20},{8,24},{12,28},{16,0},{20,4},{24,8},{28,12},{1,17},{... | collective-permute-start | bytes 1572872 | tf_op jit(solution)/shard_map/ppermute | solution.py:297
  89.9 1.1 %shard_map.92 = (f32[2,128,512]{2,1,0:T(8,128)S(1)}, bf16[2,128,512]{2,1,0:T(8,128)(2,1)S(1)}) custom-call(s32[8]{0:T(128)S(1)} %stack.32.place, bf16[2,256,512]{2,1,0:T(8,128)(2,1)S(1)} %collective-permute-done.11.refs_0_.refs_2_.refs_4_, bf16[2,256,512]{2,1,0:T(8,128)(2,1)S(1)} %collective-permute-done.14.refs_1_.refs_3_.refs_5_, ...), custom_call_target="tpu_custom_call" | custom-call | flops 5368709 | bytes 60293 | tf_op jit(solution)/shard_map/pallas_call | solution.py:25
  91.1 1.5 %collective-permute-done.18.grad_other = bf16[2,128,512]{2,1,0:T(8,128)(2,1)S(1)} collective-permute-done((bf16[2,128,512]{2,1,0:T(8,128)(2,1)S(1)}, bf16[2,128,512]{2,1,0:T(8,128)(2,1)S(1)}, u32[]{:S(2)}, u32[]{:S(2)}) %collective-permute-start.18) | collective-permute-done | bytes 262176 | tf_op jit(solution)/shard_map/ppermute | solution.py:297
  92.6 3.4 %shard_map.93 = (bf16[512,512]{1,0:T(8,128)(2,1)}, f32[128,512]{1,0:T(8,128)S(1)}, bf16[128,512]{1,0:T(8,128)(2,1)S(1)}) custom-call(s32[8]{0:T(128)S(1)} %stack.32.place, bf16[512,512]{1,0:T(8,128)(2,1)S(1)} %copy-done, bf16[2,128,512]{2,1,0:T(8,128)(2,1)S(1)} %get-tuple-element.40.kv, f32[512,128]{1,0:T(8,128)S(1)} %get-tuple-element.41.lse, ...), custom_call_target="tpu_custom_call" | custom-call | flops 5368709 | bytes 38011 | tf_op jit(solution)/shard_map/pallas_call | solution.py:25
  97.1 4.5 %collective-permute-done.19.other = bf16[128,512]{1,0:T(8,128)(2,1)S(1)} collective-permute-done((bf16[128,512]{1,0:T(8,128)(2,1)S(1)}, bf16[128,512]{1,0:T(8,128)(2,1)S(1)}, u32[]{:S(2)}, u32[]{:S(2)}) %collective-permute-start.19) | collective-permute-done | bytes 131104 | tf_op jit(solution)/shard_map/ppermute | solution.py:297
  (39 shorter events, 9.5 us)
Async XLA Ops:
  0.6 0.8 copy-start.3
  1.5 1.2 %copy-start.2 = (bf16[128,4096]{1,0:T(8,128)(2,1)S(1)}, bf16[128,4096]{1,0:T(8,128)(2,1)}, u32[]{:S(2)}) copy-start(bf16[128,4096]{1,0:T(8,128)(2,1)} %grad.1) | copy-start | bytes 3145732
  2.7 0.8 copy-start.4
  3.5 4.5 %copy-start.1 = (bf16[512,512]{1,0:T(8,128)(2,1)S(1)}, bf16[512,512]{1,0:T(8,128)(2,1)}, u32[]{:S(2)}) copy-start(bf16[512,512]{1,0:T(8,128)(2,1)} %refs_8_.1) | copy-start | bytes 1572868
  3.5 22.6 %copy-start = (bf16[512,512]{1,0:T(8,128)(2,1)S(1)}, bf16[512,512]{1,0:T(8,128)(2,1)}, u32[]{:S(2)}) copy-start(bf16[512,512]{1,0:T(8,128)(2,1)} %queries.4) | copy-start | bytes 1572868
  4.2 5.4 %collective-permute-start.1 = (bf16[4,128,512]{2,1,0:T(8,128)(2,1)S(1)}, bf16[4,128,512]{2,1,0:T(8,128)(2,1)S(1)}, u32[]{:S(2)}, u32[]{:S(2)}) collective-permute-start(bf16[4,128,512]{2,1,0:T(8,128)(2,1)S(1)} %get-tuple-element.42), channel_id=1, source_target_pairs={{0,4},{4,0},{8,12},{12,8},{16,20},{20,16},{24,28},{28,24},{1,5},{5... | collective-permute-start | bytes 1572872 | tf_op jit(solution)/shard_map/ppermute | solution.py:297
  4.7 18.2 %collective-permute-start = (bf16[640,512]{1,0:T(8,128)(2,1)S(1)}, bf16[640,512]{1,0:T(8,128)(2,1)S(1)}, u32[]{:S(2)}, u32[]{:S(2)}) collective-permute-start(bf16[640,512]{1,0:T(8,128)(2,1)S(1)} %get-tuple-element.39.refs_0_), channel_id=1, source_target_pairs={{0,1},{1,0},{2,3},{3,2},{4,5},{5,4},{6,7},{7,6},{8,9},{9,8},{10,11... | collective-permute-start | bytes 1966088 | tf_op jit(solution)/shard_map/ppermute | solution.py:297
  7.4 17.5 %collective-permute-start.3 = (bf16[4,128,512]{2,1,0:T(8,128)(2,1)S(1)}, bf16[4,128,512]{2,1,0:T(8,128)(2,1)S(1)}, u32[]{:S(2)}, u32[]{:S(2)}) collective-permute-start(bf16[4,128,512]{2,1,0:T(8,128)(2,1)S(1)} %get-tuple-element.44), channel_id=1, source_target_pairs={{1,2},{2,1},{5,6},{6,5},{9,10},{10,9},{13,14},{14,13},{17,18},{18,... | collective-permute-start | bytes 1572872 | tf_op jit(solution)/shard_map/ppermute | solution.py:300
  8.1 22.3 %collective-permute-start.6 = (bf16[512,512]{1,0:T(8,128)(2,1)S(1)}, bf16[512,512]{1,0:T(8,128)(2,1)S(1)}, u32[]{:S(2)}, u32[]{:S(2)}) collective-permute-start(bf16[512,512]{1,0:T(8,128)(2,1)S(1)} %copy-done.1), channel_id=1, source_target_pairs={{0,8},{4,12},{8,0},{12,4},{16,24},{20,28},{24,16},{28,20},{1,9},{5... | collective-permute-start | bytes 1572872 | tf_op jit(solution)/shard_map/ppermute | solution.py:297
  9.6 24.6 %collective-permute-start.2 = (bf16[4,128,512]{2,1,0:T(8,128)(2,1)S(1)}, bf16[4,128,512]{2,1,0:T(8,128)(2,1)S(1)}, u32[]{:S(2)}, u32[]{:S(2)}) collective-permute-start(bf16[4,128,512]{2,1,0:T(8,128)(2,1)S(1)} %collective-permute-done.1.refs_1_), channel_id=1, source_target_pairs={{0,1},{1,0},{2,3},{3,2},{4,5},{5,4},{6,7},{7,6},{8,9},{9,8},{10,11... | collective-permute-start | bytes 1572872 | tf_op jit(solution)/shard_map/ppermute | solution.py:297
  14.0 20.3 %collective-permute-start.9 = (bf16[4,128,512]{2,1,0:T(8,128)(2,1)S(1)}, bf16[4,128,512]{2,1,0:T(8,128)(2,1)S(1)}, u32[]{:S(2)}, u32[]{:S(2)}) collective-permute-start(bf16[4,128,512]{2,1,0:T(8,128)(2,1)S(1)} %collective-permute-done.1.refs_1_), channel_id=1, source_target_pairs={{1,2},{2,1},{5,6},{6,5},{9,10},{10,9},{13,14},{14,13},{17,18},{18,... | collective-permute-start | bytes 1572872 | tf_op jit(solution)/shard_map/ppermute | solution.py:300
  23.0 24.7 %collective-permute-start.7 = (bf16[512,512]{1,0:T(8,128)(2,1)S(1)}, bf16[512,512]{1,0:T(8,128)(2,1)S(1)}, u32[]{:S(2)}, u32[]{:S(2)}) collective-permute-start(bf16[512,512]{1,0:T(8,128)(2,1)S(1)} %copy-done.1), channel_id=1, source_target_pairs={{0,16},{4,20},{8,24},{12,28},{16,0},{20,4},{24,8},{28,12},{1,17},{... | collective-permute-start | bytes 1572872 | tf_op jit(solution)/shard_map/ppermute | solution.py:297
  24.8 24.7 %collective-permute-start.4 = (bf16[4,128,512]{2,1,0:T(8,128)(2,1)S(1)}, bf16[4,128,512]{2,1,0:T(8,128)(2,1)S(1)}, u32[]{:S(2)}, u32[]{:S(2)}) collective-permute-start(bf16[4,128,512]{2,1,0:T(8,128)(2,1)S(1)} %collective-permute-done.3.refs_0_), channel_id=1, source_target_pairs={{1,0},{2,3},{5,4},{6,7},{9,8},{10,11},{13,12},{14,15},{17,16},{18,... | collective-permute-start | bytes 1572872 | tf_op jit(solution)/shard_map/ppermute | solution.py:303
  30.3 19.2 %collective-permute-start.5 = (bf16[512,512]{1,0:T(8,128)(2,1)S(1)}, bf16[512,512]{1,0:T(8,128)(2,1)S(1)}, u32[]{:S(2)}, u32[]{:S(2)}) collective-permute-start(bf16[512,512]{1,0:T(8,128)(2,1)S(1)} %copy-done.1), channel_id=1, source_target_pairs={{0,24},{4,28},{8,16},{12,20},{16,8},{20,12},{24,0},{28,4},{1,25},{... | collective-permute-start | bytes 1572872 | tf_op jit(solution)/shard_map/ppermute | solution.py:297
  34.2 15.4 %collective-permute-start.8 = (bf16[512,512]{1,0:T(8,128)(2,1)S(1)}, bf16[512,512]{1,0:T(8,128)(2,1)S(1)}, u32[]{:S(2)}, u32[]{:S(2)}) collective-permute-start(bf16[512,512]{1,0:T(8,128)(2,1)S(1)} %get-tuple-element.46.att_own), channel_id=1, source_target_pairs={{0,4},{4,0},{8,12},{12,8},{16,20},{20,16},{24,28},{28,24},{1,5},{5... | collective-permute-start | bytes 1572872 | tf_op jit(solution)/shard_map/ppermute | solution.py:297
  47.6 2.0 %collective-permute-start.10 = (bf16[1,256,512]{2,1,0:T(8,128)(2,1)S(1)}, bf16[1,256,512]{2,1,0:T(8,128)(2,1)S(1)}, u32[]{:S(2)}, u32[]{:S(2)}) collective-permute-start(bf16[1,256,512]{2,1,0:T(8,128)(2,1)S(1)} %get-tuple-element.48), channel_id=1, source_target_pairs={{1,2},{2,1},{5,6},{6,5},{9,10},{10,9},{13,14},{14,13},{17,18},{18,... | collective-permute-start | bytes 786440 | tf_op jit(solution)/shard_map/ppermute | solution.py:300
  48.3 14.6 %collective-permute-start.12 = (bf16[4,128,512]{2,1,0:T(8,128)(2,1)S(1)}, bf16[4,128,512]{2,1,0:T(8,128)(2,1)S(1)}, u32[]{:S(2)}, u32[]{:S(2)}) collective-permute-start(bf16[4,128,512]{2,1,0:T(8,128)(2,1)S(1)} %collective-permute-done.9.refs_1_), channel_id=1, source_target_pairs={{1,0},{2,3},{5,4},{6,7},{9,8},{10,11},{13,12},{14,15},{17,16},{18,... | collective-permute-start | bytes 1572872 | tf_op jit(solution)/shard_map/ppermute | solution.py:303
  49.6 13.3 %collective-permute-start.11 = (bf16[2,256,512]{2,1,0:T(8,128)(2,1)S(1)}, bf16[2,256,512]{2,1,0:T(8,128)(2,1)S(1)}, u32[]{:S(2)}, u32[]{:S(2)}) collective-permute-start(bf16[2,256,512]{2,1,0:T(8,128)(2,1)S(1)} %get-tuple-element.49), channel_id=1, source_target_pairs={{1,2},{2,1},{5,6},{6,5},{9,10},{10,9},{13,14},{14,13},{17,18},{18,... | collective-permute-start | bytes 1572872 | tf_op jit(solution)/shard_map/ppermute | solution.py:300
  52.1 3.2 %collective-permute-start.13 = (bf16[2,128,512]{2,1,0:T(8,128)(2,1)S(1)}, bf16[2,128,512]{2,1,0:T(8,128)(2,1)S(1)}, u32[]{:S(2)}, u32[]{:S(2)}) collective-permute-start(bf16[2,128,512]{2,1,0:T(8,128)(2,1)S(1)} %get-tuple-element.51), channel_id=1, source_target_pairs={{0,4},{4,0},{8,12},{12,8},{16,20},{20,16},{24,28},{28,24},{1,5},{5... | collective-permute-start | bytes 786440 | tf_op jit(solution)/shard_map/ppermute | solution.py:297
  52.2 19.0 %collective-permute-start.17 = (bf16[1,256,512]{2,1,0:T(8,128)(2,1)S(1)}, bf16[1,256,512]{2,1,0:T(8,128)(2,1)S(1)}, u32[]{:S(2)}, u32[]{:S(2)}) collective-permute-start(bf16[1,256,512]{2,1,0:T(8,128)(2,1)S(1)} %collective-permute-done.10.refs_4_), channel_id=1, source_target_pairs={{1,0},{2,3},{5,4},{6,7},{9,8},{10,11},{13,12},{14,15},{17,16},{18,... | collective-permute-start | bytes 786440 | tf_op jit(solution)/shard_map/ppermute | solution.py:303
  62.9 19.3 %collective-permute-start.14 = (bf16[2,256,512]{2,1,0:T(8,128)(2,1)S(1)}, bf16[2,256,512]{2,1,0:T(8,128)(2,1)S(1)}, u32[]{:S(2)}, u32[]{:S(2)}) collective-permute-start(bf16[2,256,512]{2,1,0:T(8,128)(2,1)S(1)} %collective-permute-done.11.refs_0_.refs_2_.refs_4_), channel_id=1, source_target_pairs={{1,0},{2,3},{5,4},{6,7},{9,8},{10,11},{13,12},{14,15},{17,16},{18,... | collective-permute-start | bytes 1572872 | tf_op jit(solution)/shard_map/ppermute | solution.py:303
  72.2 14.9 %collective-permute-start.21 = (bf16[512,512]{1,0:T(8,128)(2,1)S(1)}, bf16[512,512]{1,0:T(8,128)(2,1)S(1)}, u32[]{:S(2)}, u32[]{:S(2)}) collective-permute-start(bf16[512,512]{1,0:T(8,128)(2,1)S(1)} %shard_map.90), channel_id=1, source_target_pairs={{0,8},{4,12},{8,0},{12,4},{16,24},{20,28},{24,16},{28,20},{1,9},{5... | collective-permute-start | bytes 1572872 | tf_op jit(solution)/shard_map/ppermute | solution.py:297
  73.8 2.1 %collective-permute-start.15 = (bf16[1,256,512]{2,1,0:T(8,128)(2,1)S(1)}, bf16[1,256,512]{2,1,0:T(8,128)(2,1)S(1)}, u32[]{:S(2)}, u32[]{:S(2)}) collective-permute-start(bf16[1,256,512]{2,1,0:T(8,128)(2,1)S(1)} %get-tuple-element.58), channel_id=1, source_target_pairs={{1,2},{2,1},{5,6},{6,5},{9,10},{10,9},{13,14},{14,13},{17,18},{18,... | collective-permute-start | bytes 786440 | tf_op jit(solution)/shard_map/ppermute | solution.py:300
  75.9 14.0 %collective-permute-start.16 = (bf16[1,256,512]{2,1,0:T(8,128)(2,1)S(1)}, bf16[1,256,512]{2,1,0:T(8,128)(2,1)S(1)}, u32[]{:S(2)}, u32[]{:S(2)}) collective-permute-start(bf16[1,256,512]{2,1,0:T(8,128)(2,1)S(1)} %collective-permute-done.15.refs_4_), channel_id=1, source_target_pairs={{1,0},{2,3},{5,4},{6,7},{9,8},{10,11},{13,12},{14,15},{17,16},{18,... | collective-permute-start | bytes 786440 | tf_op jit(solution)/shard_map/ppermute | solution.py:303
  83.3 18.3 %collective-permute-start.20 = (bf16[512,512]{1,0:T(8,128)(2,1)S(1)}, bf16[512,512]{1,0:T(8,128)(2,1)S(1)}, u32[]{:S(2)}, u32[]{:S(2)}) collective-permute-start(bf16[512,512]{1,0:T(8,128)(2,1)S(1)} %shard_map.95), channel_id=1, source_target_pairs={{0,8},{4,12},{8,0},{12,4},{16,24},{20,28},{24,16},{28,20},{1,9},{5... | collective-permute-start | bytes 1572872 | tf_op jit(solution)/shard_map/ppermute | solution.py:297
  88.2 13.4 %collective-permute-start.22 = (bf16[512,512]{1,0:T(8,128)(2,1)S(1)}, bf16[512,512]{1,0:T(8,128)(2,1)S(1)}, u32[]{:S(2)}, u32[]{:S(2)}) collective-permute-start(bf16[512,512]{1,0:T(8,128)(2,1)S(1)} %shard_map.96), channel_id=1, source_target_pairs={{0,16},{4,20},{8,24},{12,28},{16,0},{20,4},{24,8},{28,12},{1,17},{... | collective-permute-start | bytes 1572872 | tf_op jit(solution)/shard_map/ppermute | solution.py:297
  91.0 1.6 %collective-permute-start.18 = (bf16[2,128,512]{2,1,0:T(8,128)(2,1)S(1)}, bf16[2,128,512]{2,1,0:T(8,128)(2,1)S(1)}, u32[]{:S(2)}, u32[]{:S(2)}) collective-permute-start(bf16[2,128,512]{2,1,0:T(8,128)(2,1)S(1)} %get-tuple-element.61), channel_id=1, source_target_pairs={{0,4},{4,0},{8,12},{12,8},{16,20},{20,16},{24,28},{28,24},{1,5},{5... | collective-permute-start | bytes 786440 | tf_op jit(solution)/shard_map/ppermute | solution.py:297
  96.0 5.5 %collective-permute-start.19 = (bf16[128,512]{1,0:T(8,128)(2,1)S(1)}, bf16[128,512]{1,0:T(8,128)(2,1)S(1)}, u32[]{:S(2)}, u32[]{:S(2)}) collective-permute-start(bf16[128,512]{1,0:T(8,128)(2,1)S(1)} %get-tuple-element.66), channel_id=1, source_target_pairs={{0,1},{1,0},{2,3},{3,2},{4,5},{5,4},{6,7},{7,6},{8,9},{9,8},{10,11... | collective-permute-start | bytes 393224 | tf_op jit(solution)/shard_map/ppermute | solution.py:297

commit v5 on v4

--- a/solution.py
+++ b/solution.py
@@ -318,7 +318,7 @@
     near = [swap(own_kv, "tensor", 1), swap(taken, "tensor", 1)]
     weights = {0: out_weight}
     for s in reversed(order[:-1]):
-        operand = tie(out_weight, near[0]) if s > 1 else out_weight
+        operand = out_weight if s & (s - 1) else tie(out_weight, near[0])
         weights[s] = swap(operand, "dp", 2 * s)
     weights = [weights[s] for s in order]
 
@@ -328,7 +328,7 @@
     flops = 4 * length * depth * width // 100
     if tensor == 4:
         middle_own = across(own)
-        direct = [w for s, w in zip(order, weights) if s < 2]
+        direct = [w for s, w in zip(order, weights) if s & (s - 1)]
         middle_taken = across(taken)
         hold = []
         kv, attended, lse = call(
@@ -352,7 +352,7 @@
             near,
             400 * flops,
         )
-        after = [[middle_taken, attended, *weights[1:]], [in_own, *weights, att_other], []]
+        after = [[middle_taken, att_other, *direct], [in_own, *weights], []]
         for side in range(len(sizes)):
             second.append(across(tie(relay[side], *after[side], *second[-1:])))
     else:

time: 103 us -> 94.5 us (0.917)
  waiting for transfers between devices: 49.1 us -> 39.1 us
  starting transfers between devices: 28.3 us -> 29.9 us
    ppermute x13, waiting for transfers between devices: 31.4 us -> 19.3 us  [swap(): lax.ppermute(value, axis, [(i, i ^ mask) for i in range(lax.axis_size(axi...]
    ppermute x5, waiting for transfers between devices: 17.7 us -> 19.8 us  [outward(): return lax.ppermute(value, 'tensor', [(1, 0), (2, 3)])]
    ppermute x13, starting transfers between devices: 18.3 us -> 19.9 us  [swap(): lax.ppermute(value, axis, [(i, i ^ mask) for i in range(lax.axis_size(axi...]
  transfers between devices with their start and end apart: 23 -> 23, of which waited for: 9 -> 11; matrix products, arithmetic and copies ran while one was open for 0% -> 0% of each run, Pallas kernels for 19% -> 21%
where the time goes in v5:
time: 94.5 us; the launch traced here: 94.1 us
  waiting for transfers between devices  39.1 us (41%)
  starting transfers between devices  29.9 us (32%)
  Pallas kernels  21.3 us (23%)
  local copies, waits for them, and re-layouts  2.87 us (3%)
    pallas_call x14, Pallas kernels, call(): pl.pallas_call(kernel, out_shape=tuple(outs), in_specs=[SMEM] * scalars +...  21.3 us
    ppermute x13, starting transfers between devices, swap(): lax.ppermute(value, axis, [(i, i ^ mask) for i in range(lax.axis_size(axi...  19.9 us
    ppermute x5, waiting for transfers between devices, outward(): return lax.ppermute(value, 'tensor', [(1, 0), (2, 3)])  19.8 us
    ppermute x13, waiting for transfers between devices, swap(): lax.ppermute(value, axis, [(i, i ^ mask) for i in range(lax.axis_size(axi...  19.3 us
    ppermute x5, starting transfers between devices, outward(): return lax.ppermute(value, 'tensor', [(1, 0), (2, 3)])  6.63 us
    ppermute x5, starting transfers between devices, across(): return lax.ppermute(value, 'tensor', [(1, 2), (2, 1)])  3.39 us
    unnamed x10, local copies, waits for them, and re-layouts  2.78 us
  transfers between devices with their start and end apart: 23, of which 11 were waited for; matrix products, arithmetic and copies ran while one was open for 0% of the time, Pallas kernels for 21%

profile of v5, /device:TPU:0, one launch (start us, length us, event | category | flops | bytes accessed | tf_op | source)
XLA Modules:
  0.0 94.1 jit_solution(14691472746558236566)
XLA Ops:
  1.5 1.2 %copy-done.2 = bf16[128,4096]{1,0:T(8,128)(2,1)S(1)} copy-done((bf16[128,4096]{1,0:T(8,128)(2,1)S(1)}, bf16[128,4096]{1,0:T(8,128)(2,1)}, u32[]{:S(2)}) %copy-start.2) | copy-done | bytes 1048600
  4.7 2.6 %collective-permute-start = (bf16[640,512]{1,0:T(8,128)(2,1)S(1)}, bf16[640,512]{1,0:T(8,128)(2,1)S(1)}, u32[]{:S(2)}, u32[]{:S(2)}) collective-permute-start(bf16[640,512]{1,0:T(8,128)(2,1)S(1)} %get-tuple-element.39.refs_0_), channel_id=1, source_target_pairs={{0,1},{1,0},{2,3},{3,2},{4,5},{5,4},{6,7},{7,6},{8,9},{9,8},{10,11... | collective-permute-start | bytes 1966088 | tf_op jit(solution)/shard_map/ppermute | solution.py:297
  8.1 2.5 %collective-permute-start.5 = (bf16[512,512]{1,0:T(8,128)(2,1)S(1)}, bf16[512,512]{1,0:T(8,128)(2,1)S(1)}, u32[]{:S(2)}, u32[]{:S(2)}) collective-permute-start(bf16[512,512]{1,0:T(8,128)(2,1)S(1)} %copy-done.1), channel_id=1, source_target_pairs={{0,24},{4,28},{8,16},{12,20},{16,8},{20,12},{24,0},{28,4},{1,25},{... | collective-permute-start | bytes 1572872 | tf_op jit(solution)/shard_map/ppermute | solution.py:297
  10.6 4.4 %collective-permute-start.2 = (bf16[4,128,512]{2,1,0:T(8,128)(2,1)S(1)}, bf16[4,128,512]{2,1,0:T(8,128)(2,1)S(1)}, u32[]{:S(2)}, u32[]{:S(2)}) collective-permute-start(bf16[4,128,512]{2,1,0:T(8,128)(2,1)S(1)} %collective-permute-done.1.refs_1_), channel_id=1, source_target_pairs={{0,1},{1,0},{2,3},{3,2},{4,5},{5,4},{6,7},{7,6},{8,9},{9,8},{10,11... | collective-permute-start | bytes 1572872 | tf_op jit(solution)/shard_map/ppermute | solution.py:297
  15.6 7.3 %collective-permute-done.near.first.refs_2_ = bf16[640,512]{1,0:T(8,128)(2,1)S(1)} collective-permute-done((bf16[640,512]{1,0:T(8,128)(2,1)S(1)}, bf16[640,512]{1,0:T(8,128)(2,1)S(1)}, u32[]{:S(2)}, u32[]{:S(2)}) %collective-permute-start) | collective-permute-done | bytes 655392 | tf_op jit(solution)/shard_map/ppermute | solution.py:297
  23.0 4.2 %shard_map.85 = (bf16[2,128,512]{2,1,0:T(8,128)(2,1)S(1)}, bf16[512,512]{1,0:T(8,128)(2,1)S(1)}, f32[512,128]{1,0:T(8,128)S(1)}) custom-call(s32[8]{0:T(128)S(1)} %stack.32.place, bf16[512,512]{1,0:T(8,128)(2,1)S(1)} %copy-done, bf16[64,512]{1,0:T(8,128)(2,1)S(1)} %bitcast.12, bf16[64,512]{1,0:T(8,128)(2,1)S(1)} %bitcast.14, ...), custom_call_target="tpu_custom_call" | custom-call | flops 5368709 | bytes 23593 | tf_op jit(solution)/shard_map/pallas_call | solution.py:25
  27.2 1.3 %collective-permute-start.4 = (bf16[4,128,512]{2,1,0:T(8,128)(2,1)S(1)}, bf16[4,128,512]{2,1,0:T(8,128)(2,1)S(1)}, u32[]{:S(2)}, u32[]{:S(2)}) collective-permute-start(bf16[4,128,512]{2,1,0:T(8,128)(2,1)S(1)} %collective-permute-done.3.refs_0_), channel_id=1, source_target_pairs={{1,0},{2,3},{5,4},{6,7},{9,8},{10,11},{13,12},{14,15},{17,16},{18,... | collective-permute-start | bytes 1572872 | tf_op jit(solution)/shard_map/ppermute | solution.py:303
  28.5 1.9 %collective-permute-start.6 = (bf16[512,512]{1,0:T(8,128)(2,1)S(1)}, bf16[512,512]{1,0:T(8,128)(2,1)S(1)}, u32[]{:S(2)}, u32[]{:S(2)}) collective-permute-start(bf16[512,512]{1,0:T(8,128)(2,1)S(1)} %copy-done.1), channel_id=1, source_target_pairs={{0,8},{4,12},{8,0},{12,4},{16,24},{20,28},{24,16},{28,20},{1,9},{5... | collective-permute-start | bytes 1572872 | tf_op jit(solution)/shard_map/ppermute | solution.py:297
  30.5 3.7 %collective-permute-done.2.second.refs_3_ = bf16[4,128,512]{2,1,0:T(8,128)(2,1)S(1)} collective-permute-done((bf16[4,128,512]{2,1,0:T(8,128)(2,1)S(1)}, bf16[4,128,512]{2,1,0:T(8,128)(2,1)S(1)}, u32[]{:S(2)}, u32[]{:S(2)}) %collective-permute-start.2) | collective-permute-done | bytes 524320 | tf_op jit(solution)/shard_map/ppermute | solution.py:297
  34.2 1.9 %collective-permute-start.7 = (bf16[512,512]{1,0:T(8,128)(2,1)S(1)}, bf16[512,512]{1,0:T(8,128)(2,1)S(1)}, u32[]{:S(2)}, u32[]{:S(2)}) collective-permute-start(bf16[512,512]{1,0:T(8,128)(2,1)S(1)} %copy-done.1), channel_id=1, source_target_pairs={{0,16},{4,20},{8,24},{12,28},{16,0},{20,4},{24,8},{28,12},{1,17},{... | collective-permute-start | bytes 1572872 | tf_op jit(solution)/shard_map/ppermute | solution.py:297
  36.9 1.3 %collective-permute-start.12 = (bf16[4,128,512]{2,1,0:T(8,128)(2,1)S(1)}, bf16[4,128,512]{2,1,0:T(8,128)(2,1)S(1)}, u32[]{:S(2)}, u32[]{:S(2)}) collective-permute-start(bf16[4,128,512]{2,1,0:T(8,128)(2,1)S(1)} %collective-permute-done.8.refs_1_), channel_id=1, source_target_pairs={{1,0},{2,3},{5,4},{6,7},{9,8},{10,11},{13,12},{14,15},{17,16},{18,... | collective-permute-start | bytes 1572872 | tf_op jit(solution)/shard_map/ppermute | solution.py:303
  38.2 7.3 %collective-permute-done.4.refs_2_ = bf16[4,128,512]{2,1,0:T(8,128)(2,1)S(1)} collective-permute-done((bf16[4,128,512]{2,1,0:T(8,128)(2,1)S(1)}, bf16[4,128,512]{2,1,0:T(8,128)(2,1)S(1)}, u32[]{:S(2)}, u32[]{:S(2)}) %collective-permute-start.4) | collective-permute-done | bytes 524320 | tf_op jit(solution)/shard_map/ppermute | solution.py:303
  45.4 2.2 %collective-permute-done.7.refs_6_.refs_8_.refs_7_ = bf16[512,512]{1,0:T(8,128)(2,1)S(1)} collective-permute-done((bf16[512,512]{1,0:T(8,128)(2,1)S(1)}, bf16[512,512]{1,0:T(8,128)(2,1)S(1)}, u32[]{:S(2)}, u32[]{:S(2)}) %collective-permute-start.7) | collective-permute-done | bytes 524320 | tf_op jit(solution)/shard_map/ppermute | solution.py:297
  48.3 1.8 %shard_map.87 = (f32[2,128,512]{2,1,0:T(8,128)S(1)}, bf16[2,128,512]{2,1,0:T(8,128)(2,1)S(1)}) custom-call(s32[8]{0:T(128)S(1)} %stack.32.place, bf16[640,512]{1,0:T(8,128)(2,1)S(1)} %get-tuple-element.39.refs_0_, bf16[4,128,512]{2,1,0:T(8,128)(2,1)S(1)} %collective-permute-done.1.refs_1_, bf16[640,512]{1,0:T(8,128)(2,1)S(1)} %collective-permute-done.near.first.refs_2_, ...), custom_call_target="tpu_custom_call" | custom-call | flops 1610612736 | bytes 52429 | tf_op jit(solution)/shard_map/pallas_call | solution.py:25
  50.2 1.3 %collective-permute-start.17 = (bf16[1,256,512]{2,1,0:T(8,128)(2,1)S(1)}, bf16[1,256,512]{2,1,0:T(8,128)(2,1)S(1)}, u32[]{:S(2)}, u32[]{:S(2)}) collective-permute-start(bf16[1,256,512]{2,1,0:T(8,128)(2,1)S(1)} %collective-permute-done.10.refs_4_), channel_id=1, source_target_pairs={{1,0},{2,3},{5,4},{6,7},{9,8},{10,11},{13,12},{14,15},{17,16},{18,... | collective-permute-start | bytes 786440 | tf_op jit(solution)/shard_map/ppermute | solution.py:303
  51.5 1.8 %shard_map.88 = (bf16[512,512]{1,0:T(8,128)(2,1)S(1)}, bf16[512,512]{1,0:T(8,128)(2,1)S(1)}, bf16[512,512]{1,0:T(8,128)(2,1)S(1)}, bf16[512,512]{1,0:T(8,128)(2,1)S(1)}) custom-call(s32[8]{0:T(128)S(1)} %stack.32.place, bf16[512,512]{1,0:T(8,128)(2,1)S(1)} %get-tuple-element.47.att_own, bf16[512,512]{1,0:T(8,128)(2,1)S(1)} %collective-permute-done.9.att_other, ...), custom_call_target="tpu_custom_call" | custom-call | flops 5368709 | bytes 55050 | tf_op jit(solution)/shard_map/pallas_call | solution.py:25
  53.3 1.8 %shard_map.89 = (bf16[512,512]{1,0:T(8,128)(2,1)S(1)}, f32[128,512]{1,0:T(8,128)S(1)}, f32[128,512]{1,0:T(8,128)S(1)}) custom-call(s32[8]{0:T(128)S(1)} %stack.32.place, bf16[512,512]{1,0:T(8,128)(2,1)S(1)} %copy-done, bf16[2,128,512]{2,1,0:T(8,128)(2,1)S(1)} %get-tuple-element.40.kv, f32[512,128]{1,0:T(8,128)S(1)} %get-tuple-element.41.lse, ...), custom_call_target="tpu_custom_call" | custom-call | flops 5368709 | bytes 28836 | tf_op jit(solution)/shard_map/pallas_call | solution.py:25
  55.1 1.3 %collective-permute-done.12.refs_3_ = bf16[4,128,512]{2,1,0:T(8,128)(2,1)S(1)} collective-permute-done((bf16[4,128,512]{2,1,0:T(8,128)(2,1)S(1)}, bf16[4,128,512]{2,1,0:T(8,128)(2,1)S(1)}, u32[]{:S(2)}, u32[]{:S(2)}) %collective-permute-start.12) | collective-permute-done | bytes 524320 | tf_op jit(solution)/shard_map/ppermute | solution.py:303
  56.4 1.3 %collective-permute-start.14 = (bf16[2,256,512]{2,1,0:T(8,128)(2,1)S(1)}, bf16[2,256,512]{2,1,0:T(8,128)(2,1)S(1)}, u32[]{:S(2)}, u32[]{:S(2)}) collective-permute-start(bf16[2,256,512]{2,1,0:T(8,128)(2,1)S(1)} %collective-permute-done.11.refs_0_.refs_2_.refs_4_), channel_id=1, source_target_pairs={{1,0},{2,3},{5,4},{6,7},{9,8},{10,11},{13,12},{14,15},{17,16},{18,... | collective-permute-start | bytes 1572872 | tf_op jit(solution)/shard_map/ppermute | solution.py:303
  57.7 5.1 %collective-permute-done.17.refs_5_ = bf16[1,256,512]{2,1,0:T(8,128)(2,1)S(1)} collective-permute-done((bf16[1,256,512]{2,1,0:T(8,128)(2,1)S(1)}, bf16[1,256,512]{2,1,0:T(8,128)(2,1)S(1)}, u32[]{:S(2)}, u32[]{:S(2)}) %collective-permute-start.17) | collective-permute-done | bytes 262176 | tf_op jit(solution)/shard_map/ppermute | solution.py:303
  62.8 1.0 %shard_map.90 = bf16[512,512]{1,0:T(8,128)(2,1)S(1)} custom-call(s32[8]{0:T(128)S(1)} %stack.32.place, bf16[512,512]{1,0:T(8,128)(2,1)S(1)} %get-tuple-element.47.att_own, bf16[512,512]{1,0:T(8,128)(2,1)S(1)} %collective-permute-done.9.att_other, bf16[512,512]{1,0:T(8,128)(2,1)S(1)} %get-tuple-element.53.partial, ...), custom_call_target="tpu_custom_call" | custom-call | flops 1610612736 | bytes 47186 | tf_op jit(solution)/shard_map/pallas_call | solution.py:25
  63.8 1.6 %collective-permute-start.21 = (bf16[512,512]{1,0:T(8,128)(2,1)S(1)}, bf16[512,512]{1,0:T(8,128)(2,1)S(1)}, u32[]{:S(2)}, u32[]{:S(2)}) collective-permute-start(bf16[512,512]{1,0:T(8,128)(2,1)S(1)} %shard_map.90), channel_id=1, source_target_pairs={{0,8},{4,12},{8,0},{12,4},{16,24},{20,28},{24,16},{28,20},{1,9},{5... | collective-permute-start | bytes 1572872 | tf_op jit(solution)/shard_map/ppermute | solution.py:297
  66.0 1.4 %shard_map.91.refs_9_ = f32[2,256,512]{2,1,0:T(8,128)S(1)} custom-call(s32[8]{0:T(128)S(1)} %stack.32.place, bf16[4,128,512]{2,1,0:T(8,128)(2,1)S(1)} %collective-permute-done.3.refs_0_, bf16[4,128,512]{2,1,0:T(8,128)(2,1)S(1)} %collective-permute-done.8.refs_1_, bf16[4,128,512]{2,1,0:T(8,128)(2,1)S(1)} %collective-permute-done.4.refs_2_, ...), custom_call_target="tpu_custom_call" | custom-call | flops 5368709 | bytes 57672 | tf_op jit(solution)/shard_map/pallas_call | solution.py:25
  67.4 1.5 %collective-permute-start.16 = (bf16[1,256,512]{2,1,0:T(8,128)(2,1)S(1)}, bf16[1,256,512]{2,1,0:T(8,128)(2,1)S(1)}, u32[]{:S(2)}, u32[]{:S(2)}) collective-permute-start(bf16[1,256,512]{2,1,0:T(8,128)(2,1)S(1)} %collective-permute-done.15.refs_4_), channel_id=1, source_target_pairs={{1,0},{2,3},{5,4},{6,7},{9,8},{10,11},{13,12},{14,15},{17,16},{18,... | collective-permute-start | bytes 786440 | tf_op jit(solution)/shard_map/ppermute | solution.py:303
  68.9 6.1 %collective-permute-done.14.refs_1_.refs_3_.refs_5_ = bf16[2,256,512]{2,1,0:T(8,128)(2,1)S(1)} collective-permute-done((bf16[2,256,512]{2,1,0:T(8,128)(2,1)S(1)}, bf16[2,256,512]{2,1,0:T(8,128)(2,1)S(1)}, u32[]{:S(2)}, u32[]{:S(2)}) %collective-permute-start.14) | collective-permute-done | bytes 524320 | tf_op jit(solution)/shard_map/ppermute | solution.py:303
  76.0 2.5 %collective-permute-start.20 = (bf16[512,512]{1,0:T(8,128)(2,1)S(1)}, bf16[512,512]{1,0:T(8,128)(2,1)S(1)}, u32[]{:S(2)}, u32[]{:S(2)}) collective-permute-start(bf16[512,512]{1,0:T(8,128)(2,1)S(1)} %shard_map.95), channel_id=1, source_target_pairs={{0,8},{4,12},{8,0},{12,4},{16,24},{20,28},{24,16},{28,20},{1,9},{5... | collective-permute-start | bytes 1572872 | tf_op jit(solution)/shard_map/ppermute | solution.py:297
  78.7 1.0 %shard_map.96 = bf16[512,512]{1,0:T(8,128)(2,1)S(1)} custom-call(s32[8]{0:T(128)S(1)} %stack.32.place, bf16[512,512]{1,0:T(8,128)(2,1)S(1)} %get-tuple-element.47.att_own, bf16[512,512]{1,0:T(8,128)(2,1)S(1)} %collective-permute-done.9.att_other, bf16[512,512]{1,0:T(8,128)(2,1)S(1)} %get-tuple-element.70.partial, ...), custom_call_target="tpu_custom_call" | custom-call | flops 1610612736 | bytes 57672 | tf_op jit(solution)/shard_map/pallas_call | solution.py:25
  79.7 1.6 %collective-permute-start.22 = (bf16[512,512]{1,0:T(8,128)(2,1)S(1)}, bf16[512,512]{1,0:T(8,128)(2,1)S(1)}, u32[]{:S(2)}, u32[]{:S(2)}) collective-permute-start(bf16[512,512]{1,0:T(8,128)(2,1)S(1)} %shard_map.96), channel_id=1, source_target_pairs={{0,16},{4,20},{8,24},{12,28},{16,0},{20,4},{24,8},{28,12},{1,17},{... | collective-permute-start | bytes 1572872 | tf_op jit(solution)/shard_map/ppermute | solution.py:297
  81.4 1.1 %shard_map.92 = (f32[2,128,512]{2,1,0:T(8,128)S(1)}, bf16[2,128,512]{2,1,0:T(8,128)(2,1)S(1)}) custom-call(s32[8]{0:T(128)S(1)} %stack.32.place, bf16[2,256,512]{2,1,0:T(8,128)(2,1)S(1)} %collective-permute-done.11.refs_0_.refs_2_.refs_4_, bf16[2,256,512]{2,1,0:T(8,128)(2,1)S(1)} %collective-permute-done.14.refs_1_.refs_3_.refs_5_, ...), custom_call_target="tpu_custom_call" | custom-call | flops 5368709 | bytes 60293 | tf_op jit(solution)/shard_map/pallas_call | solution.py:25
  82.6 1.5 %collective-permute-done.18.grad_other = bf16[2,128,512]{2,1,0:T(8,128)(2,1)S(1)} collective-permute-done((bf16[2,128,512]{2,1,0:T(8,128)(2,1)S(1)}, bf16[2,128,512]{2,1,0:T(8,128)(2,1)S(1)}, u32[]{:S(2)}, u32[]{:S(2)}) %collective-permute-start.18) | collective-permute-done | bytes 262176 | tf_op jit(solution)/shard_map/ppermute | solution.py:297
  84.2 3.4 %shard_map.93 = (bf16[512,512]{1,0:T(8,128)(2,1)}, f32[128,512]{1,0:T(8,128)S(1)}, bf16[128,512]{1,0:T(8,128)(2,1)S(1)}) custom-call(s32[8]{0:T(128)S(1)} %stack.32.place, bf16[512,512]{1,0:T(8,128)(2,1)S(1)} %copy-done, bf16[2,128,512]{2,1,0:T(8,128)(2,1)S(1)} %get-tuple-element.40.kv, f32[512,128]{1,0:T(8,128)S(1)} %get-tuple-element.41.lse, ...), custom_call_target="tpu_custom_call" | custom-call | flops 5368709 | bytes 38011 | tf_op jit(solution)/shard_map/pallas_call | solution.py:25
  88.7 4.4 %collective-permute-done.19.other = bf16[128,512]{1,0:T(8,128)(2,1)S(1)} collective-permute-done((bf16[128,512]{1,0:T(8,128)(2,1)S(1)}, bf16[128,512]{1,0:T(8,128)(2,1)S(1)}, u32[]{:S(2)}, u32[]{:S(2)}) %collective-permute-start.19) | collective-permute-done | bytes 131104 | tf_op jit(solution)/shard_map/ppermute | solution.py:297
  (39 shorter events, 10.0 us)
Async XLA Ops:
  0.6 0.8 copy-start.3
  1.5 1.2 %copy-start.2 = (bf16[128,4096]{1,0:T(8,128)(2,1)S(1)}, bf16[128,4096]{1,0:T(8,128)(2,1)}, u32[]{:S(2)}) copy-start(bf16[128,4096]{1,0:T(8,128)(2,1)} %grad.1) | copy-start | bytes 3145732
  2.7 0.8 copy-start.4
  3.5 4.5 %copy-start.1 = (bf16[512,512]{1,0:T(8,128)(2,1)S(1)}, bf16[512,512]{1,0:T(8,128)(2,1)}, u32[]{:S(2)}) copy-start(bf16[512,512]{1,0:T(8,128)(2,1)} %refs_8_.1) | copy-start | bytes 1572868
  3.5 19.4 %copy-start = (bf16[512,512]{1,0:T(8,128)(2,1)S(1)}, bf16[512,512]{1,0:T(8,128)(2,1)}, u32[]{:S(2)}) copy-start(bf16[512,512]{1,0:T(8,128)(2,1)} %queries.4) | copy-start | bytes 1572868
  4.2 6.4 %collective-permute-start.1 = (bf16[4,128,512]{2,1,0:T(8,128)(2,1)S(1)}, bf16[4,128,512]{2,1,0:T(8,128)(2,1)S(1)}, u32[]{:S(2)}, u32[]{:S(2)}) collective-permute-start(bf16[4,128,512]{2,1,0:T(8,128)(2,1)S(1)} %get-tuple-element.42), channel_id=1, source_target_pairs={{0,4},{4,0},{8,12},{12,8},{16,20},{20,16},{24,28},{28,24},{1,5},{5... | collective-permute-start | bytes 1572872 | tf_op jit(solution)/shard_map/ppermute | solution.py:297
  4.7 18.2 %collective-permute-start = (bf16[640,512]{1,0:T(8,128)(2,1)S(1)}, bf16[640,512]{1,0:T(8,128)(2,1)S(1)}, u32[]{:S(2)}, u32[]{:S(2)}) collective-permute-start(bf16[640,512]{1,0:T(8,128)(2,1)S(1)} %get-tuple-element.39.refs_0_), channel_id=1, source_target_pairs={{0,1},{1,0},{2,3},{3,2},{4,5},{5,4},{6,7},{7,6},{8,9},{9,8},{10,11... | collective-permute-start | bytes 1966088 | tf_op jit(solution)/shard_map/ppermute | solution.py:297
  7.4 19.9 %collective-permute-start.3 = (bf16[4,128,512]{2,1,0:T(8,128)(2,1)S(1)}, bf16[4,128,512]{2,1,0:T(8,128)(2,1)S(1)}, u32[]{:S(2)}, u32[]{:S(2)}) collective-permute-start(bf16[4,128,512]{2,1,0:T(8,128)(2,1)S(1)} %get-tuple-element.44), channel_id=1, source_target_pairs={{1,2},{2,1},{5,6},{6,5},{9,10},{10,9},{13,14},{14,13},{17,18},{18,... | collective-permute-start | bytes 1572872 | tf_op jit(solution)/shard_map/ppermute | solution.py:300
  8.1 20.5 %collective-permute-start.5 = (bf16[512,512]{1,0:T(8,128)(2,1)S(1)}, bf16[512,512]{1,0:T(8,128)(2,1)S(1)}, u32[]{:S(2)}, u32[]{:S(2)}) collective-permute-start(bf16[512,512]{1,0:T(8,128)(2,1)S(1)} %copy-done.1), channel_id=1, source_target_pairs={{0,24},{4,28},{8,16},{12,20},{16,8},{20,12},{24,0},{28,4},{1,25},{... | collective-permute-start | bytes 1572872 | tf_op jit(solution)/shard_map/ppermute | solution.py:297
  10.6 23.6 %collective-permute-start.2 = (bf16[4,128,512]{2,1,0:T(8,128)(2,1)S(1)}, bf16[4,128,512]{2,1,0:T(8,128)(2,1)S(1)}, u32[]{:S(2)}, u32[]{:S(2)}) collective-permute-start(bf16[4,128,512]{2,1,0:T(8,128)(2,1)S(1)} %collective-permute-done.1.refs_1_), channel_id=1, source_target_pairs={{0,1},{1,0},{2,3},{3,2},{4,5},{5,4},{6,7},{7,6},{8,9},{9,8},{10,11... | collective-permute-start | bytes 1572872 | tf_op jit(solution)/shard_map/ppermute | solution.py:297
  15.0 21.2 %collective-permute-start.8 = (bf16[4,128,512]{2,1,0:T(8,128)(2,1)S(1)}, bf16[4,128,512]{2,1,0:T(8,128)(2,1)S(1)}, u32[]{:S(2)}, u32[]{:S(2)}) collective-permute-start(bf16[4,128,512]{2,1,0:T(8,128)(2,1)S(1)} %collective-permute-done.1.refs_1_), channel_id=1, source_target_pairs={{1,2},{2,1},{5,6},{6,5},{9,10},{10,9},{13,14},{14,13},{17,18},{18,... | collective-permute-start | bytes 1572872 | tf_op jit(solution)/shard_map/ppermute | solution.py:300
  27.1 9.0 %collective-permute-start.9 = (bf16[512,512]{1,0:T(8,128)(2,1)S(1)}, bf16[512,512]{1,0:T(8,128)(2,1)S(1)}, u32[]{:S(2)}, u32[]{:S(2)}) collective-permute-start(bf16[512,512]{1,0:T(8,128)(2,1)S(1)} %get-tuple-element.47.att_own), channel_id=1, source_target_pairs={{0,4},{4,0},{8,12},{12,8},{16,20},{20,16},{24,28},{28,24},{1,5},{5... | collective-permute-start | bytes 1572872 | tf_op jit(solution)/shard_map/ppermute | solution.py:297
  27.2 18.2 %collective-permute-start.4 = (bf16[4,128,512]{2,1,0:T(8,128)(2,1)S(1)}, bf16[4,128,512]{2,1,0:T(8,128)(2,1)S(1)}, u32[]{:S(2)}, u32[]{:S(2)}) collective-permute-start(bf16[4,128,512]{2,1,0:T(8,128)(2,1)S(1)} %collective-permute-done.3.refs_0_), channel_id=1, source_target_pairs={{1,0},{2,3},{5,4},{6,7},{9,8},{10,11},{13,12},{14,15},{17,16},{18,... | collective-permute-start | bytes 1572872 | tf_op jit(solution)/shard_map/ppermute | solution.py:303
  28.5 16.9 %collective-permute-start.6 = (bf16[512,512]{1,0:T(8,128)(2,1)S(1)}, bf16[512,512]{1,0:T(8,128)(2,1)S(1)}, u32[]{:S(2)}, u32[]{:S(2)}) collective-permute-start(bf16[512,512]{1,0:T(8,128)(2,1)S(1)} %copy-done.1), channel_id=1, source_target_pairs={{0,8},{4,12},{8,0},{12,4},{16,24},{20,28},{24,16},{28,20},{1,9},{5... | collective-permute-start | bytes 1572872 | tf_op jit(solution)/shard_map/ppermute | solution.py:297
  34.2 13.4 %collective-permute-start.7 = (bf16[512,512]{1,0:T(8,128)(2,1)S(1)}, bf16[512,512]{1,0:T(8,128)(2,1)S(1)}, u32[]{:S(2)}, u32[]{:S(2)}) collective-permute-start(bf16[512,512]{1,0:T(8,128)(2,1)S(1)} %copy-done.1), channel_id=1, source_target_pairs={{0,16},{4,20},{8,24},{12,28},{16,0},{20,4},{24,8},{28,12},{1,17},{... | collective-permute-start | bytes 1572872 | tf_op jit(solution)/shard_map/ppermute | solution.py:297
  36.2 11.4 %collective-permute-start.10 = (bf16[1,256,512]{2,1,0:T(8,128)(2,1)S(1)}, bf16[1,256,512]{2,1,0:T(8,128)(2,1)S(1)}, u32[]{:S(2)}, u32[]{:S(2)}) collective-permute-start(bf16[1,256,512]{2,1,0:T(8,128)(2,1)S(1)} %get-tuple-element.48), channel_id=1, source_target_pairs={{1,2},{2,1},{5,6},{6,5},{9,10},{10,9},{13,14},{14,13},{17,18},{18,... | collective-permute-start | bytes 786440 | tf_op jit(solution)/shard_map/ppermute | solution.py:300
  36.9 19.5 %collective-permute-start.12 = (bf16[4,128,512]{2,1,0:T(8,128)(2,1)S(1)}, bf16[4,128,512]{2,1,0:T(8,128)(2,1)S(1)}, u32[]{:S(2)}, u32[]{:S(2)}) collective-permute-start(bf16[4,128,512]{2,1,0:T(8,128)(2,1)S(1)} %collective-permute-done.8.refs_1_), channel_id=1, source_target_pairs={{1,0},{2,3},{5,4},{6,7},{9,8},{10,11},{13,12},{14,15},{17,16},{18,... | collective-permute-start | bytes 1572872 | tf_op jit(solution)/shard_map/ppermute | solution.py:303
  47.6 8.8 %collective-permute-start.11 = (bf16[2,256,512]{2,1,0:T(8,128)(2,1)S(1)}, bf16[2,256,512]{2,1,0:T(8,128)(2,1)S(1)}, u32[]{:S(2)}, u32[]{:S(2)}) collective-permute-start(bf16[2,256,512]{2,1,0:T(8,128)(2,1)S(1)} %get-tuple-element.49), channel_id=1, source_target_pairs={{1,2},{2,1},{5,6},{6,5},{9,10},{10,9},{13,14},{14,13},{17,18},{18,... | collective-permute-start | bytes 1572872 | tf_op jit(solution)/shard_map/ppermute | solution.py:300
  50.1 3.2 %collective-permute-start.13 = (bf16[2,128,512]{2,1,0:T(8,128)(2,1)S(1)}, bf16[2,128,512]{2,1,0:T(8,128)(2,1)S(1)}, u32[]{:S(2)}, u32[]{:S(2)}) collective-permute-start(bf16[2,128,512]{2,1,0:T(8,128)(2,1)S(1)} %get-tuple-element.51), channel_id=1, source_target_pairs={{0,4},{4,0},{8,12},{12,8},{16,20},{20,16},{24,28},{28,24},{1,5},{5... | collective-permute-start | bytes 786440 | tf_op jit(solution)/shard_map/ppermute | solution.py:297
  50.2 12.6 %collective-permute-start.17 = (bf16[1,256,512]{2,1,0:T(8,128)(2,1)S(1)}, bf16[1,256,512]{2,1,0:T(8,128)(2,1)S(1)}, u32[]{:S(2)}, u32[]{:S(2)}) collective-permute-start(bf16[1,256,512]{2,1,0:T(8,128)(2,1)S(1)} %collective-permute-done.10.refs_4_), channel_id=1, source_target_pairs={{1,0},{2,3},{5,4},{6,7},{9,8},{10,11},{13,12},{14,15},{17,16},{18,... | collective-permute-start | bytes 786440 | tf_op jit(solution)/shard_map/ppermute | solution.py:303
  56.4 18.6 %collective-permute-start.14 = (bf16[2,256,512]{2,1,0:T(8,128)(2,1)S(1)}, bf16[2,256,512]{2,1,0:T(8,128)(2,1)S(1)}, u32[]{:S(2)}, u32[]{:S(2)}) collective-permute-start(bf16[2,256,512]{2,1,0:T(8,128)(2,1)S(1)} %collective-permute-done.11.refs_0_.refs_2_.refs_4_), channel_id=1, source_target_pairs={{1,0},{2,3},{5,4},{6,7},{9,8},{10,11},{13,12},{14,15},{17,16},{18,... | collective-permute-start | bytes 1572872 | tf_op jit(solution)/shard_map/ppermute | solution.py:303
  63.8 14.9 %collective-permute-start.21 = (bf16[512,512]{1,0:T(8,128)(2,1)S(1)}, bf16[512,512]{1,0:T(8,128)(2,1)S(1)}, u32[]{:S(2)}, u32[]{:S(2)}) collective-permute-start(bf16[512,512]{1,0:T(8,128)(2,1)S(1)} %shard_map.90), channel_id=1, source_target_pairs={{0,8},{4,12},{8,0},{12,4},{16,24},{20,28},{24,16},{28,20},{1,9},{5... | collective-permute-start | bytes 1572872 | tf_op jit(solution)/shard_map/ppermute | solution.py:297
  65.3 2.1 %collective-permute-start.15 = (bf16[1,256,512]{2,1,0:T(8,128)(2,1)S(1)}, bf16[1,256,512]{2,1,0:T(8,128)(2,1)S(1)}, u32[]{:S(2)}, u32[]{:S(2)}) collective-permute-start(bf16[1,256,512]{2,1,0:T(8,128)(2,1)S(1)} %get-tuple-element.58), channel_id=1, source_target_pairs={{1,2},{2,1},{5,6},{6,5},{9,10},{10,9},{13,14},{14,13},{17,18},{18,... | collective-permute-start | bytes 786440 | tf_op jit(solution)/shard_map/ppermute | solution.py:300
  67.4 14.0 %collective-permute-start.16 = (bf16[1,256,512]{2,1,0:T(8,128)(2,1)S(1)}, bf16[1,256,512]{2,1,0:T(8,128)(2,1)S(1)}, u32[]{:S(2)}, u32[]{:S(2)}) collective-permute-start(bf16[1,256,512]{2,1,0:T(8,128)(2,1)S(1)} %collective-permute-done.15.refs_4_), channel_id=1, source_target_pairs={{1,0},{2,3},{5,4},{6,7},{9,8},{10,11},{13,12},{14,15},{17,16},{18,... | collective-permute-start | bytes 786440 | tf_op jit(solution)/shard_map/ppermute | solution.py:303
  76.0 17.1 %collective-permute-start.20 = (bf16[512,512]{1,0:T(8,128)(2,1)S(1)}, bf16[512,512]{1,0:T(8,128)(2,1)S(1)}, u32[]{:S(2)}, u32[]{:S(2)}) collective-permute-start(bf16[512,512]{1,0:T(8,128)(2,1)S(1)} %shard_map.95), channel_id=1, source_target_pairs={{0,8},{4,12},{8,0},{12,4},{16,24},{20,28},{24,16},{28,20},{1,9},{5... | collective-permute-start | bytes 1572872 | tf_op jit(solution)/shard_map/ppermute | solution.py:297
  79.7 13.4 %collective-permute-start.22 = (bf16[512,512]{1,0:T(8,128)(2,1)S(1)}, bf16[512,512]{1,0:T(8,128)(2,1)S(1)}, u32[]{:S(2)}, u32[]{:S(2)}) collective-permute-start(bf16[512,512]{1,0:T(8,128)(2,1)S(1)} %shard_map.96), channel_id=1, source_target_pairs={{0,16},{4,20},{8,24},{12,28},{16,0},{20,4},{24,8},{28,12},{1,17},{... | collective-permute-start | bytes 1572872 | tf_op jit(solution)/shard_map/ppermute | solution.py:297
  82.6 1.6 %collective-permute-start.18 = (bf16[2,128,512]{2,1,0:T(8,128)(2,1)S(1)}, bf16[2,128,512]{2,1,0:T(8,128)(2,1)S(1)}, u32[]{:S(2)}, u32[]{:S(2)}) collective-permute-start(bf16[2,128,512]{2,1,0:T(8,128)(2,1)S(1)} %get-tuple-element.61), channel_id=1, source_target_pairs={{0,4},{4,0},{8,12},{12,8},{16,20},{20,16},{24,28},{28,24},{1,5},{5... | collective-permute-start | bytes 786440 | tf_op jit(solution)/shard_map/ppermute | solution.py:297
  87.6 5.5 %collective-permute-start.19 = (bf16[128,512]{1,0:T(8,128)(2,1)S(1)}, bf16[128,512]{1,0:T(8,128)(2,1)S(1)}, u32[]{:S(2)}, u32[]{:S(2)}) collective-permute-start(bf16[128,512]{1,0:T(8,128)(2,1)S(1)} %get-tuple-element.66), channel_id=1, source_target_pairs={{0,1},{1,0},{2,3},{3,2},{4,5},{5,4},{6,7},{7,6},{8,9},{9,8},{10,11... | collective-permute-start | bytes 393224 | tf_op jit(solution)/shard_map/ppermute | solution.py:297

commit v6 on v3

--- a/solution.py
+++ b/solution.py
@@ -328,7 +328,7 @@
     near = [swap(own_kv, "tensor", 1), swap(taken, "tensor", 1)]
     weights = {0: out_weight}
     for s in reversed(order[:-1]):
-        operand = tie(out_weight, near[0]) if s & (s - 1) else out_weight
+        operand = out_weight if s & (s - 1) else tie(out_weight, near[0])
         weights[s] = swap(operand, "dp", 2 * s)
     weights = [weights[s] for s in order]
 
@@ -338,8 +338,8 @@
     flops = 4 * length * depth * width // 100
     if tensor == 4:
         middle_own = across(own)
-        direct = [w for s, w in zip(order, weights) if s & (s - 1) == 0]
-        middle_taken = across(tie(taken, middle_own, near[0]))
+        direct = [w for s, w in zip(order, weights) if s & (s - 1)]
+        middle_taken = across(taken)
         hold = []
         kv, attended, lse = call(
             forward_kernel,
@@ -362,7 +362,7 @@
             near,
             400 * flops,
         )
-        after = [[middle_taken, attended, *direct], [in_own, weights[0], att_other], []]
+        after = [[middle_taken, att_other, *direct], [in_own, weights[0]], []]
         for side in range(len(sizes)):
             second.append(across(tie(relay[side], *after[side], *second[-1:])))
     else:

time: 94.3 us -> 93.6 us (level)
    ppermute x5, waiting for transfers between devices: 19.9 us -> 17.1 us  [outward(): return lax.ppermute(value, 'tensor', [(1, 0), (2, 3)])]
    ppermute x14, waiting for transfers between devices: 17.6 us -> 20.4 us  [swap(): lax.ppermute(value, axis, [(i, i ^ mask) for i in range(lax.axis_size(axi...]
  transfers between devices with their start and end apart: 24 -> 24, of which waited for: 9 -> 10; matrix products, arithmetic and copies ran while one was open for 0% -> 0% of each run, Pallas kernels for 21% -> 21%
where the time goes in v6:
time: 93.6 us; the launch traced here: 93.2 us
  waiting for transfers between devices  37.4 us (40%)
  starting transfers between devices  30.7 us (33%)
  Pallas kernels  21.3 us (23%)
  local copies, waits for them, and re-layouts  2.87 us (3%)
  between operations  0.94 us (1%)
    pallas_call x14, Pallas kernels, call(): pl.pallas_call(kernel, out_shape=tuple(outs), in_specs=[SMEM] * scalars +...  21.3 us
    ppermute x14, starting transfers between devices, swap(): lax.ppermute(value, axis, [(i, i ^ mask) for i in range(lax.axis_size(axi...  20.7 us
    ppermute x14, waiting for transfers between devices, swap(): lax.ppermute(value, axis, [(i, i ^ mask) for i in range(lax.axis_size(axi...  20.4 us
    ppermute x5, waiting for transfers between devices, outward(): return lax.ppermute(value, 'tensor', [(1, 0), (2, 3)])  17.1 us
    ppermute x5, starting transfers between devices, outward(): return lax.ppermute(value, 'tensor', [(1, 0), (2, 3)])  6.63 us
    ppermute x5, starting transfers between devices, across(): return lax.ppermute(value, 'tensor', [(1, 2), (2, 1)])  3.4 us
    unnamed x10, local copies, waits for them, and re-layouts  2.78 us
  transfers between devices with their start and end apart: 24, of which 10 were waited for; matrix products, arithmetic and copies ran while one was open for 0% of the time, Pallas kernels for 21%

profile of v6, /device:TPU:0, one launch (start us, length us, event | category | flops | bytes accessed | tf_op | source)
XLA Modules:
  0.0 93.2 jit_solution(1111929637763401909)
XLA Ops:
  1.5 1.2 %copy-done.2 = bf16[128,4096]{1,0:T(8,128)(2,1)S(1)} copy-done((bf16[128,4096]{1,0:T(8,128)(2,1)S(1)}, bf16[128,4096]{1,0:T(8,128)(2,1)}, u32[]{:S(2)}) %copy-start.2) | copy-done | bytes 1048600
  4.7 2.6 %collective-permute-start = (bf16[640,512]{1,0:T(8,128)(2,1)S(1)}, bf16[640,512]{1,0:T(8,128)(2,1)S(1)}, u32[]{:S(2)}, u32[]{:S(2)}) collective-permute-start(bf16[640,512]{1,0:T(8,128)(2,1)S(1)} %get-tuple-element.41.refs_0_), channel_id=1, source_target_pairs={{0,1},{1,0},{2,3},{3,2},{4,5},{5,4},{6,7},{7,6},{8,9},{9,8},{10,11... | collective-permute-start | bytes 1966088 | tf_op jit(solution)/shard_map/ppermute | solution.py:307
  8.1 2.5 %collective-permute-start.5 = (bf16[512,512]{1,0:T(8,128)(2,1)S(1)}, bf16[512,512]{1,0:T(8,128)(2,1)S(1)}, u32[]{:S(2)}, u32[]{:S(2)}) collective-permute-start(bf16[512,512]{1,0:T(8,128)(2,1)S(1)} %copy-done.1), channel_id=1, source_target_pairs={{0,24},{4,28},{8,16},{12,20},{16,8},{20,12},{24,0},{28,4},{1,25},{... | collective-permute-start | bytes 1572872 | tf_op jit(solution)/shard_map/ppermute | solution.py:307
  10.6 4.4 %collective-permute-start.2 = (bf16[4,128,512]{2,1,0:T(8,128)(2,1)S(1)}, bf16[4,128,512]{2,1,0:T(8,128)(2,1)S(1)}, u32[]{:S(2)}, u32[]{:S(2)}) collective-permute-start(bf16[4,128,512]{2,1,0:T(8,128)(2,1)S(1)} %collective-permute-done.1.refs_1_), channel_id=1, source_target_pairs={{0,1},{1,0},{2,3},{3,2},{4,5},{5,4},{6,7},{7,6},{8,9},{9,8},{10,11... | collective-permute-start | bytes 1572872 | tf_op jit(solution)/shard_map/ppermute | solution.py:307
  15.6 7.3 %collective-permute-done.near.first.refs_2_ = bf16[640,512]{1,0:T(8,128)(2,1)S(1)} collective-permute-done((bf16[640,512]{1,0:T(8,128)(2,1)S(1)}, bf16[640,512]{1,0:T(8,128)(2,1)S(1)}, u32[]{:S(2)}, u32[]{:S(2)}) %collective-permute-start) | collective-permute-done | bytes 655392 | tf_op jit(solution)/shard_map/ppermute | solution.py:307
  23.0 4.2 %shard_map.85 = (bf16[2,128,512]{2,1,0:T(8,128)(2,1)S(1)}, bf16[512,512]{1,0:T(8,128)(2,1)S(1)}, f32[512,128]{1,0:T(8,128)S(1)}) custom-call(s32[8]{0:T(128)S(1)} %stack.32.place, bf16[512,512]{1,0:T(8,128)(2,1)S(1)} %copy-done, bf16[64,512]{1,0:T(8,128)(2,1)S(1)} %bitcast.12, bf16[64,512]{1,0:T(8,128)(2,1)S(1)} %bitcast.14, ...), custom_call_target="tpu_custom_call" | custom-call | flops 5368709 | bytes 23593 | tf_op jit(solution)/shard_map/pallas_call | solution.py:25
  27.2 1.3 %collective-permute-start.4 = (bf16[4,128,512]{2,1,0:T(8,128)(2,1)S(1)}, bf16[4,128,512]{2,1,0:T(8,128)(2,1)S(1)}, u32[]{:S(2)}, u32[]{:S(2)}) collective-permute-start(bf16[4,128,512]{2,1,0:T(8,128)(2,1)S(1)} %collective-permute-done.3.refs_0_), channel_id=1, source_target_pairs={{1,0},{2,3},{5,4},{6,7},{9,8},{10,11},{13,12},{14,15},{17,16},{18,... | collective-permute-start | bytes 1572872 | tf_op jit(solution)/shard_map/ppermute | solution.py:313
  28.5 1.9 %collective-permute-start.11 = (bf16[512,512]{1,0:T(8,128)(2,1)S(1)}, bf16[512,512]{1,0:T(8,128)(2,1)S(1)}, u32[]{:S(2)}, u32[]{:S(2)}) collective-permute-start(bf16[512,512]{1,0:T(8,128)(2,1)S(1)} %copy-done.1), channel_id=1, source_target_pairs={{0,8},{4,12},{8,0},{12,4},{16,24},{20,28},{24,16},{28,20},{1,9},{5... | collective-permute-start | bytes 1572872 | tf_op jit(solution)/shard_map/ppermute | solution.py:307
  30.5 3.7 %collective-permute-done.2.second.refs_3_ = bf16[4,128,512]{2,1,0:T(8,128)(2,1)S(1)} collective-permute-done((bf16[4,128,512]{2,1,0:T(8,128)(2,1)S(1)}, bf16[4,128,512]{2,1,0:T(8,128)(2,1)S(1)}, u32[]{:S(2)}, u32[]{:S(2)}) %collective-permute-start.2) | collective-permute-done | bytes 524320 | tf_op jit(solution)/shard_map/ppermute | solution.py:307
  34.2 1.9 %collective-permute-start.12 = (bf16[512,512]{1,0:T(8,128)(2,1)S(1)}, bf16[512,512]{1,0:T(8,128)(2,1)S(1)}, u32[]{:S(2)}, u32[]{:S(2)}) collective-permute-start(bf16[512,512]{1,0:T(8,128)(2,1)S(1)} %copy-done.1), channel_id=1, source_target_pairs={{0,16},{4,20},{8,24},{12,28},{16,0},{20,4},{24,8},{28,12},{1,17},{... | collective-permute-start | bytes 1572872 | tf_op jit(solution)/shard_map/ppermute | solution.py:307
  36.9 1.3 %collective-permute-start.10 = (bf16[4,128,512]{2,1,0:T(8,128)(2,1)S(1)}, bf16[4,128,512]{2,1,0:T(8,128)(2,1)S(1)}, u32[]{:S(2)}, u32[]{:S(2)}) collective-permute-start(bf16[4,128,512]{2,1,0:T(8,128)(2,1)S(1)} %collective-permute-done.6.refs_1_), channel_id=1, source_target_pairs={{1,0},{2,3},{5,4},{6,7},{9,8},{10,11},{13,12},{14,15},{17,16},{18,... | collective-permute-start | bytes 1572872 | tf_op jit(solution)/shard_map/ppermute | solution.py:313
  38.2 7.3 %collective-permute-done.4.refs_2_ = bf16[4,128,512]{2,1,0:T(8,128)(2,1)S(1)} collective-permute-done((bf16[4,128,512]{2,1,0:T(8,128)(2,1)S(1)}, bf16[4,128,512]{2,1,0:T(8,128)(2,1)S(1)}, u32[]{:S(2)}, u32[]{:S(2)}) %collective-permute-start.4) | collective-permute-done | bytes 524320 | tf_op jit(solution)/shard_map/ppermute | solution.py:313
  46.1 1.5 %collective-permute-done.12.refs_6_.refs_8_.refs_7_ = bf16[512,512]{1,0:T(8,128)(2,1)S(1)} collective-permute-done((bf16[512,512]{1,0:T(8,128)(2,1)S(1)}, bf16[512,512]{1,0:T(8,128)(2,1)S(1)}, u32[]{:S(2)}, u32[]{:S(2)}) %collective-permute-start.12) | collective-permute-done | bytes 524320 | tf_op jit(solution)/shard_map/ppermute | solution.py:307
  47.6 1.8 %shard_map.87 = (f32[2,128,512]{2,1,0:T(8,128)S(1)}, bf16[2,128,512]{2,1,0:T(8,128)(2,1)S(1)}) custom-call(s32[8]{0:T(128)S(1)} %stack.32.place, bf16[640,512]{1,0:T(8,128)(2,1)S(1)} %get-tuple-element.41.refs_0_, bf16[4,128,512]{2,1,0:T(8,128)(2,1)S(1)} %collective-permute-done.1.refs_1_, bf16[640,512]{1,0:T(8,128)(2,1)S(1)} %collective-permute-done.near.first.refs_2_, ...), custom_call_target="tpu_custom_call" | custom-call | flops 1610612736 | bytes 52429 | tf_op jit(solution)/shard_map/pallas_call | solution.py:25
  49.5 1.3 %collective-permute-start.17 = (bf16[1,256,512]{2,1,0:T(8,128)(2,1)S(1)}, bf16[1,256,512]{2,1,0:T(8,128)(2,1)S(1)}, u32[]{:S(2)}, u32[]{:S(2)}) collective-permute-start(bf16[1,256,512]{2,1,0:T(8,128)(2,1)S(1)} %collective-permute-done.8.refs_4_), channel_id=1, source_target_pairs={{1,0},{2,3},{5,4},{6,7},{9,8},{10,11},{13,12},{14,15},{17,16},{18,... | collective-permute-start | bytes 786440 | tf_op jit(solution)/shard_map/ppermute | solution.py:313
  50.8 1.8 %shard_map.88 = (bf16[512,512]{1,0:T(8,128)(2,1)S(1)}, bf16[512,512]{1,0:T(8,128)(2,1)S(1)}, bf16[512,512]{1,0:T(8,128)(2,1)S(1)}, bf16[512,512]{1,0:T(8,128)(2,1)S(1)}) custom-call(s32[8]{0:T(128)S(1)} %stack.32.place, bf16[512,512]{1,0:T(8,128)(2,1)S(1)} %get-tuple-element.48.att_own, bf16[512,512]{1,0:T(8,128)(2,1)S(1)} %collective-permute-done.7.att_other, ...), custom_call_target="tpu_custom_call" | custom-call | flops 5368709 | bytes 55050 | tf_op jit(solution)/shard_map/pallas_call | solution.py:25
  52.6 1.8 %shard_map.89 = (bf16[512,512]{1,0:T(8,128)(2,1)S(1)}, f32[128,512]{1,0:T(8,128)S(1)}, f32[128,512]{1,0:T(8,128)S(1)}) custom-call(s32[8]{0:T(128)S(1)} %stack.32.place, bf16[512,512]{1,0:T(8,128)(2,1)S(1)} %copy-done, bf16[2,128,512]{2,1,0:T(8,128)(2,1)S(1)} %get-tuple-element.42.kv, f32[512,128]{1,0:T(8,128)S(1)} %get-tuple-element.43.lse, ...), custom_call_target="tpu_custom_call" | custom-call | flops 5368709 | bytes 28836 | tf_op jit(solution)/shard_map/pallas_call | solution.py:25
  54.4 2.2 %collective-permute-done.10.refs_3_ = bf16[4,128,512]{2,1,0:T(8,128)(2,1)S(1)} collective-permute-done((bf16[4,128,512]{2,1,0:T(8,128)(2,1)S(1)}, bf16[4,128,512]{2,1,0:T(8,128)(2,1)S(1)}, u32[]{:S(2)}, u32[]{:S(2)}) %collective-permute-start.10) | collective-permute-done | bytes 524320 | tf_op jit(solution)/shard_map/ppermute | solution.py:313
  56.7 1.3 %collective-permute-start.14 = (bf16[2,256,512]{2,1,0:T(8,128)(2,1)S(1)}, bf16[2,256,512]{2,1,0:T(8,128)(2,1)S(1)}, u32[]{:S(2)}, u32[]{:S(2)}) collective-permute-start(bf16[2,256,512]{2,1,0:T(8,128)(2,1)S(1)} %collective-permute-done.9.refs_0_.refs_2_.refs_4_), channel_id=1, source_target_pairs={{1,0},{2,3},{5,4},{6,7},{9,8},{10,11},{13,12},{14,15},{17,16},{18,... | collective-permute-start | bytes 1572872 | tf_op jit(solution)/shard_map/ppermute | solution.py:313
  58.6 3.6 %collective-permute-done.17.refs_5_ = bf16[1,256,512]{2,1,0:T(8,128)(2,1)S(1)} collective-permute-done((bf16[1,256,512]{2,1,0:T(8,128)(2,1)S(1)}, bf16[1,256,512]{2,1,0:T(8,128)(2,1)S(1)}, u32[]{:S(2)}, u32[]{:S(2)}) %collective-permute-start.17) | collective-permute-done | bytes 262176 | tf_op jit(solution)/shard_map/ppermute | solution.py:313
  63.3 1.7 %collective-permute-start.20 = (bf16[256,512]{1,0:T(8,128)(2,1)S(1)}, bf16[256,512]{1,0:T(8,128)(2,1)S(1)}, u32[]{:S(2)}, u32[]{:S(2)}) collective-permute-start(bf16[256,512]{1,0:T(8,128)(2,1)S(1)} %get-tuple-element.73), channel_id=1, source_target_pairs={{0,16},{4,20},{8,24},{12,28},{16,0},{20,4},{24,8},{28,12},{1,17},{... | collective-permute-start | bytes 786440 | tf_op jit(solution)/shard_map/ppermute | solution.py:307
  65.0 1.5 %collective-permute-start.22 = (bf16[256,512]{1,0:T(8,128)(2,1)S(1)}, bf16[256,512]{1,0:T(8,128)(2,1)S(1)}, u32[]{:S(2)}, u32[]{:S(2)}) collective-permute-start(bf16[256,512]{1,0:T(8,128)(2,1)S(1)} %get-tuple-element.61), channel_id=1, source_target_pairs={{0,8},{4,12},{8,0},{12,4},{16,24},{20,28},{24,16},{28,20},{1,9},{5... | collective-permute-start | bytes 786440 | tf_op jit(solution)/shard_map/ppermute | solution.py:307
  66.5 1.4 %shard_map.91.refs_9_ = f32[2,256,512]{2,1,0:T(8,128)S(1)} custom-call(s32[8]{0:T(128)S(1)} %stack.32.place, bf16[4,128,512]{2,1,0:T(8,128)(2,1)S(1)} %collective-permute-done.3.refs_0_, bf16[4,128,512]{2,1,0:T(8,128)(2,1)S(1)} %collective-permute-done.6.refs_1_, bf16[4,128,512]{2,1,0:T(8,128)(2,1)S(1)} %collective-permute-done.4.refs_2_, ...), custom_call_target="tpu_custom_call" | custom-call | flops 5368709 | bytes 57672 | tf_op jit(solution)/shard_map/pallas_call | solution.py:25
  67.9 1.5 %collective-permute-start.16 = (bf16[1,256,512]{2,1,0:T(8,128)(2,1)S(1)}, bf16[1,256,512]{2,1,0:T(8,128)(2,1)S(1)}, u32[]{:S(2)}, u32[]{:S(2)}) collective-permute-start(bf16[1,256,512]{2,1,0:T(8,128)(2,1)S(1)} %collective-permute-done.15.refs_4_), channel_id=1, source_target_pairs={{1,0},{2,3},{5,4},{6,7},{9,8},{10,11},{13,12},{14,15},{17,16},{18,... | collective-permute-start | bytes 786440 | tf_op jit(solution)/shard_map/ppermute | solution.py:313
  69.4 1.8 %collective-permute-done.20.refs_6_ = bf16[256,512]{1,0:T(8,128)(2,1)S(1)} collective-permute-done((bf16[256,512]{1,0:T(8,128)(2,1)S(1)}, bf16[256,512]{1,0:T(8,128)(2,1)S(1)}, u32[]{:S(2)}, u32[]{:S(2)}) %collective-permute-start.20) | collective-permute-done | bytes 262176 | tf_op jit(solution)/shard_map/ppermute | solution.py:307
  71.2 3.9 %collective-permute-done.14.refs_1_.refs_3_.refs_5_ = bf16[2,256,512]{2,1,0:T(8,128)(2,1)S(1)} collective-permute-done((bf16[2,256,512]{2,1,0:T(8,128)(2,1)S(1)}, bf16[2,256,512]{2,1,0:T(8,128)(2,1)S(1)}, u32[]{:S(2)}, u32[]{:S(2)}) %collective-permute-start.14) | collective-permute-done | bytes 524320 | tf_op jit(solution)/shard_map/ppermute | solution.py:313
  76.1 1.8 %collective-permute-start.21 = (bf16[512,512]{1,0:T(8,128)(2,1)S(1)}, bf16[512,512]{1,0:T(8,128)(2,1)S(1)}, u32[]{:S(2)}, u32[]{:S(2)}) collective-permute-start(bf16[512,512]{1,0:T(8,128)(2,1)S(1)} %shard_map.95), channel_id=1, source_target_pairs={{0,8},{4,12},{8,0},{12,4},{16,24},{20,28},{24,16},{28,20},{1,9},{5... | collective-permute-start | bytes 1572872 | tf_op jit(solution)/shard_map/ppermute | solution.py:307
  79.0 1.6 %collective-permute-start.23 = (bf16[512,512]{1,0:T(8,128)(2,1)S(1)}, bf16[512,512]{1,0:T(8,128)(2,1)S(1)}, u32[]{:S(2)}, u32[]{:S(2)}) collective-permute-start(bf16[512,512]{1,0:T(8,128)(2,1)S(1)} %shard_map.96), channel_id=1, source_target_pairs={{0,16},{4,20},{8,24},{12,28},{16,0},{20,4},{24,8},{28,12},{1,17},{... | collective-permute-start | bytes 1572872 | tf_op jit(solution)/shard_map/ppermute | solution.py:307
  80.5 1.1 %shard_map.92 = (f32[2,128,512]{2,1,0:T(8,128)S(1)}, bf16[2,128,512]{2,1,0:T(8,128)(2,1)S(1)}) custom-call(s32[8]{0:T(128)S(1)} %stack.32.place, bf16[2,256,512]{2,1,0:T(8,128)(2,1)S(1)} %collective-permute-done.9.refs_0_.refs_2_.refs_4_, bf16[2,256,512]{2,1,0:T(8,128)(2,1)S(1)} %collective-permute-done.14.refs_1_.refs_3_.refs_5_, ...), custom_call_target="tpu_custom_call" | custom-call | flops 5368709 | bytes 60293 | tf_op jit(solution)/shard_map/pallas_call | solution.py:25
  81.7 1.5 %collective-permute-done.18.grad_other = bf16[2,128,512]{2,1,0:T(8,128)(2,1)S(1)} collective-permute-done((bf16[2,128,512]{2,1,0:T(8,128)(2,1)S(1)}, bf16[2,128,512]{2,1,0:T(8,128)(2,1)S(1)}, u32[]{:S(2)}, u32[]{:S(2)}) %collective-permute-start.18) | collective-permute-done | bytes 262176 | tf_op jit(solution)/shard_map/ppermute | solution.py:307
  83.3 3.4 %shard_map.93 = (bf16[512,512]{1,0:T(8,128)(2,1)}, f32[128,512]{1,0:T(8,128)S(1)}, bf16[128,512]{1,0:T(8,128)(2,1)S(1)}) custom-call(s32[8]{0:T(128)S(1)} %stack.32.place, bf16[512,512]{1,0:T(8,128)(2,1)S(1)} %copy-done, bf16[2,128,512]{2,1,0:T(8,128)(2,1)S(1)} %get-tuple-element.42.kv, f32[512,128]{1,0:T(8,128)S(1)} %get-tuple-element.43.lse, ...), custom_call_target="tpu_custom_call" | custom-call | flops 5368709 | bytes 38011 | tf_op jit(solution)/shard_map/pallas_call | solution.py:25
  87.7 4.5 %collective-permute-done.19.other = bf16[128,512]{1,0:T(8,128)(2,1)S(1)} collective-permute-done((bf16[128,512]{1,0:T(8,128)(2,1)S(1)}, bf16[128,512]{1,0:T(8,128)(2,1)S(1)}, u32[]{:S(2)}, u32[]{:S(2)}) %collective-permute-start.19) | collective-permute-done | bytes 131104 | tf_op jit(solution)/shard_map/ppermute | solution.py:307
  (41 shorter events, 11.6 us)
Async XLA Ops:
  0.6 0.8 copy-start.3
  1.5 1.2 %copy-start.2 = (bf16[128,4096]{1,0:T(8,128)(2,1)S(1)}, bf16[128,4096]{1,0:T(8,128)(2,1)}, u32[]{:S(2)}) copy-start(bf16[128,4096]{1,0:T(8,128)(2,1)} %grad.1) | copy-start | bytes 3145732
  2.7 0.8 copy-start.4
  3.5 4.5 %copy-start.1 = (bf16[512,512]{1,0:T(8,128)(2,1)S(1)}, bf16[512,512]{1,0:T(8,128)(2,1)}, u32[]{:S(2)}) copy-start(bf16[512,512]{1,0:T(8,128)(2,1)} %refs_8_.1) | copy-start | bytes 1572868
  3.5 19.4 %copy-start = (bf16[512,512]{1,0:T(8,128)(2,1)S(1)}, bf16[512,512]{1,0:T(8,128)(2,1)}, u32[]{:S(2)}) copy-start(bf16[512,512]{1,0:T(8,128)(2,1)} %queries.4) | copy-start | bytes 1572868
  4.2 6.4 %collective-permute-start.1 = (bf16[4,128,512]{2,1,0:T(8,128)(2,1)S(1)}, bf16[4,128,512]{2,1,0:T(8,128)(2,1)S(1)}, u32[]{:S(2)}, u32[]{:S(2)}) collective-permute-start(bf16[4,128,512]{2,1,0:T(8,128)(2,1)S(1)} %get-tuple-element.44), channel_id=1, source_target_pairs={{0,4},{4,0},{8,12},{12,8},{16,20},{20,16},{24,28},{28,24},{1,5},{5... | collective-permute-start | bytes 1572872 | tf_op jit(solution)/shard_map/ppermute | solution.py:307
  4.7 18.2 %collective-permute-start = (bf16[640,512]{1,0:T(8,128)(2,1)S(1)}, bf16[640,512]{1,0:T(8,128)(2,1)S(1)}, u32[]{:S(2)}, u32[]{:S(2)}) collective-permute-start(bf16[640,512]{1,0:T(8,128)(2,1)S(1)} %get-tuple-element.41.refs_0_), channel_id=1, source_target_pairs={{0,1},{1,0},{2,3},{3,2},{4,5},{5,4},{6,7},{7,6},{8,9},{9,8},{10,11... | collective-permute-start | bytes 1966088 | tf_op jit(solution)/shard_map/ppermute | solution.py:307
  7.4 19.9 %collective-permute-start.3 = (bf16[4,128,512]{2,1,0:T(8,128)(2,1)S(1)}, bf16[4,128,512]{2,1,0:T(8,128)(2,1)S(1)}, u32[]{:S(2)}, u32[]{:S(2)}) collective-permute-start(bf16[4,128,512]{2,1,0:T(8,128)(2,1)S(1)} %get-tuple-element.46), channel_id=1, source_target_pairs={{1,2},{2,1},{5,6},{6,5},{9,10},{10,9},{13,14},{14,13},{17,18},{18,... | collective-permute-start | bytes 1572872 | tf_op jit(solution)/shard_map/ppermute | solution.py:310
  8.1 20.5 %collective-permute-start.5 = (bf16[512,512]{1,0:T(8,128)(2,1)S(1)}, bf16[512,512]{1,0:T(8,128)(2,1)S(1)}, u32[]{:S(2)}, u32[]{:S(2)}) collective-permute-start(bf16[512,512]{1,0:T(8,128)(2,1)S(1)} %copy-done.1), channel_id=1, source_target_pairs={{0,24},{4,28},{8,16},{12,20},{16,8},{20,12},{24,0},{28,4},{1,25},{... | collective-permute-start | bytes 1572872 | tf_op jit(solution)/shard_map/ppermute | solution.py:307
  10.6 23.6 %collective-permute-start.2 = (bf16[4,128,512]{2,1,0:T(8,128)(2,1)S(1)}, bf16[4,128,512]{2,1,0:T(8,128)(2,1)S(1)}, u32[]{:S(2)}, u32[]{:S(2)}) collective-permute-start(bf16[4,128,512]{2,1,0:T(8,128)(2,1)S(1)} %collective-permute-done.1.refs_1_), channel_id=1, source_target_pairs={{0,1},{1,0},{2,3},{3,2},{4,5},{5,4},{6,7},{7,6},{8,9},{9,8},{10,11... | collective-permute-start | bytes 1572872 | tf_op jit(solution)/shard_map/ppermute | solution.py:307
  15.0 21.2 %collective-permute-start.6 = (bf16[4,128,512]{2,1,0:T(8,128)(2,1)S(1)}, bf16[4,128,512]{2,1,0:T(8,128)(2,1)S(1)}, u32[]{:S(2)}, u32[]{:S(2)}) collective-permute-start(bf16[4,128,512]{2,1,0:T(8,128)(2,1)S(1)} %collective-permute-done.1.refs_1_), channel_id=1, source_target_pairs={{1,2},{2,1},{5,6},{6,5},{9,10},{10,9},{13,14},{14,13},{17,18},{18,... | collective-permute-start | bytes 1572872 | tf_op jit(solution)/shard_map/ppermute | solution.py:310
  27.1 9.0 %collective-permute-start.7 = (bf16[512,512]{1,0:T(8,128)(2,1)S(1)}, bf16[512,512]{1,0:T(8,128)(2,1)S(1)}, u32[]{:S(2)}, u32[]{:S(2)}) collective-permute-start(bf16[512,512]{1,0:T(8,128)(2,1)S(1)} %get-tuple-element.48.att_own), channel_id=1, source_target_pairs={{0,4},{4,0},{8,12},{12,8},{16,20},{20,16},{24,28},{28,24},{1,5},{5... | collective-permute-start | bytes 1572872 | tf_op jit(solution)/shard_map/ppermute | solution.py:307
  27.2 18.2 %collective-permute-start.4 = (bf16[4,128,512]{2,1,0:T(8,128)(2,1)S(1)}, bf16[4,128,512]{2,1,0:T(8,128)(2,1)S(1)}, u32[]{:S(2)}, u32[]{:S(2)}) collective-permute-start(bf16[4,128,512]{2,1,0:T(8,128)(2,1)S(1)} %collective-permute-done.3.refs_0_), channel_id=1, source_target_pairs={{1,0},{2,3},{5,4},{6,7},{9,8},{10,11},{13,12},{14,15},{17,16},{18,... | collective-permute-start | bytes 1572872 | tf_op jit(solution)/shard_map/ppermute | solution.py:313
  28.5 17.6 %collective-permute-start.11 = (bf16[512,512]{1,0:T(8,128)(2,1)S(1)}, bf16[512,512]{1,0:T(8,128)(2,1)S(1)}, u32[]{:S(2)}, u32[]{:S(2)}) collective-permute-start(bf16[512,512]{1,0:T(8,128)(2,1)S(1)} %copy-done.1), channel_id=1, source_target_pairs={{0,8},{4,12},{8,0},{12,4},{16,24},{20,28},{24,16},{28,20},{1,9},{5... | collective-permute-start | bytes 1572872 | tf_op jit(solution)/shard_map/ppermute | solution.py:307
  34.2 13.4 %collective-permute-start.12 = (bf16[512,512]{1,0:T(8,128)(2,1)S(1)}, bf16[512,512]{1,0:T(8,128)(2,1)S(1)}, u32[]{:S(2)}, u32[]{:S(2)}) collective-permute-start(bf16[512,512]{1,0:T(8,128)(2,1)S(1)} %copy-done.1), channel_id=1, source_target_pairs={{0,16},{4,20},{8,24},{12,28},{16,0},{20,4},{24,8},{28,12},{1,17},{... | collective-permute-start | bytes 1572872 | tf_op jit(solution)/shard_map/ppermute | solution.py:307
  36.2 9.3 %collective-permute-start.8 = (bf16[1,256,512]{2,1,0:T(8,128)(2,1)S(1)}, bf16[1,256,512]{2,1,0:T(8,128)(2,1)S(1)}, u32[]{:S(2)}, u32[]{:S(2)}) collective-permute-start(bf16[1,256,512]{2,1,0:T(8,128)(2,1)S(1)} %get-tuple-element.49), channel_id=1, source_target_pairs={{1,2},{2,1},{5,6},{6,5},{9,10},{10,9},{13,14},{14,13},{17,18},{18,... | collective-permute-start | bytes 786440 | tf_op jit(solution)/shard_map/ppermute | solution.py:310
  36.9 19.8 %collective-permute-start.10 = (bf16[4,128,512]{2,1,0:T(8,128)(2,1)S(1)}, bf16[4,128,512]{2,1,0:T(8,128)(2,1)S(1)}, u32[]{:S(2)}, u32[]{:S(2)}) collective-permute-start(bf16[4,128,512]{2,1,0:T(8,128)(2,1)S(1)} %collective-permute-done.6.refs_1_), channel_id=1, source_target_pairs={{1,0},{2,3},{5,4},{6,7},{9,8},{10,11},{13,12},{14,15},{17,16},{18,... | collective-permute-start | bytes 1572872 | tf_op jit(solution)/shard_map/ppermute | solution.py:313
  45.4 11.2 %collective-permute-start.9 = (bf16[2,256,512]{2,1,0:T(8,128)(2,1)S(1)}, bf16[2,256,512]{2,1,0:T(8,128)(2,1)S(1)}, u32[]{:S(2)}, u32[]{:S(2)}) collective-permute-start(bf16[2,256,512]{2,1,0:T(8,128)(2,1)S(1)} %get-tuple-element.50), channel_id=1, source_target_pairs={{1,2},{2,1},{5,6},{6,5},{9,10},{10,9},{13,14},{14,13},{17,18},{18,... | collective-permute-start | bytes 1572872 | tf_op jit(solution)/shard_map/ppermute | solution.py:310
  49.4 3.2 %collective-permute-start.13 = (bf16[2,128,512]{2,1,0:T(8,128)(2,1)S(1)}, bf16[2,128,512]{2,1,0:T(8,128)(2,1)S(1)}, u32[]{:S(2)}, u32[]{:S(2)}) collective-permute-start(bf16[2,128,512]{2,1,0:T(8,128)(2,1)S(1)} %get-tuple-element.53), channel_id=1, source_target_pairs={{0,4},{4,0},{8,12},{12,8},{16,20},{20,16},{24,28},{28,24},{1,5},{5... | collective-permute-start | bytes 786440 | tf_op jit(solution)/shard_map/ppermute | solution.py:307
  49.5 12.8 %collective-permute-start.17 = (bf16[1,256,512]{2,1,0:T(8,128)(2,1)S(1)}, bf16[1,256,512]{2,1,0:T(8,128)(2,1)S(1)}, u32[]{:S(2)}, u32[]{:S(2)}) collective-permute-start(bf16[1,256,512]{2,1,0:T(8,128)(2,1)S(1)} %collective-permute-done.8.refs_4_), channel_id=1, source_target_pairs={{1,0},{2,3},{5,4},{6,7},{9,8},{10,11},{13,12},{14,15},{17,16},{18,... | collective-permute-start | bytes 786440 | tf_op jit(solution)/shard_map/ppermute | solution.py:313
  56.7 18.4 %collective-permute-start.14 = (bf16[2,256,512]{2,1,0:T(8,128)(2,1)S(1)}, bf16[2,256,512]{2,1,0:T(8,128)(2,1)S(1)}, u32[]{:S(2)}, u32[]{:S(2)}) collective-permute-start(bf16[2,256,512]{2,1,0:T(8,128)(2,1)S(1)} %collective-permute-done.9.refs_0_.refs_2_.refs_4_), channel_id=1, source_target_pairs={{1,0},{2,3},{5,4},{6,7},{9,8},{10,11},{13,12},{14,15},{17,16},{18,... | collective-permute-start | bytes 1572872 | tf_op jit(solution)/shard_map/ppermute | solution.py:313
  57.9 9.9 %collective-permute-start.15 = (bf16[1,256,512]{2,1,0:T(8,128)(2,1)S(1)}, bf16[1,256,512]{2,1,0:T(8,128)(2,1)S(1)}, u32[]{:S(2)}, u32[]{:S(2)}) collective-permute-start(bf16[1,256,512]{2,1,0:T(8,128)(2,1)S(1)} %get-tuple-element.60), channel_id=1, source_target_pairs={{1,2},{2,1},{5,6},{6,5},{9,10},{10,9},{13,14},{14,13},{17,18},{18,... | collective-permute-start | bytes 786440 | tf_op jit(solution)/shard_map/ppermute | solution.py:310
  63.3 7.9 %collective-permute-start.20 = (bf16[256,512]{1,0:T(8,128)(2,1)S(1)}, bf16[256,512]{1,0:T(8,128)(2,1)S(1)}, u32[]{:S(2)}, u32[]{:S(2)}) collective-permute-start(bf16[256,512]{1,0:T(8,128)(2,1)S(1)} %get-tuple-element.73), channel_id=1, source_target_pairs={{0,16},{4,20},{8,24},{12,28},{16,0},{20,4},{24,8},{28,12},{1,17},{... | collective-permute-start | bytes 786440 | tf_op jit(solution)/shard_map/ppermute | solution.py:307
  65.0 12.9 %collective-permute-start.22 = (bf16[256,512]{1,0:T(8,128)(2,1)S(1)}, bf16[256,512]{1,0:T(8,128)(2,1)S(1)}, u32[]{:S(2)}, u32[]{:S(2)}) collective-permute-start(bf16[256,512]{1,0:T(8,128)(2,1)S(1)} %get-tuple-element.61), channel_id=1, source_target_pairs={{0,8},{4,12},{8,0},{12,4},{16,24},{20,28},{24,16},{28,20},{1,9},{5... | collective-permute-start | bytes 786440 | tf_op jit(solution)/shard_map/ppermute | solution.py:307
  67.9 12.7 %collective-permute-start.16 = (bf16[1,256,512]{2,1,0:T(8,128)(2,1)S(1)}, bf16[1,256,512]{2,1,0:T(8,128)(2,1)S(1)}, u32[]{:S(2)}, u32[]{:S(2)}) collective-permute-start(bf16[1,256,512]{2,1,0:T(8,128)(2,1)S(1)} %collective-permute-done.15.refs_4_), channel_id=1, source_target_pairs={{1,0},{2,3},{5,4},{6,7},{9,8},{10,11},{13,12},{14,15},{17,16},{18,... | collective-permute-start | bytes 786440 | tf_op jit(solution)/shard_map/ppermute | solution.py:313
  76.1 16.1 %collective-permute-start.21 = (bf16[512,512]{1,0:T(8,128)(2,1)S(1)}, bf16[512,512]{1,0:T(8,128)(2,1)S(1)}, u32[]{:S(2)}, u32[]{:S(2)}) collective-permute-start(bf16[512,512]{1,0:T(8,128)(2,1)S(1)} %shard_map.95), channel_id=1, source_target_pairs={{0,8},{4,12},{8,0},{12,4},{16,24},{20,28},{24,16},{28,20},{1,9},{5... | collective-permute-start | bytes 1572872 | tf_op jit(solution)/shard_map/ppermute | solution.py:307
  79.0 13.3 %collective-permute-start.23 = (bf16[512,512]{1,0:T(8,128)(2,1)S(1)}, bf16[512,512]{1,0:T(8,128)(2,1)S(1)}, u32[]{:S(2)}, u32[]{:S(2)}) collective-permute-start(bf16[512,512]{1,0:T(8,128)(2,1)S(1)} %shard_map.96), channel_id=1, source_target_pairs={{0,16},{4,20},{8,24},{12,28},{16,0},{20,4},{24,8},{28,12},{1,17},{... | collective-permute-start | bytes 1572872 | tf_op jit(solution)/shard_map/ppermute | solution.py:307
  81.7 1.6 %collective-permute-start.18 = (bf16[2,128,512]{2,1,0:T(8,128)(2,1)S(1)}, bf16[2,128,512]{2,1,0:T(8,128)(2,1)S(1)}, u32[]{:S(2)}, u32[]{:S(2)}) collective-permute-start(bf16[2,128,512]{2,1,0:T(8,128)(2,1)S(1)} %get-tuple-element.64), channel_id=1, source_target_pairs={{0,4},{4,0},{8,12},{12,8},{16,20},{20,16},{24,28},{28,24},{1,5},{5... | collective-permute-start | bytes 786440 | tf_op jit(solution)/shard_map/ppermute | solution.py:307
  86.7 5.5 %collective-permute-start.19 = (bf16[128,512]{1,0:T(8,128)(2,1)S(1)}, bf16[128,512]{1,0:T(8,128)(2,1)S(1)}, u32[]{:S(2)}, u32[]{:S(2)}) collective-permute-start(bf16[128,512]{1,0:T(8,128)(2,1)S(1)} %get-tuple-element.69), channel_id=1, source_target_pairs={{0,1},{1,0},{2,3},{3,2},{4,5},{5,4},{6,7},{7,6},{8,9},{9,8},{10,11... | collective-permute-start | bytes 393224 | tf_op jit(solution)/shard_map/ppermute | solution.py:307
